TPU v7x, 256 devices: a whole 4x4x8 slice. The times are simulated.
256 devices in a mesh: grp: 16 (over z, core), dev: 16 (over y, x).
Axes of the slice: x: 4, y: 4, z: 8, core: 2. Of those that a mesh axis runs over, the one named last changes fastest.
Arguments:
- voxel_features: float32 [1024, 64, 512], P(('grp', 'dev')), may hold values from -6 to 6
- fine_links: int32 [1024, 26], P(('grp', 'dev')), may hold values from -1 to 1023, as said below
- parent_codes: int32 [1024], P(('grp', 'dev')), may hold values from 0 to 255, as said below
- coarse_links: int32 [512, 26], P(('grp', 'dev')), may hold values from -1 to 511, as said below
- fine_in_weight: float32 [64, 1728], replicated, may hold values from -0.15625 to 0.15625
- fine_in_bias: float32 [64], replicated, may hold values from -3 to 3
- down_weight: float32 [128, 64], replicated, may hold values from -0.75 to 0.75
- coarse_first_weight: float32 [128, 3456], replicated, may hold values from -0.109375 to 0.109375
- coarse_first_bias: float32 [128], replicated, may hold values from -3 to 3
- coarse_second_weight: float32 [128, 3456], replicated, may hold values from -0.109375 to 0.109375
- coarse_second_bias: float32 [128], replicated, may hold values from -3 to 3
- up_weight: float32 [64, 128], replicated, may hold values from -0.5 to 0.5
- fine_out_weight: float32 [64, 1728], replicated, may hold values from -0.15625 to 0.15625
- fine_out_bias: float32 [64], replicated, may hold values from -3 to 3
Outputs:
- refined: float32 [1024, 64, 512], P(('grp', 'dev'))
Inputs may be any that keep to these rules, and one draw needn't show every extreme that they name: `fine_links`: devices are numbered along grp then dev, device d holding bricks d * 4 to (d + 1) * 4 - 1. An entry is -1 or a brick from d * 4 - 2 to (d + 1) * 4 + 1 for a brick of device d, with 2 = 2. parent_codes[i] = 8 * 2 * owner + 8 * slot + octant: owner is the dev index, within the brick's group of 16 devices, of the device that holds the parent, slot the parent's slot there (0 to 1), and octant = 4 * a + 2 * b + c the child's octant. Within a group all codes differ; the number of slots in use differs from device to device, and some device of every group uses all 2. `coarse_links`: device d holds slots d * 2 to (d + 1) * 2 - 1. An entry is -1 or a slot from (d - 1) * 2 to (d + 2) * 2 - 1 for a slot of device d.
All inputs are finite; a program needn't handle non-finite values.
Results may differ from a plain program's by a relative error of at most 0.0001.
Values sent between devices are 32-bit elements; how exact they have to be, the bound alone decides.
No kernel may reach another device: no remote copies, remote signals or barrier semaphores. Data moves between devices by JAX's collectives and lax.ppermute only.
A program may use at most 128 MiB of HBM per device.

v0:
```python
import math

import jax
import jax.numpy as jnp
from jax import lax
from jax.sharding import PartitionSpec as P

neighbour_offsets = [
    (step_x, step_y, step_z)
    for step_x in (-1, 0, 1)
    for step_y in (-1, 0, 1)
    for step_z in (-1, 0, 1)
    if (step_x, step_y, step_z) != (0, 0, 0)
]
source_planes = {-1: slice(7, 8), 0: slice(0, 8), 1: slice(0, 1)}


def padded_2(array, sides, width):
    edges = {}
    for axis, dim in sides:
        count, length = (lax.axis_size(axis), array.shape[dim])
        up = [(i, (i + 1) % count) for i in range(count - 1)]
        last = lax.slice_in_dim(array, length - width, length, axis=dim)
        initial = lax.slice_in_dim(array, 0, width, axis=dim)
        edges[dim] = (
            lax.ppermute(last, axis, up),
            lax.ppermute(initial, axis, [(b, a) for a, b in up]),
        )
    done = []
    for _, dim in sides:
        low, high = edges[dim]
        around = [(width, width) if d in done else (0, 0) for d in range(array.ndim)]
        array = jnp.concatenate([jnp.pad(low, around), array, jnp.pad(high, around)], axis=dim)
        done.append(dim)
    return array


def sent_to_all(array, axis):
    count = lax.axis_size(axis)
    return lax.all_to_all(
        jnp.broadcast_to(array[None], (count, *array.shape)), axis, 0, 0, tiled=True
    )


def joined_along(blocks, dim):
    lengths = list(blocks.shape[1:])
    lengths[dim] *= blocks.shape[0]
    return jnp.moveaxis(blocks, 0, dim).reshape(lengths)


def gather_directly(array, axis, dim):
    blocks = sent_to_all(array, axis)
    return joined_along(blocks, dim)


def side_by_side(arrays, axis, dim, along):
    widths = [math.prod(a.shape[along:]) for a in arrays]
    both = jnp.concatenate(
        [a.reshape(*a.shape[:along], w) for a, w in zip(arrays, widths)], axis=along
    )
    filled = gather_directly(both, axis, dim)
    blocks = jnp.split(filled, [sum(widths[:k]) for k in range(1, len(widths))], axis=along)
    return tuple(
        (b.reshape(*filled.shape[:along], *a.shape[along:]) for a, b in zip(arrays, blocks))
    )


def cut_along(array, dim, count):
    before, after = (array.shape[:dim], array.shape[dim + 1 :])
    return jnp.moveaxis(array.reshape(*before, count, -1, *after), dim, 0)


def sent_and_summed(array, axis, dim):
    blocks = cut_along(array, dim, lax.axis_size(axis))
    arrived = lax.all_to_all(blocks, axis, split_axis=0, concat_axis=0, tiled=True)
    return arrived.sum(axis=0)


def assemble(source, center, links):
    extent = source.shape[0]
    bricks = center.shape[0]
    channels = center.shape[1]
    bricks_ext = jnp.concatenate([source, jnp.zeros((1,) + source.shape[1:], source.dtype)], 0)
    bricks_ext = bricks_ext.reshape(extent + 1, channels, 8, 8, 8)
    picked = jnp.where(links < 0, extent, links)
    middle = center.reshape(bricks, channels, 8, 8, 8)
    slabs = []
    for step_x in (-1, 0, 1):
        rows = []
        for step_y in (-1, 0, 1):
            cells = []
            for step_z in (-1, 0, 1):
                if (step_x, step_y, step_z) == (0, 0, 0):
                    cells.append(middle)
                else:
                    column = neighbour_offsets.index((step_x, step_y, step_z))
                    planes = bricks_ext[
                        :, :, source_planes[step_x], source_planes[step_y], source_planes[step_z]
                    ]
                    cells.append(planes[picked[:, column]])
            rows.append(jnp.concatenate(cells, axis=4))
        slabs.append(jnp.concatenate(rows, axis=3))
    return jnp.concatenate(slabs, axis=2)


def convolve(source, center, links, weight, biases):
    padded = assemble(source, center, links)
    bricks = center.shape[0]
    channels = center.shape[1]
    summed = jnp.zeros((bricks, weight.shape[0], 512), jnp.float32)
    for offset_x in range(3):
        windows = []
        for offset_y in range(3):
            for offset_z in range(3):
                windows.append(
                    padded[
                        :,
                        :,
                        offset_x : offset_x + 8,
                        offset_y : offset_y + 8,
                        offset_z : offset_z + 8,
                    ].reshape(bricks, channels, 512)
                )
        stacked = jnp.concatenate(windows, axis=1)
        kernel = weight[:, 9 * offset_x * channels : (9 * offset_x + 9) * channels]
        summed = summed + jnp.einsum(
            "oc,bcv->bov", kernel, stacked, precision=lax.Precision.HIGHEST
        )
    return summed + biases[None, :, None]


def fine_conv(features, links, weight, biases, position):
    margin = features.shape[0] // 2
    grown = padded_2(features, ((("grp", "dev"), 0),), margin)
    local_links = jnp.where(links < 0, -1, links - (position * features.shape[0] - margin))
    return convolve(grown, features, local_links, weight, biases)


def coarse_conv(features, links, weight, biases, position):
    margin = features.shape[0]
    grown = padded_2(features, ((("grp", "dev"), 0),), margin)
    local_links = jnp.where(links < 0, -1, links - (position * features.shape[0] - margin))
    return convolve(grown, features, local_links, weight, biases)


def pooling(hidden):
    bricks = hidden.shape[0]
    channels = hidden.shape[1]
    return (
        hidden.reshape(bricks, channels, 4, 2, 4, 2, 4, 2)
        .sum(axis=(3, 5, 7))
        .reshape(bricks, channels * 64)
        * 0.125
    )


def octants_to_bricks(pieces, channels):
    slots = pieces.shape[0] // 8
    return (
        pieces.reshape(slots, 2, 2, 2, channels, 4, 4, 4)
        .transpose(0, 4, 1, 5, 2, 6, 3, 7)
        .reshape(slots, channels, 512)
    )


def bricks_to_octants(cubes, channels):
    slots = cubes.shape[0]
    return (
        cubes.reshape(slots, channels, 2, 4, 2, 4, 2, 4)
        .transpose(0, 2, 4, 6, 1, 3, 5, 7)
        .reshape(slots * 8, channels * 64)
    )


def upsample(octants, channels):
    bricks = octants.shape[0]
    grown = jnp.broadcast_to(
        octants.reshape(bricks, channels, 4, 1, 4, 1, 4, 1), (bricks, channels, 4, 2, 4, 2, 4, 2)
    )
    return grown.reshape(bricks, channels, 512)


def per_device(
    voxel_features,
    fine_links,
    parent_codes,
    coarse_links,
    fine_in_weight,
    fine_in_bias,
    down_weight,
    coarse_first_weight,
    coarse_first_bias,
    coarse_second_weight,
    coarse_second_bias,
    up_weight,
    fine_out_weight,
    fine_out_bias,
):
    channels = voxel_features.shape[1]
    slot_count = coarse_links.shape[0]
    position = lax.axis_index("grp") * lax.axis_size("dev") + lax.axis_index("dev")
    hidden = jax.nn.silu(
        fine_conv(voxel_features, fine_links, fine_in_weight, fine_in_bias, position)
    )
    pooled = pooling(hidden)
    code_start = lax.axis_index("dev") * (slot_count * 8)
    targets = code_start + jnp.arange(slot_count * 8, dtype=jnp.int32)
    as_float = parent_codes.astype(jnp.float32)
    segment, code_rows = side_by_side((pooled, as_float), "dev", 0, 1)
    onehot = (code_rows[None, :] == targets[:, None].astype(jnp.float32)).astype(jnp.float32)
    gathered = jnp.dot(
        onehot, segment, precision=lax.Precision.HIGHEST, preferred_element_type=jnp.float32
    )
    coarse_in = octants_to_bricks(gathered, channels)
    coarse_base = jnp.einsum("oc,bcv->bov", down_weight, coarse_in, precision=lax.Precision.HIGHEST)
    coarse_first = jax.nn.silu(
        coarse_conv(coarse_base, coarse_links, coarse_first_weight, coarse_first_bias, position)
    )
    coarse_second = jax.nn.silu(
        coarse_conv(coarse_first, coarse_links, coarse_second_weight, coarse_second_bias, position)
    )
    lifted = jnp.einsum("oc,bcv->bov", up_weight, coarse_second, precision=lax.Precision.HIGHEST)
    upward = bricks_to_octants(lifted, channels)
    group_codes = gather_directly(parent_codes, "dev", 0)
    code_rows = group_codes
    onehot = (code_rows[:, None] == targets[None, :]).astype(jnp.float32)
    rows_up = sent_and_summed(
        jnp.dot(
            onehot, upward, precision=lax.Precision.HIGHEST, preferred_element_type=jnp.float32
        ),
        "dev",
        0,
    )
    rising = upsample(rows_up, channels)
    blended = jax.nn.silu(hidden + rising)
    return voxel_features + fine_conv(blended, fine_links, fine_out_weight, fine_out_bias, position)


def solution(mesh):
    placed = (
        P(("grp", "dev"), None, None),
        P(("grp", "dev"), None),
        P(("grp", "dev")),
        P(("grp", "dev"), None),
        P(),
        P(),
        P(),
        P(),
        P(),
        P(),
        P(),
        P(),
        P(),
        P(),
    )
    return jax.shard_map(
        per_device,
        mesh=mesh,
        in_specs=placed,
        out_specs=P(("grp", "dev"), None, None),
        check_vma=False,
    )
```

profile of v0, /device:TPU:97, one launch (start us, length us, event | category | flops | bytes accessed | tf_op | source)
XLA Modules:
  0.0 593.3 jit_solution(15412968138259091075)
XLA Ops:
  1.1 7.4 %collective-permute-start.1 = (f32[2,64,512]{2,1,0:T(8,128)S(1)}, f32[2,64,512]{2,1,0:T(8,128)S(1)}, u32[]{:S(2)}, u32[]{:S(2)}) collective-permute-start(f32[2,64,512]{2,1,0:T(8,128)S(1)} %get-tuple-element.280), channel_id=1, source_target_pairs={{1,0},{2,1},{3,2},{4,3},{5,4},{6,5},{7,6},{8,7},{9,8},{10,9},{11,1... | collective-permute-start | bytes 786440 | tf_op jit(solution)/shard_map/ppermute | solution.py:27
  80.6 3.8 fusion.114
  105.6 4.6 fusion.121
  128.6 4.4 fusion.120
  140.1 3.9 fusion.113
  172.7 5.5 fusion.39
  192.9 8.2 %all-to-all-start.1 = ((f32[16,4,4097]{2,1,0:T(4,128)}), f32[16,4,4097]{2,1,0:T(4,128)S(1)}, u32[]{:S(2)}, u32[]{:S(2)}) async-start(f32[16,4,4097]{2,1,0:T(4,128)} %broadcast_in_dim.28), calls=%async_computation.1 | async-start | bytes 2162688 | tf_op jit(solution)/shard_map/all_to_all | solution.py:40
  201.6 17.7 %all-to-all-done.1 = f32[16,4,4097]{2,1,0:T(4,128)S(1)} async-done(((f32[16,4,4097]{2,1,0:T(4,128)}), f32[16,4,4097]{2,1,0:T(4,128)S(1)}, u32[]{:S(2)}, u32[]{:S(2)}) %all-to-all-start.1) | async-done | bytes 1048864 | tf_op jit(solution)/shard_map/all_to_all | solution.py:40
  223.3 12.9 %reshape.435 = f32[2,2,2,2,64,4,4,4]{7,6,5,4,3,2,1,0:T(4,128)} reshape(f32[16,4096]{1,0:T(8,128)S(1)} %fusion.9) | data formatting | bytes 524288 | tf_op jit(solution)/shard_map/reshape | solution.py:160
  236.3 7.1 %copy.487 = f32[2,64,2,4,2,4,2,4]{1,7,6,5,4,3,2,0:T(4,128)S(1)} copy(f32[2,64,2,4,2,4,2,4]{7,5,3,1,6,4,2,0:T(4,128)} %bitcast.623) | data formatting | bytes 524288 | tf_op jit(solution)/shard_map/transpose | solution.py:161
  249.4 10.0 %collective-permute-done.3 = f32[2,128,512]{1,2,0:T(8,128)S(1)} collective-permute-done((f32[2,128,512]{1,2,0:T(8,128)S(1)}, f32[2,128,512]{1,2,0:T(8,128)S(1)}, u32[]{:S(2)}, u32[]{:S(2)}) %collective-permute-start.3) | collective-permute-done | bytes 524320 | tf_op jit(solution)/shard_map/ppermute | solution.py:27
  259.4 6.0 %collective-permute-done.2 = f32[2,128,512]{1,2,0:T(8,128)S(1)} collective-permute-done((f32[2,128,512]{1,2,0:T(8,128)S(1)}, f32[2,128,512]{1,2,0:T(8,128)S(1)}, u32[]{:S(2)}, u32[]{:S(2)}) %collective-permute-start.2) | collective-permute-done | bytes 524320 | tf_op jit(solution)/shard_map/ppermute | solution.py:26
  295.7 4.0 fusion.17
  303.3 6.0 %convolution_add_fusion.7 = f32[2,512,128]{2,1,0:T(8,128)S(1)} fusion(f32[2,512,128]{2,1,0:T(8,128)S(1)} %fusion.17, f32[2,1152,512]{1,2,0:T(8,128)} %constant_dynamic-update-slice_fusion.36, f32[128,3456]{1,0:T(8,128)S(1)} %copy-done.66), kind=kOutput, calls=%fused_computation.134 | convolution fusion | flops 1812070400 | bytes 6356992 | tf_op jit(solution)/shard_map/oc,bcv->bov/dot_general | solution.py:126
  310.0 4.0 divide_multiply_fusion.1
  319.9 4.6 all-to-all-start
  324.5 6.4 %all-to-all-done = s32[16,1,4]{2,1,0:T(1,128)S(1)} async-done(((s32[16,1,4]{2,1,0:T(1,128)}), s32[16,1,4]{2,1,0:T(1,128)S(1)}, u32[]{:S(2)}, u32[]{:S(2)}) %all-to-all-start) | async-done | bytes 288 | tf_op jit(solution)/shard_map/all_to_all | solution.py:40
  362.5 4.1 fusion.13
  370.2 6.1 %convolution_add_fusion.5 = f32[2,512,128]{2,1,0:T(8,128)S(1)} fusion(f32[2,512,128]{2,1,0:T(8,128)S(1)} %fusion.13, f32[2,1152,512]{1,2,0:T(8,128)} %constant_dynamic-update-slice_fusion.63, f32[128,3456]{1,0:T(8,128)S(1)} %copy-done.67), kind=kOutput, calls=%fused_computation.130 | convolution fusion | flops 1812070400 | bytes 6356992 | tf_op jit(solution)/shard_map/oc,bcv->bov/dot_general | solution.py:126
  377.0 4.1 fusion.6
  382.2 6.3 %copy.523 = f32[2,2,2,2,64,4,4,4]{7,6,5,4,3,2,1,0:T(4,128)} copy(f32[2,2,2,2,64,4,4,4]{4,7,3,6,2,5,1,0:T(4,128)S(1)} %bitcast.870) | data formatting | bytes 524288 | tf_op jit(solution)/shard_map/transpose | solution.py:170
  388.5 12.3 %reshape.2023 = f32[16,4096,1]{1,0,2:T(8,128)S(1)} reshape(f32[2,2,2,2,64,4,4,4]{7,6,5,4,3,2,1,0:T(4,128)} %copy.523) | data formatting | bytes 524288 | tf_op jit(solution)/shard_map/reshape | solution.py:171
  402.2 20.0 %all_to_all.16 = f32[16,4,4096]{2,1,0:T(4,128)S(1)} all-to-all(f32[16,4,4096]{2,1,0:T(4,128)S(1)} %copy.524), channel_id=1, replica_groups=mesh['grp'=16,'dev'=16] {'dev'}, dimensions={0} | all-to-all | bytes 2097152 | tf_op jit(solution)/shard_map/all_to_all | solution.py:75
  427.1 4.6 collective-permute-start.7
  435.0 10.0 %collective-permute-done.6 = f32[2,64,512]{2,1,0:T(8,128)S(1)} collective-permute-done((f32[2,64,512]{2,1,0:T(8,128)S(1)}, f32[2,64,512]{2,1,0:T(8,128)S(1)}, u32[]{:S(2)}, u32[]{:S(2)}) %collective-permute-start.6) | collective-permute-done | bytes 262176 | tf_op jit(solution)/shard_map/ppermute | solution.py:26
  445.2 3.7 copy.593
  486.2 3.8 fusion.112
  511.2 4.6 fusion.117
  534.2 4.4 fusion.116
  545.7 3.9 fusion.111
  578.2 5.5 fusion.35
  588.9 4.2 fusion.2
  (693 shorter events, 375.7 us)
Async XLA Ops:
  0.0 243.4 %copy-start = (f32[128,64]{0,1:T(8,128)S(1)}, f32[128,64]{0,1:T(8,128)}, u32[]{:S(2)}) copy-start(f32[128,64]{0,1:T(8,128)} %param.20) | copy-start | bytes 98308
  1.1 24.6 %collective-permute-start.1 = (f32[2,64,512]{2,1,0:T(8,128)S(1)}, f32[2,64,512]{2,1,0:T(8,128)S(1)}, u32[]{:S(2)}, u32[]{:S(2)}) collective-permute-start(f32[2,64,512]{2,1,0:T(8,128)S(1)} %get-tuple-element.280), channel_id=1, source_target_pairs={{1,0},{2,1},{3,2},{4,3},{5,4},{6,5},{7,6},{8,7},{9,8},{10,9},{11,1... | collective-permute-start | bytes 786440 | tf_op jit(solution)/shard_map/ppermute | solution.py:27
  8.5 17.1 %collective-permute-start = (f32[2,64,512]{2,1,0:T(8,128)S(1)}, f32[2,64,512]{2,1,0:T(8,128)S(1)}, u32[]{:S(2)}, u32[]{:S(2)}) collective-permute-start(f32[2,64,512]{2,1,0:T(8,128)S(1)} %get-tuple-element.279), channel_id=1, source_target_pairs={{0,1},{1,2},{2,3},{3,4},{4,5},{5,6},{6,7},{7,8},{8,9},{9,10},{10,1... | collective-permute-start | bytes 786440 | tf_op jit(solution)/shard_map/ppermute | solution.py:26
  22.4 51.9 %copy-start.2 = (f32[4,64,512]{1,2,0:T(8,128)}, f32[4,64,512]{1,2,0:T(8,128)S(1)}, u32[]{:S(2)}) copy-start(f32[4,64,512]{1,2,0:T(8,128)S(1)} %copy.433) | copy-start | bytes 1572868
  160.6 17.7 %slice-start.8 = ((s8[4718592]{0:T(1024)(128)(4,1)}), s8[524288]{0:T(1024)(128)(4,1)S(1)}, s32[]{:S(2)}) async-start(s8[4718592]{0:T(1024)(128)(4,1)} %bitcast.734), calls=%async_computation.11 | async-start | bytes 1048576
  187.8 13.4 %copy-start.101 = (s32[2]{0:T(128)S(1)}, s32[2]{0:T(128)}, u32[]{:S(2)}) copy-start(s32[2]{0:T(128)} %get-tuple-element.41) | copy-start | bytes 28
  187.8 13.4 %copy-start.102 = (s32[2]{0:T(128)S(1)}, s32[2]{0:T(128)}, u32[]{:S(2)}) copy-start(s32[2]{0:T(128)} %get-tuple-element.42) | copy-start | bytes 28
  187.8 13.4 %copy-start.99 = (s32[2]{0:T(128)S(1)}, s32[2]{0:T(128)}, u32[]{:S(2)}) copy-start(s32[2]{0:T(128)} %get-tuple-element.43) | copy-start | bytes 28
  187.8 13.4 %copy-start.100 = (s32[2]{0:T(128)S(1)}, s32[2]{0:T(128)}, u32[]{:S(2)}) copy-start(s32[2]{0:T(128)} %get-tuple-element.44) | copy-start | bytes 28
  187.8 13.4 %copy-start.97 = (s32[2]{0:T(128)S(1)}, s32[2]{0:T(128)}, u32[]{:S(2)}) copy-start(s32[2]{0:T(128)} %get-tuple-element.45) | copy-start | bytes 28
  187.9 13.4 %copy-start.98 = (s32[2]{0:T(128)S(1)}, s32[2]{0:T(128)}, u32[]{:S(2)}) copy-start(s32[2]{0:T(128)} %get-tuple-element.46) | copy-start | bytes 28
  187.9 13.4 %copy-start.95 = (s32[2]{0:T(128)S(1)}, s32[2]{0:T(128)}, u32[]{:S(2)}) copy-start(s32[2]{0:T(128)} %get-tuple-element.47) | copy-start | bytes 28
  187.9 13.4 %copy-start.96 = (s32[2]{0:T(128)S(1)}, s32[2]{0:T(128)}, u32[]{:S(2)}) copy-start(s32[2]{0:T(128)} %get-tuple-element.48) | copy-start | bytes 28
  187.9 13.4 %copy-start.71 = (s32[2,26]{1,0:T(2,128)S(1)}, s32[2,26]{1,0:T(2,128)}, u32[]{:S(2)}) copy-start(s32[2,26]{1,0:T(2,128)} %copy-done.70) | copy-start | bytes 628
  187.9 13.7 %copy-start.94 = (s32[2]{0:T(128)S(1)}, s32[2]{0:T(128)}, u32[]{:S(2)}) copy-start(s32[2]{0:T(128)} %get-tuple-element.49) | copy-start | bytes 28
  192.9 26.5 %all-to-all-start.1 = ((f32[16,4,4097]{2,1,0:T(4,128)}), f32[16,4,4097]{2,1,0:T(4,128)S(1)}, u32[]{:S(2)}, u32[]{:S(2)}) async-start(f32[16,4,4097]{2,1,0:T(4,128)} %broadcast_in_dim.28), calls=%async_computation.1 | async-start | bytes 2162688 | tf_op jit(solution)/shard_map/all_to_all | solution.py:40
  236.2 13.1 %copy-start.88 = (s32[2]{0:T(128)S(1)}, s32[2]{0:T(128)}, u32[]{:S(2)}) copy-start(s32[2]{0:T(128)} %get-tuple-element.36) | copy-start | bytes 28
  236.2 13.1 %copy-start.89 = (s32[2]{0:T(128)S(1)}, s32[2]{0:T(128)}, u32[]{:S(2)}) copy-start(s32[2]{0:T(128)} %get-tuple-element.37) | copy-start | bytes 28
  236.2 13.1 %copy-start.86 = (s32[2]{0:T(128)S(1)}, s32[2]{0:T(128)}, u32[]{:S(2)}) copy-start(s32[2]{0:T(128)} %get-tuple-element.38) | copy-start | bytes 28
  236.3 13.1 %copy-start.87 = (s32[2]{0:T(128)S(1)}, s32[2]{0:T(128)}, u32[]{:S(2)}) copy-start(s32[2]{0:T(128)} %get-tuple-element.39) | copy-start | bytes 28
  236.3 29.1 %copy-start.85 = (f32[7]{0:T(128)S(1)}, f32[7]{0:T(128)}, u32[]{:S(2)}) copy-start(f32[7]{0:T(128)} %pad.165.clone) | copy-start | bytes 88
  244.0 15.4 %collective-permute-start.3 = (f32[2,128,512]{1,2,0:T(8,128)S(1)}, f32[2,128,512]{1,2,0:T(8,128)S(1)}, u32[]{:S(2)}, u32[]{:S(2)}) collective-permute-start(f32[2,128,512]{1,2,0:T(8,128)S(1)} %bitcast.644), channel_id=1, source_target_pairs={{1,0},{2,1},{3,2},{4,3},{5,4},{6,5},{7,6},{8,7},{9,8},{10,9},{11,1... | collective-permute-start | bytes 1572872 | tf_op jit(solution)/shard_map/ppermute | solution.py:27
  245.9 19.4 %collective-permute-start.2 = (f32[2,128,512]{1,2,0:T(8,128)S(1)}, f32[2,128,512]{1,2,0:T(8,128)S(1)}, u32[]{:S(2)}, u32[]{:S(2)}) collective-permute-start(f32[2,128,512]{1,2,0:T(8,128)S(1)} %bitcast.645), channel_id=1, source_target_pairs={{0,1},{1,2},{2,3},{3,4},{4,5},{5,6},{6,7},{7,8},{8,9},{9,10},{10,1... | collective-permute-start | bytes 1572872 | tf_op jit(solution)/shard_map/ppermute | solution.py:26
  314.0 16.9 %collective-permute-start.5 = (f32[2,128,512]{1,2,0:T(8,128)S(1)}, f32[2,128,512]{1,2,0:T(8,128)S(1)}, u32[]{:S(2)}, u32[]{:S(2)}) collective-permute-start(f32[2,128,512]{1,2,0:T(8,128)S(1)} %divide_multiply_fusion.1), channel_id=1, source_target_pairs={{1,0},{2,1},{3,2},{4,3},{5,4},{6,5},{7,6},{8,7},{9,8},{10,9},{11,1... | collective-permute-start | bytes 1572872 | tf_op jit(solution)/shard_map/ppermute | solution.py:27
  315.9 16.6 %collective-permute-start.4 = (f32[2,128,512]{1,2,0:T(8,128)S(1)}, f32[2,128,512]{1,2,0:T(8,128)S(1)}, u32[]{:S(2)}, u32[]{:S(2)}) collective-permute-start(f32[2,128,512]{1,2,0:T(8,128)S(1)} %divide_multiply_fusion.1), channel_id=1, source_target_pairs={{0,1},{1,2},{2,3},{3,4},{4,5},{5,6},{6,7},{7,8},{8,9},{9,10},{10,1... | collective-permute-start | bytes 1572872 | tf_op jit(solution)/shard_map/ppermute | solution.py:26
  319.9 11.0 %all-to-all-start = ((s32[16,1,4]{2,1,0:T(1,128)}), s32[16,1,4]{2,1,0:T(1,128)S(1)}, u32[]{:S(2)}, u32[]{:S(2)}) async-start(s32[16,1,4]{2,1,0:T(1,128)} %broadcast_in_dim.27), calls=%async_computation | async-start | bytes 16384 | tf_op jit(solution)/shard_map/all_to_all | solution.py:40
  425.1 19.8 %copy-start.84 = (f32[9]{0:T(128)S(1)}, f32[9]{0:T(128)}, u32[]{:S(2)}) copy-start(f32[9]{0:T(128)} %copy-done.83) | copy-start | bytes 112
  427.0 21.9 %copy-start.6 = (f32[4,64,512]{2,1,0:T(8,128)}, f32[4,64,512]{2,1,0:T(8,128)S(1)}, u32[]{:S(2)}) copy-start(f32[4,64,512]{2,1,0:T(8,128)S(1)} %divide_multiply_fusion) | copy-start | bytes 1572868
  427.1 7.9 %collective-permute-start.7 = (f32[2,64,512]{2,1,0:T(8,128)S(1)}, f32[2,64,512]{2,1,0:T(8,128)S(1)}, u32[]{:S(2)}, u32[]{:S(2)}) collective-permute-start(f32[2,64,512]{2,1,0:T(8,128)S(1)} %get-tuple-element.274), channel_id=1, source_target_pairs={{1,0},{2,1},{3,2},{4,3},{5,4},{6,5},{7,6},{8,7},{9,8},{10,9},{11,1... | collective-permute-start | bytes 786440 | tf_op jit(solution)/shard_map/ppermute | solution.py:27
  431.7 13.3 %collective-permute-start.6 = (f32[2,64,512]{2,1,0:T(8,128)S(1)}, f32[2,64,512]{2,1,0:T(8,128)S(1)}, u32[]{:S(2)}, u32[]{:S(2)}) collective-permute-start(f32[2,64,512]{2,1,0:T(8,128)S(1)} %get-tuple-element.273), channel_id=1, source_target_pairs={{0,1},{1,2},{2,3},{3,4},{4,5},{5,6},{6,7},{7,8},{8,9},{9,10},{10,1... | collective-permute-start | bytes 786440 | tf_op jit(solution)/shard_map/ppermute | solution.py:26
  433.9 46.1 %copy-start.3 = (f32[4,64,512]{1,2,0:T(8,128)}, f32[4,64,512]{1,2,0:T(8,128)S(1)}, u32[]{:S(2)}) copy-start(f32[4,64,512]{1,2,0:T(8,128)S(1)} %copy.541) | copy-start | bytes 1572868
  566.1 17.7 %slice-start.10 = ((s8[4718592]{0:T(1024)(128)(4,1)}), s8[524288]{0:T(1024)(128)(4,1)S(1)}, s32[]{:S(2)}) async-start(s8[4718592]{0:T(1024)(128)(4,1)} %bitcast.736), calls=%async_computation.13 | async-start | bytes 1048576
  (99 other events, 569.8 us)
where the time goes:
time: 605 us; the launch traced here: 593 us
  local copies, waits for them, and re-layouts  384 us (63%)
  matrix products  57.5 us (10%)
  waiting for transfers between devices  52.6 us (9%)
  starting transfers between devices  39.2 us (6%)
  other arithmetic  36.4 us (6%)
  blocking collectives  20 us (3%)
    reshape x52, local copies, waits for them, and re-layouts, convolve(): windows.append(padded[:, :, offset_x:offset_x + 8, offset_y:offset_y + 8,...  111 us
    gather x104, local copies, waits for them, and re-layouts, assemble(): cells.append(planes[picked[:, column]])  74.3 us
    unnamed x355, local copies, waits for them, and re-layouts  65.7 us
    dot_general x12, matrix products, convolve(): jnp.einsum('oc,bcv->bov', kernel, stacked, precision=lax.Precision.HIGHEST)  53.9 us
    slice x16, local copies, waits for them, and re-layouts, convolve(): padded[:, :, offset_x:offset_x + 8, offset_y:offset_y + 8, offset_z:offse...  40.7 us
    slice x46, local copies, waits for them, and re-layouts, assemble(): bricks_ext[:, :, source_planes[step_x], source_planes[step_y], source_pla...  24.6 us
    all_to_all x2, waiting for transfers between devices, sent_to_all(): lax.all_to_all(jnp.broadcast_to(array[None], (count, *array.shape)), axis...  24.1 us
    all_to_all x1, blocking collectives, sent_and_summed(): lax.all_to_all(blocks, axis, split_axis=0, concat_axis=0, tiled=True)  20 us
  transfers between devices with their start and end apart: 10, of which 7 were waited for; matrix products, arithmetic and copies ran while one was open for 3% of the time, Pallas kernels for 0%

commit v1 on v0

v1 whole, which is shorter than its diff:
```python
import jax
import jax.numpy as jnp
from jax import lax
from jax.experimental import pallas as pl
from jax.experimental.pallas import tpu as pltpu
from jax.sharding import PartitionSpec as P

F32, BF16 = jnp.float32, jnp.bfloat16
BOTH = ("grp", "dev")
STEPS = (-1, 0, 1)
COLUMN = {
    offset: k
    for k, offset in enumerate(
        (x, y, z) for x in STEPS for y in STEPS for z in STEPS if (x, y, z) != (0, 0, 0)
    )
}
PLANE = {-1: slice(7, 8), 0: slice(0, 8), 1: slice(0, 1)}
ROOM = {-1: slice(0, 1), 0: slice(1, 9), 1: slice(9, 10)}
VMEM = pl.BlockSpec(memory_space=pltpu.VMEM)
SMEM = pl.BlockSpec(memory_space=pltpu.SMEM)


def silu(v):
    return v / (1.0 + jnp.exp(-v))


def split(v):
    high = v.astype(BF16)
    return high, (v - high.astype(F32)).astype(BF16)


def low_lanes(shape):
    return lax.broadcasted_iota(jnp.int32, shape, len(shape) - 1) < 64


def swap(v):
    return pltpu.roll(v, 64, v.ndim - 1)


def device_number():
    return lax.axis_index("grp") * lax.axis_size("dev") + lax.axis_index("dev")


def neighbours(links_ref, row, start, none):
    found = {}
    for offset, k in COLUMN.items():
        link = links_ref[row, k]
        found[offset] = jnp.where(link < 0, none, link - start)
    return found


def shifted_rows(tile):
    below, here, above = tile(-1), tile(0), tile(1)
    axis = here.ndim - 2
    row = lax.broadcasted_iota(jnp.int32, here.shape, axis)
    return (
        pltpu.roll(jnp.where(row == 7, below, here), 1, axis),
        here,
        pltpu.roll(jnp.where(row == 0, above, here), 7, axis),
    )


def product(high, low, weight_ref):
    both = jnp.dot(high, weight_ref[...], preferred_element_type=F32)
    half = both.shape[1] // 2
    rest = jnp.dot(low, weight_ref[:, :half], preferred_element_type=F32)
    return both[:, :half] + both[:, half:] + rest


def fine_rim(source, links_ref, high, low):
    start = device_number() * 4 - 2
    for pair in range(2):
        found = []
        for b in (2 * pair, 2 * pair + 1):
            near = neighbours(links_ref, b, start, 8)
            near[0, 0, 0] = b + 2
            found.append(near)
        for k in range(5):
            for dx in STEPS:
                rows = []
                for near in found:

                    def tile(dy):
                        first = near[dx, dy, -1 if k == 0 else 0]
                        second = near[dx, dy, 1 if k == 4 else 0]
                        a = source[first, (k + 3) % 4, PLANE[dx]]
                        b = source[second, k % 4, PLANE[dx]]
                        return jnp.where(low_lanes(a.shape), a, b)

                    rows.append(shifted_rows(tile))
                for j in range(3):
                    both = jnp.concatenate([rows[0][j], rows[1][j]], axis=1)
                    h, l = split(both)
                    high[j, k, ROOM[dx], 16 * pair : 16 * pair + 16, :] = h
                    low[j, k, ROOM[dx], 16 * pair : 16 * pair + 16, :] = l


def fine_columns(padded, zz):
    return jnp.concatenate(
        [
            padded[j, zz + h, i : i + 8].reshape(256, 128)
            for i in range(3)
            for j in range(3)
            for h in range(2)
        ],
        axis=1,
    )


def fine_in_kernel(
    codes_ref, links_ref, low_ref, own_ref, high_ref, weight_ref, bias_ref,
    hidden_ref, pooled_ref, source, flat, high, low, sums,
):
    source[8] = jnp.zeros((4, 8, 8, 128), F32)
    pieces = [low_ref[...], own_ref[0:2], own_ref[2:4], high_ref[...]]
    for p, piece in enumerate(pieces):
        flat[...] = piece.reshape(128, 512).T
        for zz in range(4):
            odd = flat[pl.ds(2 * zz + 1, 64, 8), :]
            even = flat[pl.ds(2 * zz, 64, 8), :]
            lower = low_lanes(odd.shape)
            source[2 * p, zz] = jnp.where(lower, odd, swap(even)).reshape(8, 8, 128)
            source[2 * p + 1, zz] = jnp.where(lower, swap(odd), even).reshape(8, 8, 128)
    fine_rim(source, links_ref, high, low)
    held = []
    for zz in range(4):
        r = product(fine_columns(high, zz), fine_columns(low, zz), weight_ref) + bias_ref[...]
        r = silu(r).reshape(8, 32, 128)
        for b in range(4):
            hidden_ref[b, zz] = r[:, 8 * b : 8 * b + 8]
        r = r.reshape(4, 2, 32, 128)
        r = r[:, 0] + r[:, 1]
        held.append(r + swap(r))
        if zz % 2 == 1:
            both = jnp.where(low_lanes(r.shape), held[zz - 1], held[zz])
            sums[64 * zz - 64 : 64 * zz + 64, :] = both.reshape(128, 128)
    means = (sums[pl.ds(0, 128, 2), :] + sums[pl.ds(1, 128, 2), :]) * 0.125
    for n in range(8):
        for b in range(4):
            at = (4 * n + b) * 4
            pooled_ref[32 * b + 4 * n : 32 * b + 4 * n + 4, :] = means[at : at + 4]
    lane = lax.broadcasted_iota(jnp.int32, (8, 128), 1)
    named = jnp.zeros((8, 128), F32)
    for b in range(4):
        named = jnp.where(lane == b, codes_ref[b].astype(F32), named)
    pooled_ref[128:136, :] = named


def collect_kernel(all_ref, cubes_ref, codes_ref, held, spelled, place, sem):
    held[...] = all_ref[:, 128, :]
    copy = pltpu.make_async_copy(held, spelled, sem)
    copy.start()
    copy.wait()
    base = lax.axis_index("dev") * 16
    for t in range(16):
        place[t] = -1

    def note(i, carry):
        code = spelled[i // 4, i % 4].astype(jnp.int32)
        codes_ref[i] = code
        local = code - base

        @pl.when((local >= 0) & (local < 16))
        def _():
            place[local] = i

        return carry

    lax.fori_loop(0, 64, note, 0)
    for t in range(16):
        s, a, b, c = t // 8, t // 4 % 2, t // 2 % 2, t % 2
        i = place[t]
        at = jnp.maximum(i, 0)
        v = all_ref[at // 4, pl.ds(pl.multiple_of(at % 4 * 32, 32), 32), :]
        v = jnp.where(i >= 0, v, 0.0)
        for r in range(8):
            cubes_ref[s, a, c, r, 4 * b : 4 * b + 4, :] = v[4 * r : 4 * r + 4]


def coarse_rim(source, links_ref, high, low):
    start = device_number() * 2 - 2
    found = []
    for s in range(2):
        near = neighbours(links_ref, s, start, 6)
        near[0, 0, 0] = s + 2
        found.append(near)
    for z in range(10):
        dz = -1 if z == 0 else 1 if z == 9 else 0
        at = {-1: 7, 0: z - 1, 1: 0}[dz]
        for dx in STEPS:
            rows = [
                shifted_rows(lambda dy, near=near: source[near[dx, dy, dz], at, PLANE[dx]])
                for near in found
            ]
            for j in range(3):
                h, l = split(jnp.concatenate([rows[0][j], rows[1][j]], axis=1))
                high[j, z, ROOM[dx]] = h
                low[j, z, ROOM[dx]] = l


def coarse_columns(padded, z):
    return jnp.concatenate(
        [
            padded[j, z + l : z + l + 2, i : i + 8].reshape(256, 128)
            for i in range(3)
            for j in range(3)
            for l in range(3)
        ],
        axis=1,
    )


def coarse_first_kernel(
    links_ref, low_ref, own_ref, high_ref, down_ref, weight_ref, bias_ref, first_ref, source, high, low
):
    source[6] = jnp.zeros((8, 8, 8, 128), F32)
    for p, part in enumerate((low_ref, own_ref, high_ref)):
        for s in range(2):
            h, l = split(part[s].reshape(256, 128))
            based = product(h, l, down_ref).reshape(2, 2, 2, 4, 8, 256)
            for a in range(2):
                for z in range(8):
                    source[2 * p + s, z, 4 * a : 4 * a + 4] = based[
                        a, z // 4, z // 2 % 2, :, :, 128 * (z % 2) : 128 * (z % 2) + 128
                    ]
    coarse_rim(source, links_ref, high, low)
    for z in range(0, 8, 2):
        r = product(coarse_columns(high, z), coarse_columns(low, z), weight_ref) + bias_ref[...]
        r = silu(r).reshape(2, 8, 16, 128)
        for s in range(2):
            first_ref[s, z : z + 2] = r[:, :, 8 * s : 8 * s + 8]


def coarse_second_kernel(
    links_ref, codes_ref, low_ref, own_ref, high_ref, weight_ref, bias_ref, up_ref,
    out_ref, source, high, low, octants,
):
    source[6] = jnp.zeros((8, 8, 8, 128), F32)
    for p, part in enumerate((low_ref, own_ref, high_ref)):
        source[2 * p : 2 * p + 2] = part[...]
    coarse_rim(source, links_ref, high, low)
    for z in range(0, 8, 2):
        c, q = z // 4, z // 2 % 2
        r = product(coarse_columns(high, z), coarse_columns(low, z), weight_ref) + bias_ref[...]
        r = silu(r)
        h, l = split(jnp.concatenate([r[:128], r[128:]], axis=1))
        lifted = product(h, l, up_ref)
        for t in range(c, 16, 2):
            s, a, b = t // 8, t // 4 % 2, t // 2 % 2
            for x in range(4):
                at = (4 * a + x) * 16 + 8 * s + 4 * b
                octants[t, 16 * q + 4 * x : 16 * q + 4 * x + 4, :] = lifted[at : at + 4]
    base = lax.axis_index("dev") * 16

    def place(i, carry):
        local = codes_ref[i] - base
        known = (local >= 0) & (local < 16)
        v = octants[jnp.clip(local, 0, 15)]
        out_ref[i] = jnp.where(known, v, 0.0)
        return carry

    lax.fori_loop(0, 64, place, 0)


def blend_kernel(hidden_ref, risen_ref, out_ref, grown):
    risen = risen_ref[0]
    for k in range(1, 16):
        risen = risen + risen_ref[k]
    for b in range(4):
        v = risen[32 * b : 32 * b + 32]
        grown[pl.ds(0, 32, 2), :] = v
        grown[pl.ds(1, 32, 2), :] = v
        full = grown[...].reshape(2, 4, 1, 8, 128)
        turned = swap(full)
        lower = low_lanes(full.shape)
        for h in range(2):
            w = jnp.where(lower, full, turned) if h == 0 else jnp.where(lower, turned, full)
            for q in range(2):
                zz = 2 * q + h
                v = silu(hidden_ref[b, zz].reshape(4, 2, 8, 128) + w[q])
                out_ref[b, zz] = v.reshape(8, 8, 128)


def fine_out_kernel(
    links_ref, low_ref, own_ref, high_ref, features_ref, weight_ref, bias_ref, out_ref, source, flat, high, low
):
    source[8] = jnp.zeros((4, 8, 8, 128), F32)
    source[0:2] = low_ref[...]
    source[2:6] = own_ref[...]
    source[6:8] = high_ref[...]
    fine_rim(source, links_ref, high, low)
    for zz in range(4):
        r = product(fine_columns(high, zz), fine_columns(low, zz), weight_ref) + bias_ref[...]
        r = r.reshape(8, 32, 128)
        for p in range(2):
            v0 = r[:, 16 * p : 16 * p + 8].reshape(64, 128)
            v1 = r[:, 16 * p + 8 : 16 * p + 16].reshape(64, 128)
            lower = low_lanes(v0.shape)
            flat[p, pl.ds(2 * zz + 1, 64, 8), :] = jnp.where(lower, v0, swap(v1))
            flat[p, pl.ds(2 * zz, 64, 8), :] = jnp.where(lower, swap(v0), v1)
    for p in range(2):
        out_ref[2 * p : 2 * p + 2] = features_ref[2 * p : 2 * p + 2] + flat[p].T.reshape(2, 64, 512)


def halves(weight):
    high = lax.reduce_precision(weight, exponent_bits=8, mantissa_bits=7)
    return jnp.concatenate([high.astype(BF16), (weight - high).astype(BF16)], axis=1)


def fine_weight(weight):
    taps = weight.reshape(64, 9, 192).transpose(1, 2, 0)
    even = jnp.pad(taps, ((0, 0), (0, 64), (0, 0)))
    odd = jnp.pad(taps, ((0, 0), (64, 0), (0, 0)))
    return halves(jnp.concatenate([odd, even], axis=2).reshape(2304, 128))


def diagonal(weight):
    n, m = weight.shape
    return halves(
        jnp.concatenate(
            [jnp.pad(weight, ((0, n), (0, 0))), jnp.pad(weight, ((n, 0), (0, 0)))], axis=1
        )
    )


def exchanged(first, last):
    count = lax.axis_size(BOTH)
    up = [(i, i + 1) for i in range(count - 1)]
    return lax.ppermute(last, BOTH, up), lax.ppermute(first, BOTH, [(b, a) for a, b in up])


def struct(*shape, dtype=F32):
    return jax.ShapeDtypeStruct(shape, dtype)


def call(kernel, out, scratch, specs, args, flops):
    return pl.pallas_call(
        kernel,
        out_shape=out,
        in_specs=specs,
        out_specs=jax.tree.map(lambda o: SMEM if o.dtype == jnp.int32 else VMEM, out),
        scratch_shapes=scratch,
        cost_estimate=pl.CostEstimate(flops=flops, bytes_accessed=1 << 21, transcendentals=0),
        compiler_params=pltpu.CompilerParams(vmem_limit_bytes=40 << 20),
    )(*args)


def per_device(
    features, fine_links, codes, coarse_links, fine_in_weight, fine_in_bias, down_weight,
    coarse_first_weight, coarse_first_bias, coarse_second_weight, coarse_second_bias,
    up_weight, fine_out_weight, fine_out_bias,
):
    fine_padded = [pltpu.VMEM((3, 5, 10, 32, 128), BF16)] * 2
    coarse_padded = [pltpu.VMEM((3, 10, 10, 16, 128), BF16)] * 2
    fine_source = pltpu.VMEM((9, 4, 8, 8, 128), F32)
    coarse_source = pltpu.VMEM((7, 8, 8, 8, 128), F32)

    below, above = exchanged(features[0:2], features[2:4])
    hidden, pooled = call(
        fine_in_kernel,
        (struct(4, 4, 8, 8, 128), struct(136, 128)),
        [fine_source, pltpu.VMEM((512, 128), F32), *fine_padded, pltpu.VMEM((256, 128), F32)],
        [SMEM, SMEM] + [VMEM] * 5,
        (
            codes, fine_links, below, features, above,
            fine_weight(fine_in_weight), jnp.tile(fine_in_bias, 2)[None],
        ),
        2 * 1024 * 2304 * 384,
    )
    spread = lax.all_to_all(
        jnp.broadcast_to(pooled[None], (16, 136, 128)), "dev", 0, 0, tiled=True
    )
    cubes, group_codes = call(
        collect_kernel,
        (struct(2, 2, 2, 8, 8, 128), struct(64, dtype=jnp.int32)),
        [
            pltpu.VMEM((16, 128), F32), pltpu.SMEM((16, 128), F32),
            pltpu.SMEM((16,), jnp.int32), pltpu.SemaphoreType.DMA,
        ],
        [VMEM],
        (spread,),
        1 << 20,
    )
    below, above = exchanged(cubes, cubes)
    first = call(
        coarse_first_kernel,
        struct(2, 8, 8, 8, 128),
        [coarse_source, *coarse_padded],
        [SMEM] + [VMEM] * 6,
        (
            coarse_links, below, cubes, above, diagonal(down_weight.T),
            halves(coarse_first_weight.T), coarse_first_bias[None],
        ),
        2 * 1024 * 3456 * 384,
    )
    below, above = exchanged(first, first)
    lifted = call(
        coarse_second_kernel,
        struct(64, 32, 128),
        [coarse_source, *coarse_padded, pltpu.VMEM((16, 32, 128), F32)],
        [SMEM, SMEM] + [VMEM] * 6,
        (
            coarse_links, group_codes, below, first, above,
            halves(coarse_second_weight.T), coarse_second_bias[None], diagonal(up_weight.T),
        ),
        2 * 1024 * 3456 * 384,
    )
    risen = lax.all_to_all(lifted.reshape(16, 128, 128), "dev", 0, 0, tiled=True)
    blended = call(
        blend_kernel,
        struct(4, 4, 8, 8, 128),
        [pltpu.VMEM((64, 128), F32)],
        [VMEM, VMEM],
        (hidden, risen),
        1 << 20,
    )
    below, above = exchanged(blended[0:2], blended[2:4])
    return call(
        fine_out_kernel,
        struct(4, 64, 512),
        [fine_source, pltpu.VMEM((2, 512, 128), F32), *fine_padded],
        [SMEM] + [VMEM] * 6,
        (
            fine_links, below, blended, above, features,
            fine_weight(fine_out_weight), jnp.tile(fine_out_bias, 2)[None],
        ),
        2 * 1024 * 2304 * 384,
    )


def solution(mesh):
    split_first = P(BOTH)
    placed = (split_first,) * 4 + (P(),) * 10
    return jax.shard_map(
        per_device,
        mesh=mesh,
        in_specs=placed,
        out_specs=split_first,
        check_vma=False,
    )
```

time: 605 us -> 149 us (0.25)
  the two profiles are of different devices: /device:TPU:97 before, /device:TPU:127 now
where the time goes in v1:
time: 149 us; the launch traced here: 148 us
  starting transfers between devices  50.4 us (34%)
  waiting for transfers between devices  43.4 us (29%)
  Pallas kernels  24.6 us (17%)
  local copies, waits for them, and re-layouts  15.7 us (11%)
  other arithmetic  13.9 us (9%)
    ppermute x4, starting transfers between devices, exchanged(): lax.ppermute(last, BOTH, up)  28.8 us
    ppermute x4, waiting for transfers between devices, exchanged(): lax.ppermute(first, BOTH, [(b, a) for a, b in up])  27.4 us
    pallas_call x6, Pallas kernels, call(): pl.pallas_call(kernel, out_shape=out, in_specs=specs, out_specs=jax.tree....  24.6 us
    ppermute x4, starting transfers between devices, exchanged(): lax.ppermute(first, BOTH, [(b, a) for a, b in up])  9.3 us
    convert_element_type x6, other arithmetic, halves(): high.astype(BF16)  8.12 us
    ppermute x4, waiting for transfers between devices, exchanged(): lax.ppermute(last, BOTH, up)  6.86 us
    unnamed x39, local copies, waits for them, and re-layouts  6.73 us
    all_to_all x1, starting transfers between devices, per_device(): lax.all_to_all(lifted.reshape(16, 128, 128), 'dev', 0, 0, tiled=True)  6.21 us
  transfers between devices with their start and end apart: 10, of which 8 were waited for; matrix products, arithmetic and copies ran while one was open for 17% of the time, Pallas kernels for 0%

profile of v1, /device:TPU:127, one launch (start us, length us, event | category | flops | bytes accessed | tf_op | source)
XLA Modules:
  0.0 148.3 jit_solution(14522848263079711057)
XLA Ops:
  0.0 1.9 %fusion.7 = (f32[2,64,512]{2,1,0:T(8,128)}, f32[2,64,512]{2,1,0:T(8,128)}) fusion(f32[4,64,512]{2,1,0:T(8,128)} %features_ref.1), kind=kLoop, calls=%fused_computation.35 | loop fusion | bytes 1048576 | tf_op jit(solution)/shard_map/slice | solution.py:358
  1.9 4.9 %collective-permute-start = (f32[2,64,512]{2,1,0:T(8,128)}, f32[2,64,512]{2,1,0:T(8,128)S(1)}, u32[]{:S(2)}, u32[]{:S(2)}) collective-permute-start(f32[2,64,512]{2,1,0:T(8,128)} %get-tuple-element.24), channel_id=1, source_target_pairs={{0,1},{1,2},{2,3},{3,4},{4,5},{5,6},{6,7},{7,8},{8,9},{9,10},{10,1... | collective-permute-start | bytes 786440 | tf_op jit(solution)/shard_map/ppermute | solution.py:329
  6.8 1.9 %collective-permute-start.1 = (f32[2,64,512]{2,1,0:T(8,128)}, f32[2,64,512]{2,1,0:T(8,128)S(1)}, u32[]{:S(2)}, u32[]{:S(2)}) collective-permute-start(f32[2,64,512]{2,1,0:T(8,128)} %get-tuple-element.23), channel_id=1, source_target_pairs={{1,0},{2,1},{3,2},{4,3},{5,4},{6,5},{7,6},{8,7},{9,8},{10,9},{11,1... | collective-permute-start | bytes 786440 | tf_op jit(solution)/shard_map/ppermute | solution.py:329
  8.7 2.3 %reshape.18 = f32[64,9,192]{2,1,0:T(8,128)} reshape(f32[64,1728]{1,0:T(8,128)} %param.18) | data formatting | bytes 884736 | tf_op jit(solution)/shard_map/reshape | solution.py:311
  11.0 1.9 %select_maximum_fusion.1 = f32[9,256,128]{1,0,2:T(8,128)S(1)} fusion(f32[9,192,64]{1,0,2:T(8,128)} %bitcast.21), kind=kLoop, calls=%fused_computation.5 | loop fusion | flops 1474560 | bytes 1622016 | tf_op jit(solution)/shard_map/concatenate | solution.py:314
  14.4 2.3 %reduce-precision_convert_fusion.3 = (bf16[2304,128]{1,0:T(8,128)(2,1)S(1)}, bf16[2304,128]{1,0:T(8,128)(2,1)}) fusion(f32[9,256,128]{2,1,0:T(8,128)} %copy.20), kind=kLoop, calls=%fused_computation.15 | loop fusion | flops 1179648 | bytes 2359296 | tf_op jit(solution)/shard_map/convert_element_type | solution.py:307
  16.8 2.2 %copy.21 = f32[128,3456]{0,1:T(8,128)S(1)} copy(f32[128,3456]{1,0:T(8,128)} %param.21) | data formatting | bytes 3538944 | tf_op args[7]
  19.0 1.5 %reduce-precision_convert_fusion.1 = (bf16[3456,128]{1,0:T(8,128)(2,1)}, bf16[3456,128]{1,0:T(8,128)(2,1)}) fusion(f32[128,3456]{0,1:T(8,128)S(1)} %copy.21), kind=kLoop, calls=%fused_computation.3 | loop fusion | flops 1769472 | bytes 3538944 | tf_op jit(solution)/shard_map/convert_element_type | solution.py:307
  21.5 4.1 %shard_map.136 = (f32[4,4,8,8,128]{4,3,2,1,0:T(8,128)S(1)}, f32[136,128]{1,0:T(8,128)S(1)}) custom-call(s32[4]{0:T(128)S(1)} %copy-done.5, s32[4,26]{1,0:T(4,128)S(1)} %copy-done.3, f32[2,64,512]{2,1,0:T(8,128)S(1)} %collective-permute-done.low_ref, f32[4,64,512]{2,1,0:T(8,128)S(1)} %copy-done, f32[2,64,512]{2,1,0:T(8,128)S(1)} %collective-permute-done.1.high_ref, ...), custom_call_target="tpu_custom_call" | custom-call | flops 1811939328 | bytes 2097152 | tf_op jit(solution)/shard_map/pallas_call | solution.py:337
  27.5 6.1 %all-to-all-start = ((f32[16,136,128]{2,1,0:T(8,128)}), f32[16,136,128]{2,1,0:T(8,128)S(1)}, u32[]{:S(2)}, u32[]{:S(2)}) async-start(f32[16,136,128]{2,1,0:T(8,128)} %broadcast_in_dim.12), calls=%async_computation | async-start | bytes 2228224 | tf_op jit(solution)/shard_map/all_to_all | solution.py:370
  33.6 1.6 %pad_maximum_fusion.weight_ref = bf16[3456,256]{1,0:T(8,128)(2,1)S(1)} fusion(bf16[3456,128]{1,0:T(8,128)(2,1)} %get-tuple-element.16, bf16[3456,128]{1,0:T(8,128)(2,1)} %get-tuple-element.15), kind=kLoop, calls=%fused_computation.10 | loop fusion | flops 3538944 | bytes 3538944 | tf_op jit(solution)/shard_map/concatenate | solution.py:307
  35.2 2.7 %copy.22 = f32[128,3456]{0,1:T(8,128)} copy(f32[128,3456]{1,0:T(8,128)} %param.23) | data formatting | bytes 3538944 | tf_op args[9]
  38.0 3.0 %reduce-precision_convert_fusion = (bf16[3456,128]{1,0:T(8,128)(2,1)}, bf16[3456,128]{1,0:T(8,128)(2,1)}) fusion(f32[128,3456]{0,1:T(8,128)} %copy.22), kind=kLoop, calls=%fused_computation.1 | loop fusion | flops 1769472 | bytes 3538944 | tf_op jit(solution)/shard_map/convert_element_type | solution.py:307
  41.0 5.8 %all-to-all-done.all_ref = f32[16,136,128]{2,1,0:T(8,128)S(1)} async-done(((f32[16,136,128]{2,1,0:T(8,128)}), f32[16,136,128]{2,1,0:T(8,128)S(1)}, u32[]{:S(2)}, u32[]{:S(2)}) %all-to-all-start) | async-done | bytes 1114144 | tf_op jit(solution)/shard_map/all_to_all | solution.py:370
  46.8 2.9 %shard_map.137 = (f32[2,2,2,8,8,128]{5,4,3,2,1,0:T(8,128)}, s32[64]{0:T(128)S(1)}) custom-call(f32[16,136,128]{2,1,0:T(8,128)S(1)} %all-to-all-done.all_ref), custom_call_target="tpu_custom_call" | custom-call | flops 1048576 | bytes 2097152 | tf_op jit(solution)/shard_map/pallas_call | solution.py:337
  49.7 10.4 %collective-permute-start.2 = (f32[2,2,2,8,8,128]{5,4,3,2,1,0:T(8,128)}, f32[2,2,2,8,8,128]{5,4,3,2,1,0:T(8,128)S(1)}, u32[]{:S(2)}, u32[]{:S(2)}) collective-permute-start(f32[2,2,2,8,8,128]{5,4,3,2,1,0:T(8,128)} %get-tuple-element.12.own_ref), channel_id=1, source_target_pairs={{0,1},{1,2},{2,3},{3,4},{4,5},{5,6},{6,7},{7,8},{8,9},{9,10},{10,1... | collective-permute-start | bytes 786440 | tf_op jit(solution)/shard_map/ppermute | solution.py:329
  60.1 1.9 %collective-permute-start.3 = (f32[2,2,2,8,8,128]{5,4,3,2,1,0:T(8,128)}, f32[2,2,2,8,8,128]{5,4,3,2,1,0:T(8,128)S(1)}, u32[]{:S(2)}, u32[]{:S(2)}) collective-permute-start(f32[2,2,2,8,8,128]{5,4,3,2,1,0:T(8,128)} %get-tuple-element.12.own_ref), channel_id=1, source_target_pairs={{1,0},{2,1},{3,2},{4,3},{5,4},{6,5},{7,6},{8,7},{9,8},{10,9},{11,1... | collective-permute-start | bytes 786440 | tf_op jit(solution)/shard_map/ppermute | solution.py:329
  63.7 9.7 %collective-permute-done.3.high_ref = f32[2,2,2,8,8,128]{5,4,3,2,1,0:T(8,128)S(1)} collective-permute-done((f32[2,2,2,8,8,128]{5,4,3,2,1,0:T(8,128)}, f32[2,2,2,8,8,128]{5,4,3,2,1,0:T(8,128)S(1)}, u32[]{:S(2)}, u32[]{:S(2)}) %collective-permute-start.3) | collective-permute-done | bytes 262176 | tf_op jit(solution)/shard_map/ppermute | solution.py:329
  73.5 5.9 %shard_map.138.own_ref = f32[2,8,8,8,128]{4,3,2,1,0:T(8,128)S(1)} custom-call(s32[2,26]{1,0:T(2,128)S(1)} %copy-done.4, f32[2,2,2,8,8,128]{5,4,3,2,1,0:T(8,128)S(1)} %collective-permute-done.2.low_ref, f32[2,2,2,8,8,128]{5,4,3,2,1,0:T(8,128)} %get-tuple-element.12.own_ref, f32[2,2,2,8,8,128]{5,4,3,2,1,0:T(8,128)S(1)} %collective-permute-done.3.high_ref, ...), custom_call_target="tpu_custom_call" | custom-call | flops 2717908992 | bytes 2097152 | tf_op jit(solution)/shard_map/pallas_call | solution.py:337
  79.4 1.9 %collective-permute-start.4 = (f32[2,8,8,8,128]{4,3,2,1,0:T(8,128)S(1)}, f32[2,8,8,8,128]{4,3,2,1,0:T(8,128)S(1)}, u32[]{:S(2)}, u32[]{:S(2)}) collective-permute-start(f32[2,8,8,8,128]{4,3,2,1,0:T(8,128)S(1)} %shard_map.138.own_ref), channel_id=1, source_target_pairs={{0,1},{1,2},{2,3},{3,4},{4,5},{5,6},{6,7},{7,8},{8,9},{9,10},{10,1... | collective-permute-start | bytes 1572872 | tf_op jit(solution)/shard_map/ppermute | solution.py:329
  81.3 3.5 %collective-permute-start.5 = (f32[2,8,8,8,128]{4,3,2,1,0:T(8,128)S(1)}, f32[2,8,8,8,128]{4,3,2,1,0:T(8,128)S(1)}, u32[]{:S(2)}, u32[]{:S(2)}) collective-permute-start(f32[2,8,8,8,128]{4,3,2,1,0:T(8,128)S(1)} %shard_map.138.own_ref), channel_id=1, source_target_pairs={{1,0},{2,1},{3,2},{4,3},{5,4},{6,5},{7,6},{8,7},{9,8},{10,9},{11,1... | collective-permute-start | bytes 1572872 | tf_op jit(solution)/shard_map/ppermute | solution.py:329
  85.1 4.2 %collective-permute-done.4.low_ref = f32[2,8,8,8,128]{4,3,2,1,0:T(8,128)S(1)} collective-permute-done((f32[2,8,8,8,128]{4,3,2,1,0:T(8,128)S(1)}, f32[2,8,8,8,128]{4,3,2,1,0:T(8,128)S(1)}, u32[]{:S(2)}, u32[]{:S(2)}) %collective-permute-start.4) | collective-permute-done | bytes 524320 | tf_op jit(solution)/shard_map/ppermute | solution.py:329
  89.3 7.9 %collective-permute-done.5.high_ref = f32[2,8,8,8,128]{4,3,2,1,0:T(8,128)S(1)} collective-permute-done((f32[2,8,8,8,128]{4,3,2,1,0:T(8,128)S(1)}, f32[2,8,8,8,128]{4,3,2,1,0:T(8,128)S(1)}, u32[]{:S(2)}, u32[]{:S(2)}) %collective-permute-start.5) | collective-permute-done | bytes 524320 | tf_op jit(solution)/shard_map/ppermute | solution.py:329
  97.2 7.0 %shard_map.139 = f32[64,32,128]{2,1,0:T(8,128)} custom-call(s32[2,26]{1,0:T(2,128)S(1)} %copy-done.4, s32[64]{0:T(128)S(1)} %get-tuple-element.11.codes_ref, f32[2,8,8,8,128]{4,3,2,1,0:T(8,128)S(1)} %collective-permute-done.4.low_ref, f32[2,8,8,8,128]{4,3,2,1,0:T(8,128)S(1)} %shard_map.138.own_ref, f32[2,8,8,8,128]{4,3,2,1,0:T(8,128)S(1)} %collective-permute-done.5.high_ref, ...), custom_call_target="tpu_custom_call" | custom-call | flops 2717908992 | bytes 2097152 | tf_op jit(solution)/shard_map/pallas_call | solution.py:337
  104.3 6.2 %all-to-all-start.1 = ((f32[16,128,128]{2,1,0:T(8,128)}), f32[16,128,128]{2,1,0:T(8,128)S(1)}, u32[]{:S(2)}, u32[]{:S(2)}) async-start(f32[16,128,128]{2,1,0:T(8,128)} %bitcast.8), calls=%async_computation.1 | async-start | bytes 2097152 | tf_op jit(solution)/shard_map/all_to_all | solution.py:408
  110.8 1.8 %select_maximum_fusion = f32[9,256,128]{1,0,2:T(8,128)} fusion(f32[9,192,64]{1,0,2:T(8,128)S(1)} %bitcast.22), kind=kLoop, calls=%fused_computation.4 | loop fusion | flops 1474560 | bytes 1622016 | tf_op jit(solution)/shard_map/concatenate | solution.py:314
  112.5 1.8 %copy.24 = f32[9,256,128]{2,1,0:T(8,128)S(1)} copy(f32[9,256,128]{1,0,2:T(8,128)} %select_maximum_fusion) | data formatting | bytes 2359296 | tf_op jit(solution)/shard_map/concatenate | solution.py:314
  115.7 3.3 %all-to-all-done.1.risen_ref = f32[16,128,128]{2,1,0:T(8,128)S(1)} async-done(((f32[16,128,128]{2,1,0:T(8,128)}), f32[16,128,128]{2,1,0:T(8,128)S(1)}, u32[]{:S(2)}, u32[]{:S(2)}) %all-to-all-start.1) | async-done | bytes 1048608 | tf_op jit(solution)/shard_map/all_to_all | solution.py:408
  119.3 11.5 %collective-permute-start.6 = (f32[2,4,8,8,128]{4,3,2,1,0:T(8,128)S(1)}, f32[2,4,8,8,128]{4,3,2,1,0:T(8,128)S(1)}, u32[]{:S(2)}, u32[]{:S(2)}) collective-permute-start(f32[2,4,8,8,128]{4,3,2,1,0:T(8,128)S(1)} %get-tuple-element.22), channel_id=1, source_target_pairs={{0,1},{1,2},{2,3},{3,4},{4,5},{5,6},{6,7},{7,8},{8,9},{9,10},{10,1... | collective-permute-start | bytes 786440 | tf_op jit(solution)/shard_map/ppermute | solution.py:329
  130.8 1.9 %collective-permute-start.7 = (f32[2,4,8,8,128]{4,3,2,1,0:T(8,128)S(1)}, f32[2,4,8,8,128]{4,3,2,1,0:T(8,128)S(1)}, u32[]{:S(2)}, u32[]{:S(2)}) collective-permute-start(f32[2,4,8,8,128]{4,3,2,1,0:T(8,128)S(1)} %get-tuple-element.21), channel_id=1, source_target_pairs={{1,0},{2,1},{3,2},{4,3},{5,4},{6,5},{7,6},{8,7},{9,8},{10,9},{11,1... | collective-permute-start | bytes 786440 | tf_op jit(solution)/shard_map/ppermute | solution.py:329
  134.2 9.8 %collective-permute-done.7.high_ref = f32[2,4,8,8,128]{4,3,2,1,0:T(8,128)S(1)} collective-permute-done((f32[2,4,8,8,128]{4,3,2,1,0:T(8,128)S(1)}, f32[2,4,8,8,128]{4,3,2,1,0:T(8,128)S(1)}, u32[]{:S(2)}, u32[]{:S(2)}) %collective-permute-start.7) | collective-permute-done | bytes 262176 | tf_op jit(solution)/shard_map/ppermute | solution.py:329
  144.0 4.4 %shard_map.141 = f32[4,64,512]{2,1,0:T(8,128)} custom-call(s32[4,26]{1,0:T(4,128)S(1)} %copy-done.3, f32[2,4,8,8,128]{4,3,2,1,0:T(8,128)S(1)} %collective-permute-done.6.low_ref, f32[4,4,8,8,128]{4,3,2,1,0:T(8,128)S(1)} %shard_map.140.own_ref, f32[2,4,8,8,128]{4,3,2,1,0:T(8,128)S(1)} %collective-permute-done.7.high_ref, f32[4,64,512]{2,1,0:T(8,128)S(1)} %copy-done, ...), custom_call_target="tpu_custom_call" | custom-call | flops 1811939328 | bytes 2097152 | tf_op jit(solution)/shard_map/pallas_call | solution.py:337
  (58 shorter events, 9.6 us)
Async XLA Ops:
  1.9 18.8 %collective-permute-start = (f32[2,64,512]{2,1,0:T(8,128)}, f32[2,64,512]{2,1,0:T(8,128)S(1)}, u32[]{:S(2)}, u32[]{:S(2)}) collective-permute-start(f32[2,64,512]{2,1,0:T(8,128)} %get-tuple-element.24), channel_id=1, source_target_pairs={{0,1},{1,2},{2,3},{3,4},{4,5},{5,6},{6,7},{7,8},{8,9},{9,10},{10,1... | collective-permute-start | bytes 786440 | tf_op jit(solution)/shard_map/ppermute | solution.py:329
  6.8 13.9 %collective-permute-start.1 = (f32[2,64,512]{2,1,0:T(8,128)}, f32[2,64,512]{2,1,0:T(8,128)S(1)}, u32[]{:S(2)}, u32[]{:S(2)}) collective-permute-start(f32[2,64,512]{2,1,0:T(8,128)} %get-tuple-element.23), channel_id=1, source_target_pairs={{1,0},{2,1},{3,2},{4,3},{5,4},{6,5},{7,6},{8,7},{9,8},{10,9},{11,1... | collective-permute-start | bytes 786440 | tf_op jit(solution)/shard_map/ppermute | solution.py:329
  14.4 2.3 %copy-start.16 = (f32[64]{0:T(128)S(1)}, f32[64]{0:T(128)}, u32[]{:S(2)}) copy-start(f32[64]{0:T(128)} %param.19) | copy-start | bytes 772
  19.0 1.5 %copy-start.12 = (bf16[2304,128]{1,0:T(8,128)(2,1)S(1)}, bf16[2304,128]{1,0:T(8,128)(2,1)}, u32[]{:S(2)}) copy-start(bf16[2304,128]{1,0:T(8,128)(2,1)} %get-tuple-element.20) | copy-start | bytes 1769476
  20.5 1.0 copy-start
  20.5 1.0 copy-start.3
  20.5 1.0 copy-start.5
  25.7 0.8 copy-start.1
  27.5 19.2 %all-to-all-start = ((f32[16,136,128]{2,1,0:T(8,128)}), f32[16,136,128]{2,1,0:T(8,128)S(1)}, u32[]{:S(2)}, u32[]{:S(2)}) async-start(f32[16,136,128]{2,1,0:T(8,128)} %broadcast_in_dim.12), calls=%async_computation | async-start | bytes 2228224 | tf_op jit(solution)/shard_map/all_to_all | solution.py:370
  38.0 24.1 %copy-start.14 = (f32[128,64]{0,1:T(8,128)S(1)}, f32[128,64]{0,1:T(8,128)}, u32[]{:S(2)}) copy-start(f32[128,64]{0,1:T(8,128)} %param.20) | copy-start | bytes 98308
  38.0 24.1 %copy-start.15 = (f32[64,128]{1,0:T(8,128)S(1)}, f32[64,128]{1,0:T(8,128)}, u32[]{:S(2)}) copy-start(f32[64,128]{1,0:T(8,128)} %param.25) | copy-start | bytes 98308
  41.0 32.5 %copy-start.4 = (s32[2,26]{1,0:T(2,128)S(1)}, s32[2,26]{1,0:T(2,128)}, u32[]{:S(2)}) copy-start(s32[2,26]{1,0:T(2,128)} %links_ref.6) | copy-start | bytes 628
  41.0 32.5 %copy-start.6 = (f32[128]{0:T(128)S(1)}, f32[128]{0:T(128)}, u32[]{:S(2)}) copy-start(f32[128]{0:T(128)} %param.22) | copy-start | bytes 1540
  49.7 14.1 %collective-permute-start.2 = (f32[2,2,2,8,8,128]{5,4,3,2,1,0:T(8,128)}, f32[2,2,2,8,8,128]{5,4,3,2,1,0:T(8,128)S(1)}, u32[]{:S(2)}, u32[]{:S(2)}) collective-permute-start(f32[2,2,2,8,8,128]{5,4,3,2,1,0:T(8,128)} %get-tuple-element.12.own_ref), channel_id=1, source_target_pairs={{0,1},{1,2},{2,3},{3,4},{4,5},{5,6},{6,7},{7,8},{8,9},{9,10},{10,1... | collective-permute-start | bytes 786440 | tf_op jit(solution)/shard_map/ppermute | solution.py:329
  60.1 13.3 %collective-permute-start.3 = (f32[2,2,2,8,8,128]{5,4,3,2,1,0:T(8,128)}, f32[2,2,2,8,8,128]{5,4,3,2,1,0:T(8,128)S(1)}, u32[]{:S(2)}, u32[]{:S(2)}) collective-permute-start(f32[2,2,2,8,8,128]{5,4,3,2,1,0:T(8,128)} %get-tuple-element.12.own_ref), channel_id=1, source_target_pairs={{1,0},{2,1},{3,2},{4,3},{5,4},{6,5},{7,6},{8,7},{9,8},{10,9},{11,1... | collective-permute-start | bytes 786440 | tf_op jit(solution)/shard_map/ppermute | solution.py:329
  73.5 11.4 %copy-start.8 = (bf16[3456,128]{1,0:T(8,128)(2,1)S(1)}, bf16[3456,128]{1,0:T(8,128)(2,1)}, u32[]{:S(2)}) copy-start(bf16[3456,128]{1,0:T(8,128)(2,1)} %get-tuple-element.13) | copy-start | bytes 2654212
  73.5 11.4 %copy-start.9 = (bf16[3456,128]{1,0:T(8,128)(2,1)S(1)}, bf16[3456,128]{1,0:T(8,128)(2,1)}, u32[]{:S(2)}) copy-start(bf16[3456,128]{1,0:T(8,128)(2,1)} %get-tuple-element.14) | copy-start | bytes 2654212
  79.4 9.9 %collective-permute-start.4 = (f32[2,8,8,8,128]{4,3,2,1,0:T(8,128)S(1)}, f32[2,8,8,8,128]{4,3,2,1,0:T(8,128)S(1)}, u32[]{:S(2)}, u32[]{:S(2)}) collective-permute-start(f32[2,8,8,8,128]{4,3,2,1,0:T(8,128)S(1)} %shard_map.138.own_ref), channel_id=1, source_target_pairs={{0,1},{1,2},{2,3},{3,4},{4,5},{5,6},{6,7},{7,8},{8,9},{9,10},{10,1... | collective-permute-start | bytes 1572872 | tf_op jit(solution)/shard_map/ppermute | solution.py:329
  81.3 15.9 %collective-permute-start.5 = (f32[2,8,8,8,128]{4,3,2,1,0:T(8,128)S(1)}, f32[2,8,8,8,128]{4,3,2,1,0:T(8,128)S(1)}, u32[]{:S(2)}, u32[]{:S(2)}) collective-permute-start(f32[2,8,8,8,128]{4,3,2,1,0:T(8,128)S(1)} %shard_map.138.own_ref), channel_id=1, source_target_pairs={{1,0},{2,1},{3,2},{4,3},{5,4},{6,5},{7,6},{8,7},{9,8},{10,9},{11,1... | collective-permute-start | bytes 1572872 | tf_op jit(solution)/shard_map/ppermute | solution.py:329
  84.9 12.3 %copy-start.7 = (f32[128]{0:T(128)S(1)}, f32[128]{0:T(128)}, u32[]{:S(2)}) copy-start(f32[128]{0:T(128)} %param.24) | copy-start | bytes 1540
  104.3 6.2 %copy-start.13 = (f32[64,1728]{1,0:T(8,128)S(1)}, f32[64,1728]{1,0:T(8,128)}, u32[]{:S(2)}) copy-start(f32[64,1728]{1,0:T(8,128)} %param.26) | copy-start | bytes 1327108
  104.3 14.7 %all-to-all-start.1 = ((f32[16,128,128]{2,1,0:T(8,128)}), f32[16,128,128]{2,1,0:T(8,128)S(1)}, u32[]{:S(2)}, u32[]{:S(2)}) async-start(f32[16,128,128]{2,1,0:T(8,128)} %bitcast.8), calls=%async_computation.1 | async-start | bytes 2097152 | tf_op jit(solution)/shard_map/all_to_all | solution.py:408
  112.5 1.8 %copy-start.17 = (f32[64]{0:T(128)S(1)}, f32[64]{0:T(128)}, u32[]{:S(2)}) copy-start(f32[64]{0:T(128)} %param.27) | copy-start | bytes 772
  114.4 4.6 %copy-start.2 = (f32[4,4,8,8,128]{4,3,2,1,0:T(8,128)S(1)}, f32[4,4,8,8,128]{4,3,2,1,0:T(8,128)}, u32[]{:S(2)}) copy-start(f32[4,4,8,8,128]{4,3,2,1,0:T(8,128)} %copy-done.1) | copy-start | bytes 1572868
  115.7 17.1 %copy-start.10 = (bf16[2304,128]{1,0:T(8,128)(2,1)S(1)}, bf16[2304,128]{1,0:T(8,128)(2,1)}, u32[]{:S(2)}) copy-start(bf16[2304,128]{1,0:T(8,128)(2,1)} %get-tuple-element.17) | copy-start | bytes 1769476
  115.7 17.1 %copy-start.11 = (bf16[2304,128]{1,0:T(8,128)(2,1)S(1)}, bf16[2304,128]{1,0:T(8,128)(2,1)}, u32[]{:S(2)}) copy-start(bf16[2304,128]{1,0:T(8,128)(2,1)} %get-tuple-element.18) | copy-start | bytes 1769476
  119.3 14.9 %collective-permute-start.6 = (f32[2,4,8,8,128]{4,3,2,1,0:T(8,128)S(1)}, f32[2,4,8,8,128]{4,3,2,1,0:T(8,128)S(1)}, u32[]{:S(2)}, u32[]{:S(2)}) collective-permute-start(f32[2,4,8,8,128]{4,3,2,1,0:T(8,128)S(1)} %get-tuple-element.22), channel_id=1, source_target_pairs={{0,1},{1,2},{2,3},{3,4},{4,5},{5,6},{6,7},{7,8},{8,9},{9,10},{10,1... | collective-permute-start | bytes 786440 | tf_op jit(solution)/shard_map/ppermute | solution.py:329
  130.8 13.1 %collective-permute-start.7 = (f32[2,4,8,8,128]{4,3,2,1,0:T(8,128)S(1)}, f32[2,4,8,8,128]{4,3,2,1,0:T(8,128)S(1)}, u32[]{:S(2)}, u32[]{:S(2)}) collective-permute-start(f32[2,4,8,8,128]{4,3,2,1,0:T(8,128)S(1)} %get-tuple-element.21), channel_id=1, source_target_pairs={{1,0},{2,1},{3,2},{4,3},{5,4},{6,5},{7,6},{8,7},{9,8},{10,9},{11,1... | collective-permute-start | bytes 786440 | tf_op jit(solution)/shard_map/ppermute | solution.py:329

commit v2 on v1

v2 whole, which is shorter than its diff:
```python
import jax
import jax.numpy as jnp
from jax import lax
from jax.experimental import pallas as pl
from jax.experimental.pallas import tpu as pltpu
from jax.sharding import PartitionSpec as P

F32, BF16 = jnp.float32, jnp.bfloat16
BOTH = ("grp", "dev")
STEPS = (-1, 0, 1)
COLUMN = {
    offset: k
    for k, offset in enumerate(
        (x, y, z) for x in STEPS for y in STEPS for z in STEPS if (x, y, z) != (0, 0, 0)
    )
}
PLANE = {-1: (56, 8), 0: (0, 64), 1: (0, 8)}
ROOM = {-1: slice(0, 1), 0: slice(1, 9), 1: slice(9, 10)}
VMEM = pl.BlockSpec(memory_space=pltpu.VMEM)
SMEM = pl.BlockSpec(memory_space=pltpu.SMEM)


def silu(v):
    return v / (1.0 + jnp.exp(-v))


def split(v):
    high = v.astype(BF16)
    return high, (v - high.astype(F32)).astype(BF16)


def low_lanes(shape):
    return lax.broadcasted_iota(jnp.int32, shape, len(shape) - 1) < 64


def swap(v):
    return pltpu.roll(v, 64, v.ndim - 1)


def device_number():
    return lax.axis_index("grp") * lax.axis_size("dev") + lax.axis_index("dev")


def neighbours(links_ref, row, start, none):
    found = {}
    for offset, k in COLUMN.items():
        link = links_ref[row, k]
        found[offset] = jnp.where(link < 0, none, link - start)
    return found


def planes(source, brick, z, dx):
    at, count = PLANE[dx]
    return source[brick, 64 * z + at : 64 * z + at + count, :].reshape(count // 8, 8, 128)


def even_device():
    return device_number() % 2 == 0


def fine_pack(brick_ref, n, out_ref, m, middle):
    first, last = brick_ref[n, 0:64], brick_ref[n, 192:256]
    lower = low_lanes(first.shape)
    out_ref[m, 0:64] = jnp.where(lower, last, first)
    middle[0:64] = jnp.where(lower, first, last)
    middle[64:192] = brick_ref[n, 64:192]
    for k in range(3):
        out_ref[m, 64 + 8 * k : 72 + 8 * k] = middle[64 * k : 64 * k + 8]
        out_ref[m, 88 + 8 * k : 96 + 8 * k] = middle[64 * k + 56 : 64 * k + 64]
    out_ref[m, 112:136] = middle[pl.ds(0, 24, 8), :]
    out_ref[m, 136:160] = middle[pl.ds(7, 24, 8), :]


def fine_unpack(packed_ref, m, source, n, middle):
    middle[pl.ds(0, 24, 8), :] = packed_ref[m, 112:136]
    middle[pl.ds(7, 24, 8), :] = packed_ref[m, 136:160]
    for k in range(3):
        middle[64 * k : 64 * k + 8] = packed_ref[m, 64 + 8 * k : 72 + 8 * k]
        middle[64 * k + 56 : 64 * k + 64] = packed_ref[m, 88 + 8 * k : 96 + 8 * k]
    ends, inner = packed_ref[m, 0:64], middle[0:64]
    lower = low_lanes(ends.shape)
    source[n, 0:64] = jnp.where(lower, inner, ends)
    source[n, 64:192] = middle[64:192]
    source[n, 192:256] = jnp.where(lower, ends, inner)


def fine_halo(first_ref, second_ref, source, middle):
    even = even_device()
    for packed_ref, at in ((first_ref, jnp.where(even, 6, 0)), (second_ref, jnp.where(even, 0, 6))):
        for m in range(2):
            fine_unpack(packed_ref, m, source, at + m, middle)


def fine_sends(brick_ref, first_ref, second_ref, middle):
    even = even_device()
    for out_ref, at in ((first_ref, jnp.where(even, 2, 0)), (second_ref, jnp.where(even, 0, 2))):
        for m in range(2):
            fine_pack(brick_ref, at + m, out_ref, m, middle)


def shifted_rows(tile):
    below, here, above = tile(-1), tile(0), tile(1)
    axis = here.ndim - 2
    row = lax.broadcasted_iota(jnp.int32, here.shape, axis)
    return (
        pltpu.roll(jnp.where(row == 7, below, here), 1, axis),
        here,
        pltpu.roll(jnp.where(row == 0, above, here), 7, axis),
    )


def product(high, low, weight_ref):
    both = jnp.dot(high, weight_ref[...], preferred_element_type=F32)
    half = both.shape[1] // 2
    rest = jnp.dot(low, weight_ref[:, :half], preferred_element_type=F32)
    return both[:, :half] + both[:, half:] + rest


def fine_rim(source, links_ref, high, low):
    start = device_number() * 4 - 2
    for pair in range(2):
        found = []
        for b in (2 * pair, 2 * pair + 1):
            near = neighbours(links_ref, b, start, 8)
            near[0, 0, 0] = b + 2
            found.append(near)
        for k in range(5):
            for dx in STEPS:
                rows = []
                for near in found:

                    def tile(dy):
                        first = near[dx, dy, -1 if k == 0 else 0]
                        second = near[dx, dy, 1 if k == 4 else 0]
                        a = planes(source, first, (k + 3) % 4, dx)
                        b = planes(source, second, k % 4, dx)
                        return jnp.where(low_lanes(a.shape), a, b)

                    rows.append(shifted_rows(tile))
                for j in range(3):
                    both = jnp.concatenate([rows[0][j], rows[1][j]], axis=1)
                    h, l = split(both)
                    high[j, k, ROOM[dx], 16 * pair : 16 * pair + 16, :] = h
                    low[j, k, ROOM[dx], 16 * pair : 16 * pair + 16, :] = l


def fine_columns(padded, zz):
    return jnp.concatenate(
        [
            padded[j, zz + h, i : i + 8].reshape(256, 128)
            for i in range(3)
            for j in range(3)
            for h in range(2)
        ],
        axis=1,
    )


def turn_kernel(features_ref, own_ref, first_ref, second_ref, flat, middle):
    for p in range(2):
        flat[...] = features_ref[2 * p : 2 * p + 2].reshape(128, 512).T
        for zz in range(4):
            odd = flat[pl.ds(2 * zz + 1, 64, 8), :]
            even = flat[pl.ds(2 * zz, 64, 8), :]
            lower = low_lanes(odd.shape)
            own_ref[2 * p, 64 * zz : 64 * zz + 64] = jnp.where(lower, odd, swap(even))
            own_ref[2 * p + 1, 64 * zz : 64 * zz + 64] = jnp.where(lower, swap(odd), even)
    fine_sends(own_ref, first_ref, second_ref, middle)


def fine_weight_rows(weight_ref, out_ref):
    taps = []
    for at in range(0, 1728, 128):
        part = weight_ref[:, at : min(at + 128, 1728)]
        turned = jnp.concatenate([part, part], axis=0).T
        taps += [turned[r : r + 64] for r in range(0, turned.shape[0], 64)]
    nothing = jnp.zeros((64, 128), F32)
    lower = low_lanes((64, 128))
    for n in range(9):
        for z in range(4):
            odd = taps[3 * n + z - 1] if z >= 1 else nothing
            even = taps[3 * n + z] if z <= 2 else nothing
            h, l = split(jnp.where(lower, odd, even))
            at = 256 * n + 64 * z
            out_ref[at : at + 64, 0:128] = h
            out_ref[at : at + 64, 128:256] = l


def coarse_weight_rows(weight_ref, out_ref):
    for at in range(0, 3456, 128):
        h, l = split(weight_ref[:, at : at + 128].T)
        out_ref[at : at + 128, 0:128] = h
        out_ref[at : at + 128, 128:256] = l


def first_weight_kernel(weight_ref, out_ref):
    fine_weight_rows(weight_ref, out_ref)


def later_weights_kernel(
    first_ref, second_ref, down_ref, up_ref, fine_ref, first_out, second_out, down_out, up_out, fine_out
):
    coarse_weight_rows(first_ref, first_out)
    coarse_weight_rows(second_ref, second_out)
    fine_weight_rows(fine_ref, fine_out)
    nothing = jnp.zeros((64, 128), F32)
    h, l = split(jnp.concatenate([down_ref[...].T, nothing], axis=0))
    down_out[:, 0:128] = h
    down_out[:, 256:384] = l
    h, l = split(jnp.concatenate([nothing, down_ref[...].T], axis=0))
    down_out[:, 128:256] = h
    down_out[:, 384:512] = l
    both = jnp.concatenate([up_ref[...], up_ref[...]], axis=0).T
    lower = low_lanes(both.shape)
    for k in range(2):
        h, l = split(jnp.where(lower if k == 0 else ~lower, both, 0.0))
        up_out[128 * k : 128 * k + 128, 0:128] = h
        up_out[128 * k : 128 * k + 128, 128:256] = l


def fine_in_kernel(
    codes_ref, links_ref, own_ref, first_ref, second_ref, weight_ref, bias_ref,
    hidden_ref, pooled_ref, source, high, low, sums, middle,
):
    source[8] = jnp.zeros((256, 128), F32)
    source[2:6] = own_ref[...]
    fine_halo(first_ref, second_ref, source, middle)
    fine_rim(source, links_ref, high, low)
    bias = jnp.concatenate([bias_ref[...]] * 2, axis=1)
    held = []
    for zz in range(4):
        r = product(fine_columns(high, zz), fine_columns(low, zz), weight_ref) + bias
        r = silu(r).reshape(8, 32, 128)
        for b in range(4):
            hidden_ref[b, 64 * zz : 64 * zz + 64] = r[:, 8 * b : 8 * b + 8].reshape(64, 128)
        r = r.reshape(4, 2, 32, 128)
        r = r[:, 0] + r[:, 1]
        held.append(r + swap(r))
        if zz % 2 == 1:
            both = jnp.where(low_lanes(r.shape), held[zz - 1], held[zz])
            sums[64 * zz - 64 : 64 * zz + 64, :] = both.reshape(128, 128)
    means = (sums[pl.ds(0, 128, 2), :] + sums[pl.ds(1, 128, 2), :]) * 0.125
    for n in range(8):
        for b in range(4):
            at = (4 * n + b) * 4
            pooled_ref[0, 32 * b + 4 * n : 32 * b + 4 * n + 4, :] = means[at : at + 4]
    lane = lax.broadcasted_iota(jnp.int32, (8, 128), 1)
    named = jnp.zeros((8, 128), F32)
    for b in range(4):
        named = jnp.where(lane == b, codes_ref[b].astype(F32), named)
    pooled_ref[0, 128:136, :] = named
    for k in range(1, 16):
        pooled_ref[k] = pooled_ref[0]


def cube_rows(all_ref, place_ref, code, store):
    for t in range(16):
        a, b, c = t // 4 % 2, t // 2 % 2, t % 2
        i = place_ref[code + t]
        at = jnp.maximum(i, 0)
        v = all_ref[at // 4, pl.ds(pl.multiple_of(at % 4 * 32, 32), 32), :]
        v = jnp.where(i >= 0, v, 0.0)
        for r in range(8):
            store(t // 8, ((2 * a + c) * 8 + r) * 8 + 4 * b, v[4 * r : 4 * r + 4])


def edge_kernel(all_ref, cubes_ref, place_ref, codes_ref, held, spelled, sem):
    held[...] = all_ref[:, 128, :]
    copy = pltpu.make_async_copy(held, spelled, sem)
    copy.start()
    me = lax.axis_index("dev")
    for t in range(256):
        place_ref[t] = -1
    copy.wait()
    for i in range(64):
        code = spelled[i // 4, i % 4].astype(jnp.int32)
        codes_ref[i] = code
        place_ref[code] = i

    @pl.when((me == 0) | (me == 15))
    def _():
        def store(s, at, v):
            cubes_ref[s, at : at + 4, :] = v

        cube_rows(all_ref, place_ref, jnp.where(me == 0, 15 * 16, 0), store)


def bring_down(cubes, down_ref, source, n):
    h, l = split(cubes)
    based = product(h, l, down_ref).reshape(2, 2, 2, 32, 256)
    for a in range(2):
        for z in range(8):
            source[n, 64 * z + 32 * a : 64 * z + 32 * a + 32] = based[
                a, z // 4, z // 2 % 2, :, 128 * (z % 2) : 128 * (z % 2) + 128
            ]


def base_kernel(all_ref, place_ref, down_ref, out_ref, cubes):
    me = lax.axis_index("dev")
    for n in range(3):
        owner = jnp.clip(me + (n - 1), 0, 15)

        def store(s, at, v):
            cubes[s, at : at + 4, :] = v

        cube_rows(all_ref, place_ref, owner * 16, store)
        for s in range(2):
            bring_down(cubes[s], down_ref, out_ref, 2 * n + s)


def coarse_rim(source, links_ref, high, low):
    start = device_number() * 2 - 2
    found = []
    for s in range(2):
        near = neighbours(links_ref, s, start, 6)
        near[0, 0, 0] = s + 2
        found.append(near)
    for z in range(10):
        dz = -1 if z == 0 else 1 if z == 9 else 0
        at = {-1: 7, 0: z - 1, 1: 0}[dz]
        for dx in STEPS:
            rows = [
                shifted_rows(lambda dy, near=near: planes(source, near[dx, dy, dz], at, dx))
                for near in found
            ]
            for j in range(3):
                h, l = split(jnp.concatenate([rows[0][j], rows[1][j]], axis=1))
                high[j, z, ROOM[dx]] = h
                low[j, z, ROOM[dx]] = l


def coarse_columns(padded, z):
    return jnp.concatenate(
        [
            padded[j, z + l : z + l + 2, i : i + 8].reshape(256, 128)
            for i in range(3)
            for j in range(3)
            for l in range(3)
        ],
        axis=1,
    )


def coarse_first_kernel(
    links_ref, based_ref, edge_ref, down_ref, weight_ref, bias_ref, first_ref, packed_ref, source, high, low
):
    source[6] = jnp.zeros((512, 128), F32)
    source[0:6] = based_ref[...]
    me = lax.axis_index("dev")

    @pl.when((me == 0) | (me == 15))
    def _():
        at = jnp.where(me == 0, 0, 4)
        for s in range(2):
            bring_down(edge_ref[s], down_ref, source, at + s)

    coarse_rim(source, links_ref, high, low)
    for z in range(0, 8, 2):
        r = product(coarse_columns(high, z), coarse_columns(low, z), weight_ref) + bias_ref[...]
        r = silu(r).reshape(2, 8, 16, 128)
        for s in range(2):
            first_ref[s, 64 * z : 64 * z + 128] = r[:, :, 8 * s : 8 * s + 8].reshape(128, 128)
    for s in range(2):
        packed_ref[s, 0:64] = first_ref[s, 0:64]
        packed_ref[s, 64:128] = first_ref[s, 448:512]
        for z in range(1, 7):
            packed_ref[s, 120 + 8 * z : 128 + 8 * z] = first_ref[s, 64 * z : 64 * z + 8]
            packed_ref[s, 168 + 8 * z : 176 + 8 * z] = first_ref[s, 64 * z + 56 : 64 * z + 64]
        packed_ref[s, 224:272] = first_ref[s, pl.ds(64, 48, 8), :]
        packed_ref[s, 272:320] = first_ref[s, pl.ds(71, 48, 8), :]


def coarse_second_kernel(
    links_ref, codes_ref, own_ref, first_ref, second_ref, weight_ref, bias_ref, up_ref,
    out_ref, source, high, low, octants,
):
    source[6] = jnp.zeros((512, 128), F32)
    source[2:4] = own_ref[...]
    even = even_device()
    for packed_ref, n in ((first_ref, jnp.where(even, 4, 0)), (second_ref, jnp.where(even, 0, 4))):
        for s in range(2):
            source[n + s, pl.ds(64, 48, 8), :] = packed_ref[s, 224:272]
            source[n + s, pl.ds(71, 48, 8), :] = packed_ref[s, 272:320]
            source[n + s, 0:64] = packed_ref[s, 0:64]
            source[n + s, 448:512] = packed_ref[s, 64:128]
            for z in range(1, 7):
                source[n + s, 64 * z : 64 * z + 8] = packed_ref[s, 120 + 8 * z : 128 + 8 * z]
                source[n + s, 64 * z + 56 : 64 * z + 64] = packed_ref[s, 168 + 8 * z : 176 + 8 * z]
    coarse_rim(source, links_ref, high, low)
    for z in range(0, 8, 2):
        c, q = z // 4, z // 2 % 2
        r = product(coarse_columns(high, z), coarse_columns(low, z), weight_ref) + bias_ref[...]
        r = silu(r)
        h, l = split(jnp.concatenate([r[:128], r[128:]], axis=1))
        lifted = product(h, l, up_ref)
        for t in range(c, 16, 2):
            s, a, b = t // 8, t // 4 % 2, t // 2 % 2
            for x in range(4):
                at = (4 * a + x) * 16 + 8 * s + 4 * b
                octants[t, 16 * q + 4 * x : 16 * q + 4 * x + 4, :] = lifted[at : at + 4]
    base = lax.axis_index("dev") * 16

    def place(i, carry):
        local = codes_ref[i] - base
        known = (local >= 0) & (local < 16)
        v = octants[jnp.clip(local, 0, 15)]
        out_ref[i] = jnp.where(known, v, 0.0)
        return carry

    lax.fori_loop(0, 64, place, 0)


def blend_kernel(hidden_ref, risen_ref, out_ref, first_ref, second_ref, grown, middle):
    risen = risen_ref[0]
    for k in range(1, 16):
        risen = risen + risen_ref[k]
    for b in range(4):
        v = risen[32 * b : 32 * b + 32]
        grown[pl.ds(0, 32, 2), :] = v
        grown[pl.ds(1, 32, 2), :] = v
        full = grown[...].reshape(2, 4, 1, 8, 128)
        turned = swap(full)
        lower = low_lanes(full.shape)
        for h in range(2):
            w = jnp.where(lower, full, turned) if h == 0 else jnp.where(lower, turned, full)
            for q in range(2):
                at = 64 * (2 * q + h)
                v = silu(hidden_ref[b, at : at + 64].reshape(4, 2, 8, 128) + w[q])
                out_ref[b, at : at + 64] = v.reshape(64, 128)
    fine_sends(out_ref, first_ref, second_ref, middle)


def fine_out_kernel(
    links_ref, own_ref, first_ref, second_ref, features_ref, weight_ref, bias_ref,
    out_ref, source, flat, high, low, middle,
):
    source[8] = jnp.zeros((256, 128), F32)
    source[2:6] = own_ref[...]
    fine_halo(first_ref, second_ref, source, middle)
    fine_rim(source, links_ref, high, low)
    bias = jnp.concatenate([bias_ref[...]] * 2, axis=1)
    for zz in range(4):
        r = product(fine_columns(high, zz), fine_columns(low, zz), weight_ref) + bias
        r = r.reshape(8, 32, 128)
        for p in range(2):
            v0 = r[:, 16 * p : 16 * p + 8].reshape(64, 128)
            v1 = r[:, 16 * p + 8 : 16 * p + 16].reshape(64, 128)
            lower = low_lanes(v0.shape)
            flat[p, pl.ds(2 * zz + 1, 64, 8), :] = jnp.where(lower, v0, swap(v1))
            flat[p, pl.ds(2 * zz, 64, 8), :] = jnp.where(lower, swap(v0), v1)
    for p in range(2):
        out_ref[2 * p : 2 * p + 2] = features_ref[2 * p : 2 * p + 2] + flat[p].T.reshape(2, 64, 512)


def exchanged(first, second):
    count = lax.axis_size(BOTH)
    inner = [(i, i ^ 1) for i in range(count)]
    outer = [(i, i + 1) for i in range(1, count - 1, 2)]
    outer += [(b, a) for a, b in outer]
    return lax.ppermute(first, BOTH, inner), lax.ppermute(second, BOTH, outer)


def struct(*shape, dtype=F32):
    return jax.ShapeDtypeStruct(shape, dtype)


def call(kernel, out, scratch, specs, args, flops):
    return pl.pallas_call(
        kernel,
        out_shape=out,
        in_specs=specs,
        out_specs=jax.tree.map(lambda o: SMEM if o.dtype == jnp.int32 else VMEM, out),
        scratch_shapes=scratch,
        cost_estimate=pl.CostEstimate(flops=flops, bytes_accessed=1 << 21, transcendentals=0),
        compiler_params=pltpu.CompilerParams(vmem_limit_bytes=40 << 20),
    )(*args)


def per_device(
    features, fine_links, codes, coarse_links, fine_in_weight, fine_in_bias, down_weight,
    coarse_first_weight, coarse_first_bias, coarse_second_weight, coarse_second_bias,
    up_weight, fine_out_weight, fine_out_bias,
):
    fine_padded = [pltpu.VMEM((3, 5, 10, 32, 128), BF16)] * 2
    coarse_padded = [pltpu.VMEM((3, 10, 10, 16, 128), BF16)] * 2
    fine_source = pltpu.VMEM((9, 256, 128), F32)
    coarse_source = pltpu.VMEM((7, 512, 128), F32)
    middle = pltpu.VMEM((192, 128), F32)
    brick, shell = struct(4, 256, 128), struct(2, 160, 128)

    own, first, second = call(
        turn_kernel,
        (brick, shell, shell),
        [pltpu.VMEM((512, 128), F32), middle],
        [VMEM],
        (features,),
        1 << 20,
    )
    first, second = exchanged(first, second)
    weight_in = call(
        first_weight_kernel, struct(2304, 256, dtype=BF16), [], [VMEM], (fine_in_weight,), 1 << 20
    )
    hidden, pooled = call(
        fine_in_kernel,
        (brick, struct(16, 136, 128)),
        [fine_source, *fine_padded, pltpu.VMEM((256, 128), F32), middle],
        [SMEM, SMEM] + [VMEM] * 5,
        (codes, fine_links, own, first, second, weight_in, fine_in_bias[None]),
        2 * 1024 * 2304 * 384,
    )
    later = (coarse_first_weight, coarse_second_weight, down_weight, up_weight, fine_out_weight)
    pooled, *later = lax.optimization_barrier((pooled, *later))
    weight_first, weight_second, down, up, weight_out = call(
        later_weights_kernel,
        (
            struct(3456, 256, dtype=BF16), struct(3456, 256, dtype=BF16),
            struct(128, 512, dtype=BF16), struct(256, 256, dtype=BF16),
            struct(2304, 256, dtype=BF16),
        ),
        [],
        [VMEM] * 5,
        later,
        1 << 30,
    )
    spread = lax.all_to_all(pooled, "dev", 0, 0, tiled=True)
    cubes, place, group_codes = call(
        edge_kernel,
        (struct(2, 256, 128), struct(256, dtype=jnp.int32), struct(64, dtype=jnp.int32)),
        [pltpu.VMEM((16, 128), F32), pltpu.SMEM((16, 128), F32), pltpu.SemaphoreType.DMA],
        [VMEM],
        (spread,),
        1 << 20,
    )
    groups, devices = lax.axis_size("grp"), lax.axis_size("dev")
    edges = [(g * devices, (g + 1) * devices) for g in range(groups - 1)]
    edges += [((g + 2) * devices - 1, (g + 1) * devices - 1) for g in range(groups - 1)]
    edge = lax.ppermute(cubes, BOTH, edges)
    based = call(
        base_kernel,
        struct(6, 512, 128),
        [pltpu.VMEM((2, 256, 128), F32)],
        [VMEM, SMEM, VMEM],
        (spread, place, down),
        1 << 28,
    )
    first_own, packed = call(
        coarse_first_kernel,
        (struct(2, 512, 128), struct(2, 320, 128)),
        [coarse_source, *coarse_padded],
        [SMEM] + [VMEM] * 5,
        (coarse_links, based, edge, down, weight_first, coarse_first_bias[None]),
        2 * 1024 * 3456 * 384,
    )
    first, second = exchanged(packed, packed)
    lifted = call(
        coarse_second_kernel,
        struct(64, 32, 128),
        [coarse_source, *coarse_padded, pltpu.VMEM((16, 32, 128), F32)],
        [SMEM, SMEM] + [VMEM] * 6,
        (
            coarse_links, group_codes, first_own, first, second, weight_second,
            coarse_second_bias[None], up,
        ),
        2 * 1024 * 3456 * 384,
    )
    risen = lax.all_to_all(lifted.reshape(16, 128, 128), "dev", 0, 0, tiled=True)
    blended, first, second = call(
        blend_kernel,
        (brick, shell, shell),
        [pltpu.VMEM((64, 128), F32), middle],
        [VMEM, VMEM],
        (hidden, risen),
        1 << 20,
    )
    first, second = exchanged(first, second)
    return call(
        fine_out_kernel,
        struct(4, 64, 512),
        [fine_source, pltpu.VMEM((2, 512, 128), F32), *fine_padded, middle],
        [SMEM] + [VMEM] * 6,
        (fine_links, blended, first, second, features, weight_out, fine_out_bias[None]),
        2 * 1024 * 2304 * 384,
    )


def solution(mesh):
    split_first = P(BOTH)
    placed = (split_first,) * 4 + (P(),) * 10
    return jax.shard_map(
        per_device,
        mesh=mesh,
        in_specs=placed,
        out_specs=split_first,
        check_vma=False,
    )
```

time: 149 us -> 118 us (0.79)
  the two profiles are of different devices: /device:TPU:127 before, /device:TPU:97 now
where the time goes in v2:
time: 118 us; the launch traced here: 116 us
  blocking collectives  45.4 us (38%)
  Pallas kernels  24.9 us (21%)
  waiting for transfers between devices  20.3 us (17%)
  starting transfers between devices  20 us (17%)
  local copies, waits for them, and re-layouts  4.7 us (4%)
    pallas_call x10, Pallas kernels, call(): pl.pallas_call(kernel, out_shape=out, in_specs=specs, out_specs=jax.tree....  24.9 us
    all_to_all x1, blocking collectives, per_device(): spread = lax.all_to_all(pooled, 'dev', 0, 0, tiled=True)  23.7 us
    all_to_all x1, blocking collectives, per_device(): lax.all_to_all(lifted.reshape(16, 128, 128), 'dev', 0, 0, tiled=True)  21.7 us
    ppermute x6, waiting for transfers between devices, exchanged(): return (lax.ppermute(first, BOTH, inner), lax.ppermute(second, BOTH, outer))  20.3 us
    ppermute x6, starting transfers between devices, exchanged(): return (lax.ppermute(first, BOTH, inner), lax.ppermute(second, BOTH, outer))  15.3 us
    ppermute x1, starting transfers between devices, per_device(): edge = lax.ppermute(cubes, BOTH, edges)  4.72 us
    unnamed x30, local copies, waits for them, and re-layouts  4.61 us
  transfers between devices with their start and end apart: 7, of which 3 were waited for; matrix products, arithmetic and copies ran while one was open for 0% of the time, Pallas kernels for 3%

profile of v2, /device:TPU:97, one launch (start us, length us, event | category | flops | bytes accessed | tf_op | source)
XLA Modules:
  0.0 115.6 jit_solution(17632287361604428331)
XLA Ops:
  0.0 1.0 copy-done.2
  1.0 0.5 shard_map.136
  1.5 1.3 %collective-permute-start = (f32[2,160,128]{2,1,0:T(8,128)S(1)}, f32[2,160,128]{2,1,0:T(8,128)S(1)}, u32[]{:S(2)}, u32[]{:S(2)}) collective-permute-start(f32[2,160,128]{2,1,0:T(8,128)S(1)} %get-tuple-element.30), channel_id=1, source_target_pairs={{0,1},{1,0},{2,3},{3,2},{4,5},{5,4},{6,7},{7,6},{8,9},{9,8},{10,11... | collective-permute-start | bytes 491528 | tf_op jit(solution)/shard_map/ppermute | solution.py:460
  2.8 7.0 %collective-permute-start.1 = (f32[2,160,128]{2,1,0:T(8,128)S(1)}, f32[2,160,128]{2,1,0:T(8,128)S(1)}, u32[]{:S(2)}, u32[]{:S(2)}) collective-permute-start(f32[2,160,128]{2,1,0:T(8,128)S(1)} %get-tuple-element.31), channel_id=1, source_target_pairs={{1,2},{3,4},{5,6},{7,8},{9,10},{11,12},{13,14},{15,16},{17,18},{19... | collective-permute-start | bytes 491528 | tf_op jit(solution)/shard_map/ppermute | solution.py:460
  9.8 0.0 copy-start.4
  9.8 1.0 copy-done.4
  10.9 0.3 shard_map.137.weight_ref
  11.2 3.4 %collective-permute-done.1.second_ref = f32[2,160,128]{2,1,0:T(8,128)S(1)} collective-permute-done((f32[2,160,128]{2,1,0:T(8,128)S(1)}, f32[2,160,128]{2,1,0:T(8,128)S(1)}, u32[]{:S(2)}, u32[]{:S(2)}) %collective-permute-start.1) | collective-permute-done | bytes 163872 | tf_op jit(solution)/shard_map/ppermute | solution.py:460
  14.6 3.5 %shard_map.138 = (f32[4,256,128]{2,1,0:T(8,128)S(1)}, f32[16,136,128]{2,1,0:T(8,128)S(1)}) custom-call(s32[4]{0:T(128)S(1)} %copy-done.9, s32[4,26]{1,0:T(4,128)S(1)} %copy-done.7, f32[4,256,128]{2,1,0:T(8,128)S(1)} %get-tuple-element.29.own_ref, f32[2,160,128]{2,1,0:T(8,128)S(1)} %collective-permute-done.first_ref, ...), custom_call_target="tpu_custom_call" | custom-call | flops 1811939328 | bytes 2097152 | tf_op jit(solution)/shard_map/pallas_call | solution.py:468
  18.1 0.0 copy-start.6
  18.2 23.7 %all_to_all.10.all_ref = f32[16,136,128]{2,1,0:T(8,128)S(1)} all-to-all(f32[16,136,128]{2,1,0:T(8,128)S(1)} %get-tuple-element.34), channel_id=1, replica_groups=mesh['grp'=16,'dev'=16] {'dev'}, dimensions={0} | all-to-all | bytes 2228224 | tf_op jit(solution)/shard_map/all_to_all | solution.py:525
  41.8 1.7 %shard_map.139 = (f32[2,256,128]{2,1,0:T(8,128)}, s32[256]{0:T(256)S(1)}, s32[64]{0:T(128)S(1)}) custom-call(f32[16,136,128]{2,1,0:T(8,128)S(1)} %all_to_all.10.all_ref), custom_call_target="tpu_custom_call" | custom-call | flops 1048576 | bytes 2097152 | tf_op jit(solution)/shard_map/pallas_call | solution.py:468
  43.5 4.7 %collective-permute-start.2 = (f32[2,256,128]{2,1,0:T(8,128)}, f32[2,256,128]{2,1,0:T(8,128)}, u32[]{:S(2)}, u32[]{:S(2)}) collective-permute-start(f32[2,256,128]{2,1,0:T(8,128)} %get-tuple-element.43), channel_id=1, source_target_pairs={{0,16},{16,32},{32,48},{48,64},{64,80},{80,96},{96,112},{112,128},... | collective-permute-start | bytes 786440 | tf_op jit(solution)/shard_map/ppermute | solution.py:537
  48.2 0.1 copy.15.down_ref
  48.4 1.5 %copy-done.1 = f32[128,3456]{1,0:T(8,128)S(1)} copy-done((f32[128,3456]{1,0:T(8,128)S(1)}, f32[128,3456]{1,0:T(8,128)}, u32[]{:S(2)}) %copy-start.1) | copy-done | bytes 1769496
  49.8 1.0 copy-done.5
  50.8 1.3 %shard_map.140 = (bf16[3456,256]{1,0:T(8,128)(2,1)S(1)}, bf16[3456,256]{1,0:T(8,128)(2,1)S(1)}, bf16[128,512]{1,0:T(8,128)(2,1)S(1)}, bf16[256,256]{1,0:T(8,128)(2,1)S(1)}, bf16[2304,256]{1,0:T(8,128)(2,1)S(1)}) custom-call(f32[128,3456]{1,0:T(8,128)S(1)} %copy-done, f32[128,3456]{1,0:T(8,128)S(1)} %copy-done.1, f32[128,64]{1,0:T(8,128)S(1)} %copy.15.down_ref, ...), custom_call_target="tpu_custom_call" | custom-call | flops 1073741824 | bytes 2097152 | tf_op jit(solution)/shard_map/pallas_call | solution.py:468
  52.1 0.0 copy-start.8
  52.1 0.0 copy-start.11
  52.1 1.4 %shard_map.141.based_ref = f32[6,512,128]{2,1,0:T(8,128)S(1)} custom-call(f32[16,136,128]{2,1,0:T(8,128)S(1)} %all_to_all.10.all_ref, s32[256]{0:T(256)S(1)} %get-tuple-element.36.place_ref, bf16[128,512]{1,0:T(8,128)(2,1)S(1)} %get-tuple-element.42.down_ref), custom_call_target="tpu_custom_call" | custom-call | flops 268435456 | bytes 2097152 | tf_op jit(solution)/shard_map/pallas_call | solution.py:468
  53.6 0.0 copy-start.12
  53.6 5.4 %shard_map.142 = (f32[2,512,128]{2,1,0:T(8,128)S(1)}, f32[2,320,128]{2,1,0:T(8,128)S(1)}) custom-call(s32[2,26]{1,0:T(2,128)S(1)} %copy-done.8, f32[6,512,128]{2,1,0:T(8,128)S(1)} %shard_map.141.based_ref, f32[2,256,128]{2,1,0:T(8,128)} %collective-permute-done.2.edge_ref, bf16[128,512]{1,0:T(8,128)(2,1)S(1)} %get-tuple-element.42.down_ref, ...), custom_call_target="tpu_custom_call" | custom-call | flops 2717908992 | bytes 2097152 | tf_op jit(solution)/shard_map/pallas_call | solution.py:468
  59.0 1.9 %collective-permute-start.4 = (f32[2,320,128]{2,1,0:T(8,128)S(1)}, f32[2,320,128]{2,1,0:T(8,128)S(1)}, u32[]{:S(2)}, u32[]{:S(2)}) collective-permute-start(f32[2,320,128]{2,1,0:T(8,128)S(1)} %get-tuple-element.46), channel_id=1, source_target_pairs={{1,2},{3,4},{5,6},{7,8},{9,10},{11,12},{13,14},{15,16},{17,18},{19... | collective-permute-start | bytes 983048 | tf_op jit(solution)/shard_map/ppermute | solution.py:460
  60.9 0.3 collective-permute-start.3
  61.2 11.4 %collective-permute-done.4.second_ref = f32[2,320,128]{2,1,0:T(8,128)S(1)} collective-permute-done((f32[2,320,128]{2,1,0:T(8,128)S(1)}, f32[2,320,128]{2,1,0:T(8,128)S(1)}, u32[]{:S(2)}, u32[]{:S(2)}) %collective-permute-start.4) | collective-permute-done | bytes 327712 | tf_op jit(solution)/shard_map/ppermute | solution.py:460
  72.7 6.0 %shard_map.143 = f32[64,32,128]{2,1,0:T(8,128)S(1)} custom-call(s32[2,26]{1,0:T(2,128)S(1)} %copy-done.8, s32[64]{0:T(128)S(1)} %get-tuple-element.35.codes_ref, f32[2,512,128]{2,1,0:T(8,128)S(1)} %get-tuple-element.45.own_ref, f32[2,320,128]{2,1,0:T(8,128)S(1)} %collective-permute-done.3.first_ref, f32[2,320,128]{2,1,0:T(8,128)S(1)} %collective-permute-done.4.second_ref, ...), custom_call_target="tpu_custom_call" | custom-call | flops 2717908992 | bytes 2097152 | tf_op jit(solution)/shard_map/pallas_call | solution.py:468
  78.8 21.7 %all_to_all.11.risen_ref = f32[16,128,128]{2,1,0:T(8,128)S(1)} all-to-all(f32[16,128,128]{2,1,0:T(8,128)S(1)} %bitcast.5), channel_id=1, replica_groups=mesh['grp'=16,'dev'=16] {'dev'}, dimensions={0} | all-to-all | bytes 2097152 | tf_op jit(solution)/shard_map/all_to_all | solution.py:566
  100.5 0.4 shard_map.144
  100.8 0.4 collective-permute-start.5
  101.2 4.5 %collective-permute-start.6 = (f32[2,160,128]{2,1,0:T(8,128)S(1)}, f32[2,160,128]{2,1,0:T(8,128)S(1)}, u32[]{:S(2)}, u32[]{:S(2)}) collective-permute-start(f32[2,160,128]{2,1,0:T(8,128)S(1)} %get-tuple-element.51), channel_id=1, source_target_pairs={{1,2},{3,4},{5,6},{7,8},{9,10},{11,12},{13,14},{15,16},{17,18},{19... | collective-permute-start | bytes 491528 | tf_op jit(solution)/shard_map/ppermute | solution.py:460
  105.7 5.5 %collective-permute-done.6.second_ref = f32[2,160,128]{2,1,0:T(8,128)S(1)} collective-permute-done((f32[2,160,128]{2,1,0:T(8,128)S(1)}, f32[2,160,128]{2,1,0:T(8,128)S(1)}, u32[]{:S(2)}, u32[]{:S(2)}) %collective-permute-start.6) | collective-permute-done | bytes 163872 | tf_op jit(solution)/shard_map/ppermute | solution.py:460
  111.2 4.4 %shard_map.145 = f32[4,64,512]{2,1,0:T(8,128)} custom-call(s32[4,26]{1,0:T(4,128)S(1)} %copy-done.7, f32[4,256,128]{2,1,0:T(8,128)S(1)} %get-tuple-element.49.own_ref, f32[2,160,128]{2,1,0:T(8,128)S(1)} %collective-permute-done.5.first_ref, f32[2,160,128]{2,1,0:T(8,128)S(1)} %collective-permute-done.6.second_ref, f32[4,64,512]{2,1,0:T(8,128)S(1)} %copy-done.3, ...), custom_call_target="tpu_custom_call" | custom-call | flops 1811939328 | bytes 2097152 | tf_op jit(solution)/shard_map/pallas_call | solution.py:468
  (25 shorter events, 0.1 us)
Async XLA Ops:
  0.0 1.0 copy-start.2
  1.0 13.5 %copy-start.7 = (s32[4,26]{1,0:T(4,128)S(1)}, s32[4,26]{1,0:T(4,128)}, u32[]{:S(2)}) copy-start(s32[4,26]{1,0:T(4,128)} %links_ref.7) | copy-start | bytes 1252
  1.0 13.5 %copy-start.9 = (s32[4]{0:T(128)S(1)}, s32[4]{0:T(128)}, u32[]{:S(2)}) copy-start(s32[4]{0:T(128)} %codes_ref.1) | copy-start | bytes 52
  1.0 13.5 %copy-start.10 = (f32[64]{0:T(128)S(1)}, f32[64]{0:T(128)}, u32[]{:S(2)}) copy-start(f32[64]{0:T(128)} %param.19) | copy-start | bytes 772
  1.5 9.6 %collective-permute-start = (f32[2,160,128]{2,1,0:T(8,128)S(1)}, f32[2,160,128]{2,1,0:T(8,128)S(1)}, u32[]{:S(2)}, u32[]{:S(2)}) collective-permute-start(f32[2,160,128]{2,1,0:T(8,128)S(1)} %get-tuple-element.30), channel_id=1, source_target_pairs={{0,1},{1,0},{2,3},{3,2},{4,5},{5,4},{6,7},{7,6},{8,9},{9,8},{10,11... | collective-permute-start | bytes 491528 | tf_op jit(solution)/shard_map/ppermute | solution.py:460
  2.8 11.8 %collective-permute-start.1 = (f32[2,160,128]{2,1,0:T(8,128)S(1)}, f32[2,160,128]{2,1,0:T(8,128)S(1)}, u32[]{:S(2)}, u32[]{:S(2)}) collective-permute-start(f32[2,160,128]{2,1,0:T(8,128)S(1)} %get-tuple-element.31), channel_id=1, source_target_pairs={{1,2},{3,4},{5,6},{7,8},{9,10},{11,12},{13,14},{15,16},{17,18},{19... | collective-permute-start | bytes 491528 | tf_op jit(solution)/shard_map/ppermute | solution.py:460
  9.8 1.0 copy-start.4
  18.1 30.1 %copy-start.14 = (f32[128,64]{0,1:T(8,128)S(1)}, f32[128,64]{0,1:T(8,128)}, u32[]{:S(2)}) copy-start(f32[128,64]{0,1:T(8,128)} %param.20) | copy-start | bytes 98308
  18.1 30.2 %copy-start = (f32[128,3456]{1,0:T(8,128)S(1)}, f32[128,3456]{1,0:T(8,128)}, u32[]{:S(2)}) copy-start(f32[128,3456]{1,0:T(8,128)} %first_ref) | copy-start | bytes 5308420
  18.1 30.2 %copy-start.6 = (f32[64,128]{1,0:T(8,128)S(1)}, f32[64,128]{1,0:T(8,128)}, u32[]{:S(2)}) copy-start(f32[64,128]{1,0:T(8,128)} %up_ref) | copy-start | bytes 98308
  43.5 10.1 %collective-permute-start.2 = (f32[2,256,128]{2,1,0:T(8,128)}, f32[2,256,128]{2,1,0:T(8,128)}, u32[]{:S(2)}, u32[]{:S(2)}) collective-permute-start(f32[2,256,128]{2,1,0:T(8,128)} %get-tuple-element.43), channel_id=1, source_target_pairs={{0,16},{16,32},{32,48},{48,64},{64,80},{80,96},{96,112},{112,128},... | collective-permute-start | bytes 786440 | tf_op jit(solution)/shard_map/ppermute | solution.py:537
  48.3 1.5 %copy-start.1 = (f32[128,3456]{1,0:T(8,128)S(1)}, f32[128,3456]{1,0:T(8,128)}, u32[]{:S(2)}) copy-start(f32[128,3456]{1,0:T(8,128)} %second_ref) | copy-start | bytes 5308420
  49.8 1.0 copy-start.5
  52.1 1.5 %copy-start.8 = (s32[2,26]{1,0:T(2,128)S(1)}, s32[2,26]{1,0:T(2,128)}, u32[]{:S(2)}) copy-start(s32[2,26]{1,0:T(2,128)} %links_ref.6) | copy-start | bytes 628
  52.1 1.5 %copy-start.11 = (f32[128]{0:T(128)S(1)}, f32[128]{0:T(128)}, u32[]{:S(2)}) copy-start(f32[128]{0:T(128)} %param.22) | copy-start | bytes 1540
  53.6 19.1 %copy-start.12 = (f32[128]{0:T(128)S(1)}, f32[128]{0:T(128)}, u32[]{:S(2)}) copy-start(f32[128]{0:T(128)} %param.24) | copy-start | bytes 1540
  59.0 13.7 %collective-permute-start.4 = (f32[2,320,128]{2,1,0:T(8,128)S(1)}, f32[2,320,128]{2,1,0:T(8,128)S(1)}, u32[]{:S(2)}, u32[]{:S(2)}) collective-permute-start(f32[2,320,128]{2,1,0:T(8,128)S(1)} %get-tuple-element.46), channel_id=1, source_target_pairs={{1,2},{3,4},{5,6},{7,8},{9,10},{11,12},{13,14},{15,16},{17,18},{19... | collective-permute-start | bytes 983048 | tf_op jit(solution)/shard_map/ppermute | solution.py:460
  60.9 11.7 %collective-permute-start.3 = (f32[2,320,128]{2,1,0:T(8,128)S(1)}, f32[2,320,128]{2,1,0:T(8,128)S(1)}, u32[]{:S(2)}, u32[]{:S(2)}) collective-permute-start(f32[2,320,128]{2,1,0:T(8,128)S(1)} %get-tuple-element.46), channel_id=1, source_target_pairs={{0,1},{1,0},{2,3},{3,2},{4,5},{5,4},{6,7},{7,6},{8,9},{9,8},{10,11... | collective-permute-start | bytes 983048 | tf_op jit(solution)/shard_map/ppermute | solution.py:460
  78.7 32.4 %copy-start.3 = (f32[4,64,512]{2,1,0:T(8,128)S(1)}, f32[4,64,512]{2,1,0:T(8,128)}, u32[]{:S(2)}) copy-start(f32[4,64,512]{2,1,0:T(8,128)} %features_ref.3) | copy-start | bytes 1572868
  78.7 32.4 %copy-start.13 = (f32[64]{0:T(128)S(1)}, f32[64]{0:T(128)}, u32[]{:S(2)}) copy-start(f32[64]{0:T(128)} %param.27) | copy-start | bytes 772
  100.8 4.8 %collective-permute-start.5 = (f32[2,160,128]{2,1,0:T(8,128)S(1)}, f32[2,160,128]{2,1,0:T(8,128)S(1)}, u32[]{:S(2)}, u32[]{:S(2)}) collective-permute-start(f32[2,160,128]{2,1,0:T(8,128)S(1)} %get-tuple-element.50), channel_id=1, source_target_pairs={{0,1},{1,0},{2,3},{3,2},{4,5},{5,4},{6,7},{7,6},{8,9},{9,8},{10,11... | collective-permute-start | bytes 491528 | tf_op jit(solution)/shard_map/ppermute | solution.py:460
  101.2 9.9 %collective-permute-start.6 = (f32[2,160,128]{2,1,0:T(8,128)S(1)}, f32[2,160,128]{2,1,0:T(8,128)S(1)}, u32[]{:S(2)}, u32[]{:S(2)}) collective-permute-start(f32[2,160,128]{2,1,0:T(8,128)S(1)} %get-tuple-element.51), channel_id=1, source_target_pairs={{1,2},{3,4},{5,6},{7,8},{9,10},{11,12},{13,14},{15,16},{17,18},{19... | collective-permute-start | bytes 491528 | tf_op jit(solution)/shard_map/ppermute | solution.py:460

commit v3 on v2

--- a/solution.py
+++ b/solution.py
@@ -44,8 +44,8 @@
 def neighbours(links_ref, row, start, none):
     found = {}
     for offset, k in COLUMN.items():
-        link = links_ref[row, k]
-        found[offset] = jnp.where(link < 0, none, link - start)
+        link = links_ref[row, k].astype(jnp.int32)
+        found[offset] = jnp.where(link < 0, none, jnp.clip(link - start, 0, none))
     return found
 
 
@@ -58,44 +58,44 @@
     return device_number() % 2 == 0
 
 
-def fine_pack(brick_ref, n, out_ref, m, middle):
-    first, last = brick_ref[n, 0:64], brick_ref[n, 192:256]
+def fine_pack(brick_ref, out_ref, middle):
+    first, last = brick_ref[0:64], brick_ref[192:256]
     lower = low_lanes(first.shape)
-    out_ref[m, 0:64] = jnp.where(lower, last, first)
+    out_ref[0:64] = jnp.where(lower, last, first)
     middle[0:64] = jnp.where(lower, first, last)
-    middle[64:192] = brick_ref[n, 64:192]
+    middle[64:192] = brick_ref[64:192]
     for k in range(3):
-        out_ref[m, 64 + 8 * k : 72 + 8 * k] = middle[64 * k : 64 * k + 8]
-        out_ref[m, 88 + 8 * k : 96 + 8 * k] = middle[64 * k + 56 : 64 * k + 64]
-    out_ref[m, 112:136] = middle[pl.ds(0, 24, 8), :]
-    out_ref[m, 136:160] = middle[pl.ds(7, 24, 8), :]
-
-
-def fine_unpack(packed_ref, m, source, n, middle):
-    middle[pl.ds(0, 24, 8), :] = packed_ref[m, 112:136]
-    middle[pl.ds(7, 24, 8), :] = packed_ref[m, 136:160]
+        out_ref[64 + 8 * k : 72 + 8 * k] = middle[64 * k : 64 * k + 8]
+        out_ref[88 + 8 * k : 96 + 8 * k] = middle[64 * k + 56 : 64 * k + 64]
+    out_ref[112:136] = middle[pl.ds(0, 24, 8), :]
+    out_ref[136:160] = middle[pl.ds(7, 24, 8), :]
+
+
+def fine_unpack(packed_ref, brick_ref, middle):
+    middle[pl.ds(0, 24, 8), :] = packed_ref[112:136]
+    middle[pl.ds(7, 24, 8), :] = packed_ref[136:160]
     for k in range(3):
-        middle[64 * k : 64 * k + 8] = packed_ref[m, 64 + 8 * k : 72 + 8 * k]
-        middle[64 * k + 56 : 64 * k + 64] = packed_ref[m, 88 + 8 * k : 96 + 8 * k]
-    ends, inner = packed_ref[m, 0:64], middle[0:64]
+        middle[64 * k : 64 * k + 8] = packed_ref[64 + 8 * k : 72 + 8 * k]
+        middle[64 * k + 56 : 64 * k + 64] = packed_ref[88 + 8 * k : 96 + 8 * k]
+    ends, inner = packed_ref[0:64], middle[0:64]
     lower = low_lanes(ends.shape)
-    source[n, 0:64] = jnp.where(lower, inner, ends)
-    source[n, 64:192] = middle[64:192]
-    source[n, 192:256] = jnp.where(lower, ends, inner)
+    brick_ref[0:64] = jnp.where(lower, inner, ends)
+    brick_ref[64:192] = middle[64:192]
+    brick_ref[192:256] = jnp.where(lower, ends, inner)
 
 
 def fine_halo(first_ref, second_ref, source, middle):
     even = even_device()
     for packed_ref, at in ((first_ref, jnp.where(even, 6, 0)), (second_ref, jnp.where(even, 0, 6))):
         for m in range(2):
-            fine_unpack(packed_ref, m, source, at + m, middle)
+            fine_unpack(packed_ref.at[m], source.at[at + m], middle)
 
 
 def fine_sends(brick_ref, first_ref, second_ref, middle):
     even = even_device()
     for out_ref, at in ((first_ref, jnp.where(even, 2, 0)), (second_ref, jnp.where(even, 0, 2))):
         for m in range(2):
-            fine_pack(brick_ref, at + m, out_ref, m, middle)
+            fine_pack(brick_ref.at[at + m], out_ref.at[m], middle)
 
 
 def shifted_rows(tile):
@@ -219,7 +219,7 @@
 
 
 def fine_in_kernel(
-    codes_ref, links_ref, own_ref, first_ref, second_ref, weight_ref, bias_ref,
+    codes_ref, links_ref, coarse_links_ref, own_ref, first_ref, second_ref, weight_ref, bias_ref,
     hidden_ref, pooled_ref, source, high, low, sums, middle,
 ):
     source[8] = jnp.zeros((256, 128), F32)
@@ -237,7 +237,7 @@
         r = r[:, 0] + r[:, 1]
         held.append(r + swap(r))
         if zz % 2 == 1:
-            both = jnp.where(low_lanes(r.shape), held[zz - 1], held[zz])
+            both = jnp.where(low_lanes(r.shape), held[zz], held[zz - 1])
             sums[64 * zz - 64 : 64 * zz + 64, :] = both.reshape(128, 128)
     means = (sums[pl.ds(0, 128, 2), :] + sums[pl.ds(1, 128, 2), :]) * 0.125
     for n in range(8):
@@ -249,6 +249,7 @@
     for b in range(4):
         named = jnp.where(lane == b, codes_ref[b].astype(F32), named)
     pooled_ref[0, 128:136, :] = named
+    pooled_ref[0, 129:131, 0:26] = coarse_links_ref[...].astype(F32)
     for k in range(1, 16):
         pooled_ref[k] = pooled_ref[0]
 
@@ -261,10 +262,10 @@
         v = all_ref[at // 4, pl.ds(pl.multiple_of(at % 4 * 32, 32), 32), :]
         v = jnp.where(i >= 0, v, 0.0)
         for r in range(8):
-            store(t // 8, ((2 * a + c) * 8 + r) * 8 + 4 * b, v[4 * r : 4 * r + 4])
-
-
-def edge_kernel(all_ref, cubes_ref, place_ref, codes_ref, held, spelled, sem):
+            store(t // 8, (2 * c + r // 4) * 64 + (4 * a + r % 4) * 8 + 4 * b, v[4 * r : 4 * r + 4])
+
+
+def edge_kernel(all_ref, cubes_ref, place_ref, codes_ref, held, spelled, cubes, middle, sem):
     held[...] = all_ref[:, 128, :]
     copy = pltpu.make_async_copy(held, spelled, sem)
     copy.start()
@@ -276,29 +277,37 @@
         code = spelled[i // 4, i % 4].astype(jnp.int32)
         codes_ref[i] = code
         place_ref[code] = i
-
-    @pl.when((me == 0) | (me == 15))
+    cubes_ref[832:840] = all_ref[jnp.where(me < 8, 15, 0), 128:136, :]
+
+    @pl.when((me < 2) | (me > 13))
     def _():
         def store(s, at, v):
-            cubes_ref[s, at : at + 4, :] = v
-
-        cube_rows(all_ref, place_ref, jnp.where(me == 0, 15 * 16, 0), store)
+            cubes_ref[256 * s + at : 256 * s + at + 4, :] = v
+
+        cube_rows(all_ref, place_ref, jnp.where(me < 2, 15, 0) * 16, store)
+
+        def hold(s, at, v):
+            cubes[s, at : at + 4, :] = v
+
+        cube_rows(all_ref, place_ref, jnp.where(me < 2, 14, 1) * 16, hold)
+        for s in range(2):
+            fine_pack(cubes.at[s], cubes_ref.at[512 + 160 * s : 672 + 160 * s], middle)
 
 
 def bring_down(cubes, down_ref, source, n):
     h, l = split(cubes)
-    based = product(h, l, down_ref).reshape(2, 2, 2, 32, 256)
-    for a in range(2):
-        for z in range(8):
-            source[n, 64 * z + 32 * a : 64 * z + 32 * a + 32] = based[
-                a, z // 4, z // 2 % 2, :, 128 * (z % 2) : 128 * (z % 2) + 128
-            ]
-
-
-def base_kernel(all_ref, place_ref, down_ref, out_ref, cubes):
+    based = product(h, l, down_ref)
+    for z in range(8):
+        k = 1 - z % 2
+        source[n, 64 * z : 64 * z + 64] = based[64 * (z // 2) : 64 * (z // 2) + 64, 128 * k : 128 * k + 128]
+
+
+def base_kernel(all_ref, place_ref, down_ref, out_ref, links_ref, cubes):
     me = lax.axis_index("dev")
-    for n in range(3):
-        owner = jnp.clip(me + (n - 1), 0, 15)
+    links_ref[...] = jnp.zeros((8, 128), F32)
+    out_ref[10] = jnp.zeros((512, 128), F32)
+    for n in range(5):
+        owner = jnp.clip(me + (n - 2), 0, 15)
 
         def store(s, at, v):
             cubes[s, at : at + 4, :] = v
@@ -306,14 +315,15 @@
         cube_rows(all_ref, place_ref, owner * 16, store)
         for s in range(2):
             bring_down(cubes[s], down_ref, out_ref, 2 * n + s)
-
-
-def coarse_rim(source, links_ref, high, low):
-    start = device_number() * 2 - 2
+        if 1 <= n <= 3:
+            links_ref[2 * n - 2 : 2 * n] = all_ref[owner, 129:131, :]
+
+
+def coarse_rim(source, links_ref, row, home, start, none, high, low):
     found = []
     for s in range(2):
-        near = neighbours(links_ref, s, start, 6)
-        near[0, 0, 0] = s + 2
+        near = neighbours(links_ref, row + s, start, none)
+        near[0, 0, 0] = home + s
         found.append(near)
     for z in range(10):
         dz = -1 if z == 0 else 1 if z == 9 else 0
@@ -341,52 +351,65 @@
     )
 
 
-def coarse_first_kernel(
-    links_ref, based_ref, edge_ref, down_ref, weight_ref, bias_ref, first_ref, packed_ref, source, high, low
-):
-    source[6] = jnp.zeros((512, 128), F32)
-    source[0:6] = based_ref[...]
-    me = lax.axis_index("dev")
-
-    @pl.when((me == 0) | (me == 15))
-    def _():
-        at = jnp.where(me == 0, 0, 4)
-        for s in range(2):
-            bring_down(edge_ref[s], down_ref, source, at + s)
-
-    coarse_rim(source, links_ref, high, low)
+def coarse_first_pair(source, links_ref, pair, weight_ref, bias_ref, out_ref, n, high, low):
+    coarse_rim(source, links_ref, 2 * pair, 2 * pair + 2, device_number() * 2 - 4, 10, high, low)
     for z in range(0, 8, 2):
         r = product(coarse_columns(high, z), coarse_columns(low, z), weight_ref) + bias_ref[...]
         r = silu(r).reshape(2, 8, 16, 128)
         for s in range(2):
-            first_ref[s, 64 * z : 64 * z + 128] = r[:, :, 8 * s : 8 * s + 8].reshape(128, 128)
+            out_ref[n + s, 64 * z : 64 * z + 128] = r[:, :, 8 * s : 8 * s + 8].reshape(128, 128)
+
+
+def inner_pair():
+    return jnp.where(lax.axis_index("dev") < 8, 2, 0)
+
+
+def inner_kernel(links_ref, based_ref, weight_ref, bias_ref, out_ref, high, low):
+    coarse_first_pair(based_ref, links_ref, inner_pair(), weight_ref, bias_ref, out_ref, 0, high, low)
+
+
+def coarse_kernel(
+    links_ref, near_links_ref, codes_ref, based_ref, edge_ref, inner_ref, down_ref, first_weight_ref, first_bias_ref,
+    weight_ref, bias_ref, up_ref, out_ref, source, high, low, seconds, high2, low2, octants, held, spelled,
+    cubes, middle, sem,
+):
+    me = lax.axis_index("dev")
+    held[...] = near_links_ref[...]
+
+    @pl.when(me == 0)
+    def _():
+        held[0:2] = edge_ref[833:835]
+
+    @pl.when(me == 15)
+    def _():
+        held[4:6] = edge_ref[833:835]
+
+    copy = pltpu.make_async_copy(held, spelled, sem)
+    copy.start()
+    source[...] = based_ref[...]
+
+    @pl.when((me < 2) | (me > 13))
+    def _():
+        at = jnp.where(me < 2, jnp.where(me == 0, 2, 0), jnp.where(me == 15, 6, 8))
+        for s in range(2):
+            bring_down(edge_ref[256 * s : 256 * s + 256], down_ref, source, at + s)
+
+    @pl.when((me == 0) | (me == 15))
+    def _():
+        at = jnp.where(me == 0, 0, 8)
+        for s in range(2):
+            fine_unpack(edge_ref.at[512 + 160 * s : 672 + 160 * s], cubes, middle)
+            bring_down(cubes[...], down_ref, source, at + s)
+
+    seconds[6] = jnp.zeros((512, 128), F32)
+    inner = inner_pair()
     for s in range(2):
-        packed_ref[s, 0:64] = first_ref[s, 0:64]
-        packed_ref[s, 64:128] = first_ref[s, 448:512]
-        for z in range(1, 7):
-            packed_ref[s, 120 + 8 * z : 128 + 8 * z] = first_ref[s, 64 * z : 64 * z + 8]
-            packed_ref[s, 168 + 8 * z : 176 + 8 * z] = first_ref[s, 64 * z + 56 : 64 * z + 64]
-        packed_ref[s, 224:272] = first_ref[s, pl.ds(64, 48, 8), :]
-        packed_ref[s, 272:320] = first_ref[s, pl.ds(71, 48, 8), :]
-
-
-def coarse_second_kernel(
-    links_ref, codes_ref, own_ref, first_ref, second_ref, weight_ref, bias_ref, up_ref,
-    out_ref, source, high, low, octants,
-):
-    source[6] = jnp.zeros((512, 128), F32)
-    source[2:4] = own_ref[...]
-    even = even_device()
-    for packed_ref, n in ((first_ref, jnp.where(even, 4, 0)), (second_ref, jnp.where(even, 0, 4))):
-        for s in range(2):
-            source[n + s, pl.ds(64, 48, 8), :] = packed_ref[s, 224:272]
-            source[n + s, pl.ds(71, 48, 8), :] = packed_ref[s, 272:320]
-            source[n + s, 0:64] = packed_ref[s, 0:64]
-            source[n + s, 448:512] = packed_ref[s, 64:128]
-            for z in range(1, 7):
-                source[n + s, 64 * z : 64 * z + 8] = packed_ref[s, 120 + 8 * z : 128 + 8 * z]
-                source[n + s, 64 * z + 56 : 64 * z + 64] = packed_ref[s, 168 + 8 * z : 176 + 8 * z]
-    coarse_rim(source, links_ref, high, low)
+        seconds[2 * inner + s] = inner_ref[s]
+    copy.wait()
+    outer = 2 - inner
+    coarse_first_pair(source, spelled, outer, first_weight_ref, first_bias_ref, seconds, 2 * outer, high, low)
+    coarse_first_pair(source, spelled, 1, first_weight_ref, first_bias_ref, seconds, 2, high2, low2)
+    coarse_rim(seconds, links_ref, 0, 2, device_number() * 2 - 2, 6, high, low)
     for z in range(0, 8, 2):
         c, q = z // 4, z // 2 % 2
         r = product(coarse_columns(high, z), coarse_columns(low, z), weight_ref) + bias_ref[...]
@@ -457,7 +480,8 @@
     inner = [(i, i ^ 1) for i in range(count)]
     outer = [(i, i + 1) for i in range(1, count - 1, 2)]
     outer += [(b, a) for a, b in outer]
-    return lax.ppermute(first, BOTH, inner), lax.ppermute(second, BOTH, outer)
+    second = lax.ppermute(second, BOTH, outer)
+    return lax.ppermute(first, BOTH, inner), second
 
 
 def struct(*shape, dtype=F32):
@@ -482,9 +506,7 @@
     up_weight, fine_out_weight, fine_out_bias,
 ):
     fine_padded = [pltpu.VMEM((3, 5, 10, 32, 128), BF16)] * 2
-    coarse_padded = [pltpu.VMEM((3, 10, 10, 16, 128), BF16)] * 2
     fine_source = pltpu.VMEM((9, 256, 128), F32)
-    coarse_source = pltpu.VMEM((7, 512, 128), F32)
     middle = pltpu.VMEM((192, 128), F32)
     brick, shell = struct(4, 256, 128), struct(2, 160, 128)
 
@@ -500,16 +522,7 @@
     weight_in = call(
         first_weight_kernel, struct(2304, 256, dtype=BF16), [], [VMEM], (fine_in_weight,), 1 << 20
     )
-    hidden, pooled = call(
-        fine_in_kernel,
-        (brick, struct(16, 136, 128)),
-        [fine_source, *fine_padded, pltpu.VMEM((256, 128), F32), middle],
-        [SMEM, SMEM] + [VMEM] * 5,
-        (codes, fine_links, own, first, second, weight_in, fine_in_bias[None]),
-        2 * 1024 * 2304 * 384,
-    )
     later = (coarse_first_weight, coarse_second_weight, down_weight, up_weight, fine_out_weight)
-    pooled, *later = lax.optimization_barrier((pooled, *later))
     weight_first, weight_second, down, up, weight_out = call(
         later_weights_kernel,
         (
@@ -522,46 +535,64 @@
         later,
         1 << 30,
     )
+    weight_in, weight_first, weight_second, down, up, weight_out = lax.optimization_barrier(
+        (weight_in, weight_first, weight_second, down, up, weight_out)
+    )
+    hidden, pooled = call(
+        fine_in_kernel,
+        (brick, struct(16, 136, 128)),
+        [fine_source, *fine_padded, pltpu.VMEM((256, 128), F32), middle],
+        [SMEM, SMEM] + [VMEM] * 6,
+        (codes, fine_links, coarse_links, own, first, second, weight_in, fine_in_bias[None]),
+        2 * 1024 * 2304 * 384,
+    )
     spread = lax.all_to_all(pooled, "dev", 0, 0, tiled=True)
     cubes, place, group_codes = call(
         edge_kernel,
-        (struct(2, 256, 128), struct(256, dtype=jnp.int32), struct(64, dtype=jnp.int32)),
-        [pltpu.VMEM((16, 128), F32), pltpu.SMEM((16, 128), F32), pltpu.SemaphoreType.DMA],
+        (struct(840, 128), struct(256, dtype=jnp.int32), struct(64, dtype=jnp.int32)),
+        [
+            pltpu.VMEM((16, 128), F32), pltpu.SMEM((16, 128), F32), pltpu.VMEM((2, 256, 128), F32),
+            middle, pltpu.SemaphoreType.DMA,
+        ],
         [VMEM],
         (spread,),
         1 << 20,
     )
     groups, devices = lax.axis_size("grp"), lax.axis_size("dev")
-    edges = [(g * devices, (g + 1) * devices) for g in range(groups - 1)]
-    edges += [((g + 2) * devices - 1, (g + 1) * devices - 1) for g in range(groups - 1)]
+    edges = [(g * devices + k, (g + 1) * devices + k) for g in range(groups - 1) for k in (0, 1)]
+    edges += [((g + 1) * devices + k, g * devices + k) for g in range(groups - 1) for k in (14, 15)]
     edge = lax.ppermute(cubes, BOTH, edges)
-    based = call(
+    based, near_links = call(
         base_kernel,
-        struct(6, 512, 128),
+        (struct(11, 512, 128), struct(8, 128)),
         [pltpu.VMEM((2, 256, 128), F32)],
         [VMEM, SMEM, VMEM],
         (spread, place, down),
         1 << 28,
     )
-    first_own, packed = call(
-        coarse_first_kernel,
-        (struct(2, 512, 128), struct(2, 320, 128)),
-        [coarse_source, *coarse_padded],
-        [SMEM] + [VMEM] * 5,
-        (coarse_links, based, edge, down, weight_first, coarse_first_bias[None]),
+    coarse_padded = [pltpu.VMEM((3, 10, 10, 16, 128), BF16)] * 2
+    inner = call(
+        inner_kernel,
+        struct(2, 512, 128),
+        coarse_padded,
+        [SMEM] + [VMEM] * 3,
+        (near_links, based, weight_first, coarse_first_bias[None]),
         2 * 1024 * 3456 * 384,
     )
-    first, second = exchanged(packed, packed)
     lifted = call(
-        coarse_second_kernel,
+        coarse_kernel,
         struct(64, 32, 128),
-        [coarse_source, *coarse_padded, pltpu.VMEM((16, 32, 128), F32)],
-        [SMEM, SMEM] + [VMEM] * 6,
+        [
+            pltpu.VMEM((11, 512, 128), F32), *coarse_padded, pltpu.VMEM((7, 512, 128), F32), *coarse_padded,
+            pltpu.VMEM((16, 32, 128), F32), pltpu.VMEM((8, 128), F32), pltpu.SMEM((8, 128), F32),
+            pltpu.VMEM((256, 128), F32), middle, pltpu.SemaphoreType.DMA,
+        ],
+        [SMEM, VMEM, SMEM] + [VMEM] * 9,
         (
-            coarse_links, group_codes, first_own, first, second, weight_second,
-            coarse_second_bias[None], up,
+            coarse_links, near_links, group_codes, based, edge, inner, down, weight_first,
+            coarse_first_bias[None], weight_second, coarse_second_bias[None], up,
         ),
-        2 * 1024 * 3456 * 384,
+        6 * 1024 * 3456 * 384,
     )
     risen = lax.all_to_all(lifted.reshape(16, 128, 128), "dev", 0, 0, tiled=True)
     blended, first, second = call(

time: 118 us -> 108 us (0.915); the launches traced: 116 us -> 108 us
  waiting for transfers between devices: 20.3 us -> 8.03 us
  Pallas kernels: 24.9 us -> 33.9 us
  starting transfers between devices: 20 us -> 15.7 us
  blocking collectives: 45.4 us -> 43.6 us
  local copies, waits for them, and re-layouts: 4.7 us -> 6.33 us
    ppermute x6 -> x4, waiting for transfers between devices: 20.3 us -> 8.02 us  [the longest x2 6.54 us: exchanged(): second = lax.ppermute(second, BOTH, outer)]
    pallas_call x10, Pallas kernels: 24.9 us -> 33.9 us  [call(): pl.pallas_call(kernel, out_shape=out, in_specs=specs, out_specs=jax.tree....]
    ppermute x6 -> x4, starting transfers between devices: 15.3 us -> 12.3 us  [the longest x2 10.7 us: exchanged(): second = lax.ppermute(second, BOTH, outer)]
    unnamed x30 -> x29, local copies, waits for them, and re-layouts: 4.61 us -> 6.33 us
    ppermute x1, starting transfers between devices: 4.72 us -> 3.46 us  [per_device(): edge = lax.ppermute(cubes, BOTH, edges)]
  transfers between devices with their start and end apart: 7 -> 5, of which waited for: 3 -> 2; matrix products, arithmetic and copies ran while one was open for 0% -> 1% of each run, Pallas kernels for 3% -> 8%
where the time goes in v3:
time: 108 us
  blocking collectives  43.6 us (40%)
  Pallas kernels  33.9 us (31%)
  starting transfers between devices  15.7 us (15%)
  waiting for transfers between devices  8.03 us (7%)
  local copies, waits for them, and re-layouts  6.33 us (6%)
    pallas_call x10, Pallas kernels, call(): pl.pallas_call(kernel, out_shape=out, in_specs=specs, out_specs=jax.tree....  33.9 us
    all_to_all x1, blocking collectives, per_device(): spread = lax.all_to_all(pooled, 'dev', 0, 0, tiled=True)  22.7 us
    all_to_all x1, blocking collectives, per_device(): lax.all_to_all(lifted.reshape(16, 128, 128), 'dev', 0, 0, tiled=True)  20.9 us
    ppermute x2, starting transfers between devices, exchanged(): second = lax.ppermute(second, BOTH, outer)  10.7 us
    ppermute x2, waiting for transfers between devices, exchanged(): second = lax.ppermute(second, BOTH, outer)  6.54 us
    unnamed x29, local copies, waits for them, and re-layouts  6.33 us
    ppermute x1, starting transfers between devices, per_device(): edge = lax.ppermute(cubes, BOTH, edges)  3.46 us
  transfers between devices with their start and end apart: 5, of which 2 were waited for; matrix products, arithmetic and copies ran while one was open for 1% of the time, Pallas kernels for 8%

profile of v3, /device:TPU:97, one launch (start us, length us, event | category | flops | bytes accessed | tf_op | source)
XLA Modules:
  0.0 107.8 jit_solution(2666552646290440295)
XLA Ops:
  0.0 1.2 %copy-done.2 = f32[4,64,512]{2,1,0:T(8,128)S(1)} copy-done((f32[4,64,512]{2,1,0:T(8,128)S(1)}, f32[4,64,512]{2,1,0:T(8,128)}, u32[]{:S(2)}) %copy-start.2) | copy-done | bytes 524312
  1.2 0.5 shard_map.136
  1.7 1.3 %collective-permute-start = (f32[2,160,128]{2,1,0:T(8,128)S(1)}, f32[2,160,128]{2,1,0:T(8,128)S(1)}, u32[]{:S(2)}, u32[]{:S(2)}) collective-permute-start(f32[2,160,128]{2,1,0:T(8,128)S(1)} %get-tuple-element.30), channel_id=1, source_target_pairs={{0,1},{1,0},{2,3},{3,2},{4,5},{5,4},{6,7},{7,6},{8,9},{9,8},{10,11... | collective-permute-start | bytes 491528 | tf_op jit(solution)/shard_map/ppermute | solution.py:484
  3.0 7.0 %collective-permute-start.1 = (f32[2,160,128]{2,1,0:T(8,128)S(1)}, f32[2,160,128]{2,1,0:T(8,128)S(1)}, u32[]{:S(2)}, u32[]{:S(2)}) collective-permute-start(f32[2,160,128]{2,1,0:T(8,128)S(1)} %get-tuple-element.31), channel_id=1, source_target_pairs={{1,2},{3,4},{5,6},{7,8},{9,10},{11,12},{13,14},{15,16},{17,18},{19... | collective-permute-start | bytes 491528 | tf_op jit(solution)/shard_map/ppermute | solution.py:483
  10.0 0.8 copy.15.down_ref
  10.8 0.0 copy-start.4
  10.8 1.0 copy-done.4
  11.8 0.3 shard_map.137.weight_ref
  12.2 0.0 copy-start.1
  12.2 1.5 %copy-done.1 = f32[128,3456]{1,0:T(8,128)S(1)} copy-done((f32[128,3456]{1,0:T(8,128)S(1)}, f32[128,3456]{1,0:T(8,128)}, u32[]{:S(2)}) %copy-start.1) | copy-done | bytes 1769496
  13.6 1.0 copy-done.5
  14.7 0.8 copy-done.6
  15.4 1.3 %shard_map.138 = (bf16[3456,256]{1,0:T(8,128)(2,1)S(1)}, bf16[3456,256]{1,0:T(8,128)(2,1)S(1)}, bf16[128,512]{1,0:T(8,128)(2,1)S(1)}, bf16[256,256]{1,0:T(8,128)(2,1)S(1)}, bf16[2304,256]{1,0:T(8,128)(2,1)S(1)}) custom-call(f32[128,3456]{1,0:T(8,128)S(1)} %copy-done, f32[128,3456]{1,0:T(8,128)S(1)} %copy-done.1, f32[128,64]{1,0:T(8,128)S(1)} %copy.15.down_ref, ...), custom_call_target="tpu_custom_call" | custom-call | flops 1073741824 | bytes 2097152 | tf_op jit(solution)/shard_map/pallas_call | solution.py:492
  16.7 0.0 collective-permute-done.first_ref
  16.8 3.5 %shard_map.139 = (f32[4,256,128]{2,1,0:T(8,128)S(1)}, f32[16,136,128]{2,1,0:T(8,128)S(1)}) custom-call(s32[4]{0:T(128)S(1)} %copy-done.9, s32[4,26]{1,0:T(4,128)S(1)} %copy-done.7, s32[2,26]{1,0:T(2,128)S(1)} %copy-done.8, f32[4,256,128]{2,1,0:T(8,128)S(1)} %get-tuple-element.29.own_ref, f32[2,160,128]{2,1,0:T(8,128)S(1)} %collective-permute-done.first_ref, ...), custom_call_target="tpu_custom_call" | custom-call | flops 1811939328 | bytes 2097152 | tf_op jit(solution)/shard_map/pallas_call | solution.py:492
  20.3 0.0 copy-start.11
  20.3 22.7 %all_to_all.10.all_ref = f32[16,136,128]{2,1,0:T(8,128)S(1)} all-to-all(f32[16,136,128]{2,1,0:T(8,128)S(1)} %get-tuple-element.39), channel_id=1, replica_groups=mesh['grp'=16,'dev'=16] {'dev'}, dimensions={0} | all-to-all | bytes 2228224 | tf_op jit(solution)/shard_map/all_to_all | solution.py:549
  43.0 1.7 %shard_map.140 = (f32[840,128]{1,0:T(8,128)S(1)}, s32[256]{0:T(256)S(1)}, s32[64]{0:T(128)S(1)}) custom-call(f32[16,136,128]{2,1,0:T(8,128)S(1)} %all_to_all.10.all_ref), custom_call_target="tpu_custom_call" | custom-call | flops 1048576 | bytes 2097152 | tf_op jit(solution)/shard_map/pallas_call | solution.py:492
  44.7 3.5 %collective-permute-start.2 = (f32[840,128]{1,0:T(8,128)S(1)}, f32[840,128]{1,0:T(8,128)S(1)}, u32[]{:S(2)}, u32[]{:S(2)}) collective-permute-start(f32[840,128]{1,0:T(8,128)S(1)} %get-tuple-element.45), channel_id=1, source_target_pairs={{0,16},{1,17},{16,32},{17,33},{32,48},{33,49},{48,64},{49,65},{64,... | collective-permute-start | bytes 1290248 | tf_op jit(solution)/shard_map/ppermute | solution.py:564
  48.2 1.9 %shard_map.141 = (f32[11,512,128]{2,1,0:T(8,128)S(1)}, f32[8,128]{1,0:T(8,128)S(1)}) custom-call(f32[16,136,128]{2,1,0:T(8,128)S(1)} %all_to_all.10.all_ref, s32[256]{0:T(256)S(1)} %get-tuple-element.40.place_ref, bf16[128,512]{1,0:T(8,128)(2,1)S(1)} %get-tuple-element.41.down_ref), custom_call_target="tpu_custom_call" | custom-call | flops 268435456 | bytes 2097152 | tf_op jit(solution)/shard_map/pallas_call | solution.py:492
  50.1 0.0 copy-start.12
  50.1 4.6 %shard_map.142.inner_ref = f32[2,512,128]{2,1,0:T(8,128)S(1)} custom-call(f32[8,128]{1,0:T(8,128)S(1)} %get-tuple-element.42.links_ref.near_links_ref, f32[11,512,128]{2,1,0:T(8,128)S(1)} %get-tuple-element.44.based_ref, bf16[3456,256]{1,0:T(8,128)(2,1)S(1)} %get-tuple-element.46.weight_ref.first_weight_ref, f32[1,128]{1,0:T(1,128)S(1)} %bitcast.7), custom_call_target="tpu_custom_call" | custom-call | flops 2717908992 | bytes 2097152 | tf_op jit(solution)/shard_map/pallas_call | solution.py:492
  54.8 15.2 %shard_map.143 = f32[64,32,128]{2,1,0:T(8,128)S(1)} custom-call(s32[2,26]{1,0:T(2,128)S(1)} %copy-done.8, f32[8,128]{1,0:T(8,128)S(1)} %get-tuple-element.42.links_ref.near_links_ref, s32[64]{0:T(128)S(1)} %get-tuple-element.43.codes_ref, f32[11,512,128]{2,1,0:T(8,128)S(1)} %get-tuple-element.44.based_ref, f32[840,128]{1,0:T(8,128)S(1)} %collective-permute-done.2.edge_ref, ...), custom_call_target="tpu_custom_call" | custom-call | flops 8153726976 | bytes 2097152 | tf_op jit(solution)/shard_map/pallas_call | solution.py:492
  69.9 0.0 copy-start.3
  70.0 0.0 copy-start.13
  70.0 20.9 %all_to_all.11.risen_ref = f32[16,128,128]{2,1,0:T(8,128)S(1)} all-to-all(f32[16,128,128]{2,1,0:T(8,128)S(1)} %bitcast.5), channel_id=1, replica_groups=mesh['grp'=16,'dev'=16] {'dev'}, dimensions={0} | all-to-all | bytes 2097152 | tf_op jit(solution)/shard_map/all_to_all | solution.py:597
  90.8 0.4 shard_map.144
  91.2 0.3 collective-permute-start.3
  91.5 3.7 %collective-permute-start.4 = (f32[2,160,128]{2,1,0:T(8,128)S(1)}, f32[2,160,128]{2,1,0:T(8,128)S(1)}, u32[]{:S(2)}, u32[]{:S(2)}) collective-permute-start(f32[2,160,128]{2,1,0:T(8,128)S(1)} %get-tuple-element.51), channel_id=1, source_target_pairs={{1,2},{3,4},{5,6},{7,8},{9,10},{11,12},{13,14},{15,16},{17,18},{19... | collective-permute-start | bytes 491528 | tf_op jit(solution)/shard_map/ppermute | solution.py:483
  95.2 1.5 %collective-permute-done.3.first_ref = f32[2,160,128]{2,1,0:T(8,128)S(1)} collective-permute-done((f32[2,160,128]{2,1,0:T(8,128)S(1)}, f32[2,160,128]{2,1,0:T(8,128)S(1)}, u32[]{:S(2)}, u32[]{:S(2)}) %collective-permute-start.3) | collective-permute-done | bytes 163872 | tf_op jit(solution)/shard_map/ppermute | solution.py:484
  96.7 6.5 %collective-permute-done.4.second_ref = f32[2,160,128]{2,1,0:T(8,128)S(1)} collective-permute-done((f32[2,160,128]{2,1,0:T(8,128)S(1)}, f32[2,160,128]{2,1,0:T(8,128)S(1)}, u32[]{:S(2)}, u32[]{:S(2)}) %collective-permute-start.4) | collective-permute-done | bytes 163872 | tf_op jit(solution)/shard_map/ppermute | solution.py:483
  103.2 4.6 %shard_map.145 = f32[4,64,512]{2,1,0:T(8,128)} custom-call(s32[4,26]{1,0:T(4,128)S(1)} %copy-done.7, f32[4,256,128]{2,1,0:T(8,128)S(1)} %get-tuple-element.49.own_ref, f32[2,160,128]{2,1,0:T(8,128)S(1)} %collective-permute-done.3.first_ref, f32[2,160,128]{2,1,0:T(8,128)S(1)} %collective-permute-done.4.second_ref, f32[4,64,512]{2,1,0:T(8,128)S(1)} %copy-done.3, ...), custom_call_target="tpu_custom_call" | custom-call | flops 1811939328 | bytes 2097152 | tf_op jit(solution)/shard_map/pallas_call | solution.py:492
  (19 shorter events, 0.0 us)
Async XLA Ops:
  0.0 12.2 %copy-start = (f32[128,3456]{1,0:T(8,128)S(1)}, f32[128,3456]{1,0:T(8,128)}, u32[]{:S(2)}) copy-start(f32[128,3456]{1,0:T(8,128)} %first_ref.1) | copy-start | bytes 5308420
  0.0 1.2 %copy-start.2 = (f32[4,64,512]{2,1,0:T(8,128)S(1)}, f32[4,64,512]{2,1,0:T(8,128)}, u32[]{:S(2)}) copy-start(f32[4,64,512]{2,1,0:T(8,128)} %features_ref.3) | copy-start | bytes 1572868
  1.7 15.1 %collective-permute-start = (f32[2,160,128]{2,1,0:T(8,128)S(1)}, f32[2,160,128]{2,1,0:T(8,128)S(1)}, u32[]{:S(2)}, u32[]{:S(2)}) collective-permute-start(f32[2,160,128]{2,1,0:T(8,128)S(1)} %get-tuple-element.30), channel_id=1, source_target_pairs={{0,1},{1,0},{2,3},{3,2},{4,5},{5,4},{6,7},{7,6},{8,9},{9,8},{10,11... | collective-permute-start | bytes 491528 | tf_op jit(solution)/shard_map/ppermute | solution.py:484
  3.0 13.8 %collective-permute-start.1 = (f32[2,160,128]{2,1,0:T(8,128)S(1)}, f32[2,160,128]{2,1,0:T(8,128)S(1)}, u32[]{:S(2)}, u32[]{:S(2)}) collective-permute-start(f32[2,160,128]{2,1,0:T(8,128)S(1)} %get-tuple-element.31), channel_id=1, source_target_pairs={{1,2},{3,4},{5,6},{7,8},{9,10},{11,12},{13,14},{15,16},{17,18},{19... | collective-permute-start | bytes 491528 | tf_op jit(solution)/shard_map/ppermute | solution.py:483
  10.8 1.0 copy-start.4
  12.2 1.5 %copy-start.1 = (f32[128,3456]{1,0:T(8,128)S(1)}, f32[128,3456]{1,0:T(8,128)}, u32[]{:S(2)}) copy-start(f32[128,3456]{1,0:T(8,128)} %second_ref.1) | copy-start | bytes 5308420
  13.6 1.0 copy-start.5
  14.7 0.8 copy-start.6
  15.4 1.3 %copy-start.7 = (s32[4,26]{1,0:T(4,128)S(1)}, s32[4,26]{1,0:T(4,128)}, u32[]{:S(2)}) copy-start(s32[4,26]{1,0:T(4,128)} %links_ref.5) | copy-start | bytes 1252
  15.4 1.3 %copy-start.8 = (s32[2,26]{1,0:T(2,128)S(1)}, s32[2,26]{1,0:T(2,128)}, u32[]{:S(2)}) copy-start(s32[2,26]{1,0:T(2,128)} %links_ref.4) | copy-start | bytes 628
  15.4 1.3 %copy-start.9 = (s32[4]{0:T(128)S(1)}, s32[4]{0:T(128)}, u32[]{:S(2)}) copy-start(s32[4]{0:T(128)} %codes_ref.1) | copy-start | bytes 52
  15.4 1.3 %copy-start.10 = (f32[64]{0:T(128)S(1)}, f32[64]{0:T(128)}, u32[]{:S(2)}) copy-start(f32[64]{0:T(128)} %param.19) | copy-start | bytes 772
  20.3 29.8 %copy-start.11 = (f32[128]{0:T(128)S(1)}, f32[128]{0:T(128)}, u32[]{:S(2)}) copy-start(f32[128]{0:T(128)} %param.22) | copy-start | bytes 1540
  44.7 10.0 %collective-permute-start.2 = (f32[840,128]{1,0:T(8,128)S(1)}, f32[840,128]{1,0:T(8,128)S(1)}, u32[]{:S(2)}, u32[]{:S(2)}) collective-permute-start(f32[840,128]{1,0:T(8,128)S(1)} %get-tuple-element.45), channel_id=1, source_target_pairs={{0,16},{1,17},{16,32},{17,33},{32,48},{33,49},{48,64},{49,65},{64,... | collective-permute-start | bytes 1290248 | tf_op jit(solution)/shard_map/ppermute | solution.py:564
  50.1 4.6 %copy-start.12 = (f32[128]{0:T(128)S(1)}, f32[128]{0:T(128)}, u32[]{:S(2)}) copy-start(f32[128]{0:T(128)} %param.24) | copy-start | bytes 1540
  69.9 33.2 %copy-start.3 = (f32[4,64,512]{2,1,0:T(8,128)S(1)}, f32[4,64,512]{2,1,0:T(8,128)}, u32[]{:S(2)}) copy-start(f32[4,64,512]{2,1,0:T(8,128)} %features_ref.3) | copy-start | bytes 1572868
  70.0 33.2 %copy-start.13 = (f32[64]{0:T(128)S(1)}, f32[64]{0:T(128)}, u32[]{:S(2)}) copy-start(f32[64]{0:T(128)} %param.27) | copy-start | bytes 772
  91.2 5.5 %collective-permute-start.3 = (f32[2,160,128]{2,1,0:T(8,128)S(1)}, f32[2,160,128]{2,1,0:T(8,128)S(1)}, u32[]{:S(2)}, u32[]{:S(2)}) collective-permute-start(f32[2,160,128]{2,1,0:T(8,128)S(1)} %get-tuple-element.50), channel_id=1, source_target_pairs={{0,1},{1,0},{2,3},{3,2},{4,5},{5,4},{6,7},{7,6},{8,9},{9,8},{10,11... | collective-permute-start | bytes 491528 | tf_op jit(solution)/shard_map/ppermute | solution.py:484
  91.5 11.7 %collective-permute-start.4 = (f32[2,160,128]{2,1,0:T(8,128)S(1)}, f32[2,160,128]{2,1,0:T(8,128)S(1)}, u32[]{:S(2)}, u32[]{:S(2)}) collective-permute-start(f32[2,160,128]{2,1,0:T(8,128)S(1)} %get-tuple-element.51), channel_id=1, source_target_pairs={{1,2},{3,4},{5,6},{7,8},{9,10},{11,12},{13,14},{15,16},{17,18},{19... | collective-permute-start | bytes 491528 | tf_op jit(solution)/shard_map/ppermute | solution.py:483

commit v4 on v3

--- a/solution.py
+++ b/solution.py
@@ -15,7 +15,7 @@
     )
 }
 PLANE = {-1: (56, 8), 0: (0, 64), 1: (0, 8)}
-ROOM = {-1: slice(0, 1), 0: slice(1, 9), 1: slice(9, 10)}
+CHUNKS = [(-1, 56, 1, 0), (0, 0, 2, 1), (0, 16, 2, 3), (0, 32, 2, 5), (0, 48, 2, 7), (1, 0, 1, 9)]
 VMEM = pl.BlockSpec(memory_space=pltpu.VMEM)
 SMEM = pl.BlockSpec(memory_space=pltpu.SMEM)
 
@@ -109,11 +109,28 @@
     )
 
 
-def product(high, low, weight_ref):
-    both = jnp.dot(high, weight_ref[...], preferred_element_type=F32)
+def product(high, low, weight):
+    both = jnp.dot(high, weight, preferred_element_type=F32)
     half = both.shape[1] // 2
-    rest = jnp.dot(low, weight_ref[:, :half], preferred_element_type=F32)
+    rest = jnp.dot(low, weight[:, :half], preferred_element_type=F32)
     return both[:, :half] + both[:, half:] + rest
+
+
+def filter_data(a, b, c, d):
+    return a - c, b + c, c - b, b - d
+
+
+def filter_taps(a, b, c):
+    return a, (a + b + c) * 0.5, (a - b + c) * 0.5, c
+
+
+def filtered(high, low, columns, weight_ref):
+    depth = weight_ref.shape[0] // 4
+    m = [
+        product(columns(high, k), columns(low, k), weight_ref[depth * k : depth * k + depth, :])
+        for k in range(4)
+    ]
+    return m[0] + m[1] + m[2], m[1] - m[2] - m[3]
 
 
 def fine_rim(source, links_ref, high, low):
@@ -125,35 +142,42 @@
             near[0, 0, 0] = b + 2
             found.append(near)
         for k in range(5):
-            for dx in STEPS:
-                rows = []
-                for near in found:
-
-                    def tile(dy):
+            rows = []
+            for near in found:
+
+                def tile(dy):
+                    parts = []
+                    for dx in STEPS:
                         first = near[dx, dy, -1 if k == 0 else 0]
                         second = near[dx, dy, 1 if k == 4 else 0]
                         a = planes(source, first, (k + 3) % 4, dx)
                         b = planes(source, second, k % 4, dx)
-                        return jnp.where(low_lanes(a.shape), a, b)
-
-                    rows.append(shifted_rows(tile))
-                for j in range(3):
-                    both = jnp.concatenate([rows[0][j], rows[1][j]], axis=1)
-                    h, l = split(both)
-                    high[j, k, ROOM[dx], 16 * pair : 16 * pair + 16, :] = h
-                    low[j, k, ROOM[dx], 16 * pair : 16 * pair + 16, :] = l
-
-
-def fine_columns(padded, zz):
-    return jnp.concatenate(
-        [
-            padded[j, zz + h, i : i + 8].reshape(256, 128)
-            for i in range(3)
-            for j in range(3)
-            for h in range(2)
-        ],
-        axis=1,
-    )
+                        parts.append(jnp.where(low_lanes(a.shape), a, b))
+                    return jnp.concatenate(parts, axis=0)
+
+                rows.append(shifted_rows(tile))
+            for j in range(3):
+                both = jnp.concatenate([rows[0][j], rows[1][j]], axis=1).reshape(5, 2, 16, 128)
+                parts = filter_data(both[:4, 0], both[:4, 1], both[1:, 0], both[1:, 1])
+                for n, part in enumerate(parts):
+                    h, l = split(part)
+                    high[n, j, k, :, 16 * pair : 16 * pair + 16, :] = h
+                    low[n, j, k, :, 16 * pair : 16 * pair + 16, :] = l
+
+
+def fine_convolved(high, low, half, weight_ref, bias):
+    def columns(padded, k):
+        return jnp.concatenate(
+            [
+                padded[k, j, 2 * half + h : 2 * half + h + 2].reshape(256, 128)
+                for j in range(3)
+                for h in range(2)
+            ],
+            axis=1,
+        )
+
+    pair = [y.reshape(2, 4, 32, 128) for y in filtered(high, low, columns, weight_ref)]
+    return jnp.stack(pair, axis=2).reshape(2, 8, 32, 128) + bias
 
 
 def turn_kernel(features_ref, own_ref, first_ref, second_ref, flat, middle):
@@ -176,21 +200,29 @@
         taps += [turned[r : r + 64] for r in range(0, turned.shape[0], 64)]
     nothing = jnp.zeros((64, 128), F32)
     lower = low_lanes((64, 128))
+    for j in range(3):
+        for z in range(4):
+            across = []
+            for i in range(3):
+                at = 3 * (3 * i + j) + z
+                odd = taps[at - 1] if z >= 1 else nothing
+                even = taps[at] if z <= 2 else nothing
+                across.append(jnp.where(lower, odd, even))
+            for n, part in enumerate(filter_taps(*across)):
+                h, l = split(part)
+                at = 768 * n + 256 * j + 64 * z
+                out_ref[at : at + 64, 0:128] = h
+                out_ref[at : at + 64, 128:256] = l
+
+
+def coarse_weight_rows(weight_ref, out_ref):
     for n in range(9):
-        for z in range(4):
-            odd = taps[3 * n + z - 1] if z >= 1 else nothing
-            even = taps[3 * n + z] if z <= 2 else nothing
-            h, l = split(jnp.where(lower, odd, even))
-            at = 256 * n + 64 * z
-            out_ref[at : at + 64, 0:128] = h
-            out_ref[at : at + 64, 128:256] = l
-
-
-def coarse_weight_rows(weight_ref, out_ref):
-    for at in range(0, 3456, 128):
-        h, l = split(weight_ref[:, at : at + 128].T)
-        out_ref[at : at + 128, 0:128] = h
-        out_ref[at : at + 128, 128:256] = l
+        taps = [weight_ref[:, 128 * t : 128 * t + 128].T for t in range(3 * n, 3 * n + 3)]
+        for k, part in enumerate(filter_taps(*taps)):
+            h, l = split(part)
+            at = 1152 * k + 128 * n
+            out_ref[at : at + 128, 0:128] = h
+            out_ref[at : at + 128, 128:256] = l
 
 
 def first_weight_kernel(weight_ref, out_ref):
@@ -227,18 +259,17 @@
     fine_halo(first_ref, second_ref, source, middle)
     fine_rim(source, links_ref, high, low)
     bias = jnp.concatenate([bias_ref[...]] * 2, axis=1)
-    held = []
-    for zz in range(4):
-        r = product(fine_columns(high, zz), fine_columns(low, zz), weight_ref) + bias
-        r = silu(r).reshape(8, 32, 128)
-        for b in range(4):
-            hidden_ref[b, 64 * zz : 64 * zz + 64] = r[:, 8 * b : 8 * b + 8].reshape(64, 128)
-        r = r.reshape(4, 2, 32, 128)
-        r = r[:, 0] + r[:, 1]
-        held.append(r + swap(r))
-        if zz % 2 == 1:
-            both = jnp.where(low_lanes(r.shape), held[zz], held[zz - 1])
-            sums[64 * zz - 64 : 64 * zz + 64, :] = both.reshape(128, 128)
+    for half in range(2):
+        r = silu(fine_convolved(high, low, half, weight_ref, bias))
+        for h in range(2):
+            at = 64 * (2 * half + h)
+            for b in range(4):
+                hidden_ref[b, at : at + 64] = r[h, :, 8 * b : 8 * b + 8].reshape(64, 128)
+        r = r.reshape(2, 4, 2, 32, 128)
+        r = r[:, :, 0] + r[:, :, 1]
+        r = r + swap(r)
+        both = jnp.where(low_lanes(r[0].shape), r[1], r[0])
+        sums[128 * half : 128 * half + 128, :] = both.reshape(128, 128)
     means = (sums[pl.ds(0, 128, 2), :] + sums[pl.ds(1, 128, 2), :]) * 0.125
     for n in range(8):
         for b in range(4):
@@ -296,7 +327,7 @@
 
 def bring_down(cubes, down_ref, source, n):
     h, l = split(cubes)
-    based = product(h, l, down_ref)
+    based = product(h, l, down_ref[...])
     for z in range(8):
         k = 1 - z % 2
         source[n, 64 * z : 64 * z + 64] = based[64 * (z // 2) : 64 * (z // 2) + 64, 128 * k : 128 * k + 128]
@@ -325,39 +356,49 @@
         near = neighbours(links_ref, row + s, start, none)
         near[0, 0, 0] = home + s
         found.append(near)
-    for z in range(10):
-        dz = -1 if z == 0 else 1 if z == 9 else 0
-        at = {-1: 7, 0: z - 1, 1: 0}[dz]
-        for dx in STEPS:
+    for dx, at, count, room in CHUNKS:
+        window = []
+        for z in range(10):
+            dz = -1 if z == 0 else 1 if z == 9 else 0
+            begin = 64 * {-1: 7, 0: z - 1, 1: 0}[dz] + at
             rows = [
-                shifted_rows(lambda dy, near=near: planes(source, near[dx, dy, dz], at, dx))
+                shifted_rows(
+                    lambda dy, near=near: source[near[dx, dy, dz], begin : begin + 8 * count, :].reshape(count, 8, 128)
+                )
                 for near in found
             ]
-            for j in range(3):
-                h, l = split(jnp.concatenate([rows[0][j], rows[1][j]], axis=1))
-                high[j, z, ROOM[dx]] = h
-                low[j, z, ROOM[dx]] = l
-
-
-def coarse_columns(padded, z):
-    return jnp.concatenate(
-        [
-            padded[j, z + l : z + l + 2, i : i + 8].reshape(256, 128)
-            for i in range(3)
-            for j in range(3)
-            for l in range(3)
-        ],
-        axis=1,
-    )
+            window.append([jnp.concatenate([rows[0][j], rows[1][j]], axis=1) for j in range(3)])
+            if z >= 3 and z % 2 == 1:
+                for j in range(3):
+                    for k, part in enumerate(filter_data(*[w[j] for w in window[z - 3 :]])):
+                        h, l = split(part)
+                        high[k, j, z // 2 - 1, room : room + count] = h
+                        low[k, j, z // 2 - 1, room : room + count] = l
+
+
+def coarse_convolved(high, low, half, weight_ref, bias):
+    def columns(padded, k):
+        return jnp.concatenate(
+            [
+                padded[k, j, 2 * half : 2 * half + 2, i : i + 8].reshape(256, 128)
+                for i in range(3)
+                for j in range(3)
+            ],
+            axis=1,
+        )
+
+    return [silu(y + bias) for y in filtered(high, low, columns, weight_ref)]
 
 
 def coarse_first_pair(source, links_ref, pair, weight_ref, bias_ref, out_ref, n, high, low):
     coarse_rim(source, links_ref, 2 * pair, 2 * pair + 2, device_number() * 2 - 4, 10, high, low)
-    for z in range(0, 8, 2):
-        r = product(coarse_columns(high, z), coarse_columns(low, z), weight_ref) + bias_ref[...]
-        r = silu(r).reshape(2, 8, 16, 128)
-        for s in range(2):
-            out_ref[n + s, 64 * z : 64 * z + 128] = r[:, :, 8 * s : 8 * s + 8].reshape(128, 128)
+    for half in range(2):
+        for odd, r in enumerate(coarse_convolved(high, low, half, weight_ref, bias_ref[...])):
+            r = r.reshape(2, 8, 16, 128)
+            for s in range(2):
+                for h in range(2):
+                    at = 64 * (4 * half + 2 * h + odd)
+                    out_ref[n + s, at : at + 64] = r[h, :, 8 * s : 8 * s + 8].reshape(64, 128)
 
 
 def inner_pair():
@@ -410,17 +451,15 @@
     coarse_first_pair(source, spelled, outer, first_weight_ref, first_bias_ref, seconds, 2 * outer, high, low)
     coarse_first_pair(source, spelled, 1, first_weight_ref, first_bias_ref, seconds, 2, high2, low2)
     coarse_rim(seconds, links_ref, 0, 2, device_number() * 2 - 2, 6, high, low)
-    for z in range(0, 8, 2):
-        c, q = z // 4, z // 2 % 2
-        r = product(coarse_columns(high, z), coarse_columns(low, z), weight_ref) + bias_ref[...]
-        r = silu(r)
-        h, l = split(jnp.concatenate([r[:128], r[128:]], axis=1))
-        lifted = product(h, l, up_ref)
+    for c in range(2):
+        h, l = split(jnp.concatenate(coarse_convolved(high, low, c, weight_ref, bias_ref[...]), axis=1))
+        lifted = product(h, l, up_ref[...])
         for t in range(c, 16, 2):
             s, a, b = t // 8, t // 4 % 2, t // 2 % 2
-            for x in range(4):
-                at = (4 * a + x) * 16 + 8 * s + 4 * b
-                octants[t, 16 * q + 4 * x : 16 * q + 4 * x + 4, :] = lifted[at : at + 4]
+            for q in range(2):
+                for x in range(4):
+                    at = 128 * q + (4 * a + x) * 16 + 8 * s + 4 * b
+                    octants[t, 16 * q + 4 * x : 16 * q + 4 * x + 4, :] = lifted[at : at + 4]
     base = lax.axis_index("dev") * 16
 
     def place(i, carry):
@@ -463,8 +502,9 @@
     fine_rim(source, links_ref, high, low)
     bias = jnp.concatenate([bias_ref[...]] * 2, axis=1)
     for zz in range(4):
-        r = product(fine_columns(high, zz), fine_columns(low, zz), weight_ref) + bias
-        r = r.reshape(8, 32, 128)
+        if zz % 2 == 0:
+            both = fine_convolved(high, low, zz // 2, weight_ref, bias)
+        r = both[zz % 2]
         for p in range(2):
             v0 = r[:, 16 * p : 16 * p + 8].reshape(64, 128)
             v1 = r[:, 16 * p + 8 : 16 * p + 16].reshape(64, 128)
@@ -505,7 +545,7 @@
     coarse_first_weight, coarse_first_bias, coarse_second_weight, coarse_second_bias,
     up_weight, fine_out_weight, fine_out_bias,
 ):
-    fine_padded = [pltpu.VMEM((3, 5, 10, 32, 128), BF16)] * 2
+    fine_padded = [pltpu.VMEM((4, 3, 5, 4, 32, 128), BF16)] * 2
     fine_source = pltpu.VMEM((9, 256, 128), F32)
     middle = pltpu.VMEM((192, 128), F32)
     brick, shell = struct(4, 256, 128), struct(2, 160, 128)
@@ -520,15 +560,15 @@
     )
     first, second = exchanged(first, second)
     weight_in = call(
-        first_weight_kernel, struct(2304, 256, dtype=BF16), [], [VMEM], (fine_in_weight,), 1 << 20
+        first_weight_kernel, struct(3072, 256, dtype=BF16), [], [VMEM], (fine_in_weight,), 1 << 20
     )
     later = (coarse_first_weight, coarse_second_weight, down_weight, up_weight, fine_out_weight)
     weight_first, weight_second, down, up, weight_out = call(
         later_weights_kernel,
         (
-            struct(3456, 256, dtype=BF16), struct(3456, 256, dtype=BF16),
+            struct(4608, 256, dtype=BF16), struct(4608, 256, dtype=BF16),
             struct(128, 512, dtype=BF16), struct(256, 256, dtype=BF16),
-            struct(2304, 256, dtype=BF16),
+            struct(3072, 256, dtype=BF16),
         ),
         [],
         [VMEM] * 5,
@@ -570,7 +610,7 @@
         (spread, place, down),
         1 << 28,
     )
-    coarse_padded = [pltpu.VMEM((3, 10, 10, 16, 128), BF16)] * 2
+    coarse_padded = [pltpu.VMEM((4, 3, 4, 10, 16, 128), BF16)] * 2
     inner = call(
         inner_kernel,
         struct(2, 512, 128),

time: 108 us -> 102 us (0.944)
  Pallas kernels: 33.9 us -> 28.1 us
  starting transfers between devices: 15.7 us -> 17 us
  local copies, waits for them, and re-layouts: 6.33 us -> 5.08 us
    pallas_call x10, Pallas kernels: 33.9 us -> 28.1 us  [call(): pl.pallas_call(kernel, out_shape=out, in_specs=specs, out_specs=jax.tree....]
    ppermute x1, starting transfers between devices: 3.46 us -> 4.73 us  [per_device(): edge = lax.ppermute(cubes, BOTH, edges)]
    unnamed x29, local copies, waits for them, and re-layouts: 6.33 us -> 5.08 us
  transfers between devices with their start and end apart: 5 -> 5, of which waited for: 2 -> 2; matrix products, arithmetic and copies ran while one was open for 1% -> 1% of each run, Pallas kernels for 8% -> 7%
where the time goes in v4:
time: 102 us; the launch traced here: 101 us
  blocking collectives  42.6 us (42%)
  Pallas kernels  28.1 us (28%)
  starting transfers between devices  17 us (17%)
  waiting for transfers between devices  8.14 us (8%)
  local copies, waits for them, and re-layouts  5.08 us (5%)
    pallas_call x10, Pallas kernels, call(): pl.pallas_call(kernel, out_shape=out, in_specs=specs, out_specs=jax.tree....  28.1 us
    all_to_all x1, blocking collectives, per_device(): spread = lax.all_to_all(pooled, 'dev', 0, 0, tiled=True)  22.3 us
    all_to_all x1, blocking collectives, per_device(): lax.all_to_all(lifted.reshape(16, 128, 128), 'dev', 0, 0, tiled=True)  20.3 us
    ppermute x2, starting transfers between devices, exchanged(): second = lax.ppermute(second, BOTH, outer)  10.6 us
    ppermute x2, waiting for transfers between devices, exchanged(): second = lax.ppermute(second, BOTH, outer)  6.48 us
    unnamed x29, local copies, waits for them, and re-layouts  5.08 us
    ppermute x1, starting transfers between devices, per_device(): edge = lax.ppermute(cubes, BOTH, edges)  4.73 us
  transfers between devices with their start and end apart: 5, of which 2 were waited for; matrix products, arithmetic and copies ran while one was open for 1% of the time, Pallas kernels for 7%

profile of v4, /device:TPU:97, one launch (start us, length us, event | category | flops | bytes accessed | tf_op | source)
XLA Modules:
  0.0 101.1 jit_solution(9483459725622665917)
XLA Ops:
  0.0 1.2 %copy-done.2 = f32[4,64,512]{2,1,0:T(8,128)S(1)} copy-done((f32[4,64,512]{2,1,0:T(8,128)S(1)}, f32[4,64,512]{2,1,0:T(8,128)}, u32[]{:S(2)}) %copy-start.2) | copy-done | bytes 524312
  1.2 0.5 shard_map.136
  1.7 1.3 %collective-permute-start = (f32[2,160,128]{2,1,0:T(8,128)S(1)}, f32[2,160,128]{2,1,0:T(8,128)S(1)}, u32[]{:S(2)}, u32[]{:S(2)}) collective-permute-start(f32[2,160,128]{2,1,0:T(8,128)S(1)} %get-tuple-element.30), channel_id=1, source_target_pairs={{0,1},{1,0},{2,3},{3,2},{4,5},{5,4},{6,7},{7,6},{8,9},{9,8},{10,11... | collective-permute-start | bytes 491528 | tf_op jit(solution)/shard_map/ppermute | solution.py:524
  3.0 7.0 %collective-permute-start.1 = (f32[2,160,128]{2,1,0:T(8,128)S(1)}, f32[2,160,128]{2,1,0:T(8,128)S(1)}, u32[]{:S(2)}, u32[]{:S(2)}) collective-permute-start(f32[2,160,128]{2,1,0:T(8,128)S(1)} %get-tuple-element.31), channel_id=1, source_target_pairs={{1,2},{3,4},{5,6},{7,8},{9,10},{11,12},{13,14},{15,16},{17,18},{19... | collective-permute-start | bytes 491528 | tf_op jit(solution)/shard_map/ppermute | solution.py:523
  10.0 0.8 copy.15.down_ref
  10.8 0.0 copy-start.4
  10.8 1.0 %copy-done.4 = f32[64,1728]{1,0:T(8,128)S(1)} copy-done((f32[64,1728]{1,0:T(8,128)S(1)}, f32[64,1728]{1,0:T(8,128)}, u32[]{:S(2)}) %copy-start.4) | copy-done | bytes 442392
  11.8 0.5 shard_map.137.weight_ref
  12.3 0.5 copy-done.5
  12.9 1.5 %copy-done.1 = f32[128,3456]{1,0:T(8,128)S(1)} copy-done((f32[128,3456]{1,0:T(8,128)S(1)}, f32[128,3456]{1,0:T(8,128)}, u32[]{:S(2)}) %copy-start.1) | copy-done | bytes 1769496
  14.4 1.5 %shard_map.138 = (bf16[4608,256]{1,0:T(8,128)(2,1)S(1)}, bf16[4608,256]{1,0:T(8,128)(2,1)S(1)}, bf16[128,512]{1,0:T(8,128)(2,1)S(1)}, bf16[256,256]{1,0:T(8,128)(2,1)S(1)}, bf16[3072,256]{1,0:T(8,128)(2,1)S(1)}) custom-call(f32[128,3456]{1,0:T(8,128)S(1)} %copy-done, f32[128,3456]{1,0:T(8,128)S(1)} %copy-done.1, f32[128,64]{1,0:T(8,128)S(1)} %copy.15.down_ref, ...), custom_call_target="tpu_custom_call" | custom-call | flops 1073741824 | bytes 2097152 | tf_op jit(solution)/shard_map/pallas_call | solution.py:532
  15.9 0.0 collective-permute-done.first_ref
  15.9 0.0 collective-permute-done.1.second_ref
  15.9 2.8 %shard_map.139 = (f32[4,256,128]{2,1,0:T(8,128)S(1)}, f32[16,136,128]{2,1,0:T(8,128)S(1)}) custom-call(s32[4]{0:T(128)S(1)} %copy-done.9, s32[4,26]{1,0:T(4,128)S(1)} %copy-done.7, s32[2,26]{1,0:T(2,128)S(1)} %copy-done.8, f32[4,256,128]{2,1,0:T(8,128)S(1)} %get-tuple-element.29.own_ref, f32[2,160,128]{2,1,0:T(8,128)S(1)} %collective-permute-done.first_ref, ...), custom_call_target="tpu_custom_call" | custom-call | flops 1811939328 | bytes 2097152 | tf_op jit(solution)/shard_map/pallas_call | solution.py:532
  18.7 0.0 copy-start.11
  18.8 22.3 %all_to_all.10.all_ref = f32[16,136,128]{2,1,0:T(8,128)S(1)} all-to-all(f32[16,136,128]{2,1,0:T(8,128)S(1)} %get-tuple-element.39), channel_id=1, replica_groups=mesh['grp'=16,'dev'=16] {'dev'}, dimensions={0} | all-to-all | bytes 2228224 | tf_op jit(solution)/shard_map/all_to_all | solution.py:589
  41.1 1.7 %shard_map.140 = (f32[840,128]{1,0:T(8,128)S(1)}, s32[256]{0:T(256)S(1)}, s32[64]{0:T(128)S(1)}) custom-call(f32[16,136,128]{2,1,0:T(8,128)S(1)} %all_to_all.10.all_ref), custom_call_target="tpu_custom_call" | custom-call | flops 1048576 | bytes 2097152 | tf_op jit(solution)/shard_map/pallas_call | solution.py:532
  42.8 4.7 %collective-permute-start.2 = (f32[840,128]{1,0:T(8,128)S(1)}, f32[840,128]{1,0:T(8,128)S(1)}, u32[]{:S(2)}, u32[]{:S(2)}) collective-permute-start(f32[840,128]{1,0:T(8,128)S(1)} %get-tuple-element.45), channel_id=1, source_target_pairs={{0,16},{1,17},{16,32},{17,33},{32,48},{33,49},{48,64},{49,65},{64,... | collective-permute-start | bytes 1290248 | tf_op jit(solution)/shard_map/ppermute | solution.py:604
  47.5 1.9 %shard_map.141 = (f32[11,512,128]{2,1,0:T(8,128)S(1)}, f32[8,128]{1,0:T(8,128)S(1)}) custom-call(f32[16,136,128]{2,1,0:T(8,128)S(1)} %all_to_all.10.all_ref, s32[256]{0:T(256)S(1)} %get-tuple-element.40.place_ref, bf16[128,512]{1,0:T(8,128)(2,1)S(1)} %get-tuple-element.41.down_ref), custom_call_target="tpu_custom_call" | custom-call | flops 268435456 | bytes 2097152 | tf_op jit(solution)/shard_map/pallas_call | solution.py:532
  49.4 0.0 copy-start.12
  49.4 3.5 %shard_map.142.inner_ref = f32[2,512,128]{2,1,0:T(8,128)S(1)} custom-call(f32[8,128]{1,0:T(8,128)S(1)} %get-tuple-element.42.links_ref.near_links_ref, f32[11,512,128]{2,1,0:T(8,128)S(1)} %get-tuple-element.44.based_ref, bf16[4608,256]{1,0:T(8,128)(2,1)S(1)} %get-tuple-element.46.weight_ref.first_weight_ref, f32[1,128]{1,0:T(1,128)S(1)} %bitcast.7), custom_call_target="tpu_custom_call" | custom-call | flops 2717908992 | bytes 2097152 | tf_op jit(solution)/shard_map/pallas_call | solution.py:532
  52.9 0.0 collective-permute-done.2.edge_ref
  52.9 11.8 %shard_map.143 = f32[64,32,128]{2,1,0:T(8,128)S(1)} custom-call(s32[2,26]{1,0:T(2,128)S(1)} %copy-done.8, f32[8,128]{1,0:T(8,128)S(1)} %get-tuple-element.42.links_ref.near_links_ref, s32[64]{0:T(128)S(1)} %get-tuple-element.43.codes_ref, f32[11,512,128]{2,1,0:T(8,128)S(1)} %get-tuple-element.44.based_ref, f32[840,128]{1,0:T(8,128)S(1)} %collective-permute-done.2.edge_ref, ...), custom_call_target="tpu_custom_call" | custom-call | flops 8153726976 | bytes 2097152 | tf_op jit(solution)/shard_map/pallas_call | solution.py:532
  64.7 0.0 copy-start.3
  64.7 0.0 copy-start.13
  64.7 20.3 %all_to_all.11.risen_ref = f32[16,128,128]{2,1,0:T(8,128)S(1)} all-to-all(f32[16,128,128]{2,1,0:T(8,128)S(1)} %bitcast.5), channel_id=1, replica_groups=mesh['grp'=16,'dev'=16] {'dev'}, dimensions={0} | all-to-all | bytes 2097152 | tf_op jit(solution)/shard_map/all_to_all | solution.py:637
  85.0 0.4 shard_map.144
  85.4 0.4 collective-permute-start.3
  85.8 3.6 %collective-permute-start.4 = (f32[2,160,128]{2,1,0:T(8,128)S(1)}, f32[2,160,128]{2,1,0:T(8,128)S(1)}, u32[]{:S(2)}, u32[]{:S(2)}) collective-permute-start(f32[2,160,128]{2,1,0:T(8,128)S(1)} %get-tuple-element.51), channel_id=1, source_target_pairs={{1,2},{3,4},{5,6},{7,8},{9,10},{11,12},{13,14},{15,16},{17,18},{19... | collective-permute-start | bytes 491528 | tf_op jit(solution)/shard_map/ppermute | solution.py:523
  89.4 1.7 %collective-permute-done.3.first_ref = f32[2,160,128]{2,1,0:T(8,128)S(1)} collective-permute-done((f32[2,160,128]{2,1,0:T(8,128)S(1)}, f32[2,160,128]{2,1,0:T(8,128)S(1)}, u32[]{:S(2)}, u32[]{:S(2)}) %collective-permute-start.3) | collective-permute-done | bytes 163872 | tf_op jit(solution)/shard_map/ppermute | solution.py:524
  91.0 6.5 %collective-permute-done.4.second_ref = f32[2,160,128]{2,1,0:T(8,128)S(1)} collective-permute-done((f32[2,160,128]{2,1,0:T(8,128)S(1)}, f32[2,160,128]{2,1,0:T(8,128)S(1)}, u32[]{:S(2)}, u32[]{:S(2)}) %collective-permute-start.4) | collective-permute-done | bytes 163872 | tf_op jit(solution)/shard_map/ppermute | solution.py:523
  97.5 3.6 %shard_map.145 = f32[4,64,512]{2,1,0:T(8,128)} custom-call(s32[4,26]{1,0:T(4,128)S(1)} %copy-done.7, f32[4,256,128]{2,1,0:T(8,128)S(1)} %get-tuple-element.49.own_ref, f32[2,160,128]{2,1,0:T(8,128)S(1)} %collective-permute-done.3.first_ref, f32[2,160,128]{2,1,0:T(8,128)S(1)} %collective-permute-done.4.second_ref, f32[4,64,512]{2,1,0:T(8,128)S(1)} %copy-done.3, ...), custom_call_target="tpu_custom_call" | custom-call | flops 1811939328 | bytes 2097152 | tf_op jit(solution)/shard_map/pallas_call | solution.py:532
  (19 shorter events, 0.0 us)
Async XLA Ops:
  0.0 12.3 %copy-start = (f32[128,3456]{1,0:T(8,128)S(1)}, f32[128,3456]{1,0:T(8,128)}, u32[]{:S(2)}) copy-start(f32[128,3456]{1,0:T(8,128)} %first_ref.1) | copy-start | bytes 5308420
  0.0 1.2 %copy-start.2 = (f32[4,64,512]{2,1,0:T(8,128)S(1)}, f32[4,64,512]{2,1,0:T(8,128)}, u32[]{:S(2)}) copy-start(f32[4,64,512]{2,1,0:T(8,128)} %features_ref.3) | copy-start | bytes 1572868
  1.7 14.2 %collective-permute-start = (f32[2,160,128]{2,1,0:T(8,128)S(1)}, f32[2,160,128]{2,1,0:T(8,128)S(1)}, u32[]{:S(2)}, u32[]{:S(2)}) collective-permute-start(f32[2,160,128]{2,1,0:T(8,128)S(1)} %get-tuple-element.30), channel_id=1, source_target_pairs={{0,1},{1,0},{2,3},{3,2},{4,5},{5,4},{6,7},{7,6},{8,9},{9,8},{10,11... | collective-permute-start | bytes 491528 | tf_op jit(solution)/shard_map/ppermute | solution.py:524
  3.0 12.9 %collective-permute-start.1 = (f32[2,160,128]{2,1,0:T(8,128)S(1)}, f32[2,160,128]{2,1,0:T(8,128)S(1)}, u32[]{:S(2)}, u32[]{:S(2)}) collective-permute-start(f32[2,160,128]{2,1,0:T(8,128)S(1)} %get-tuple-element.31), channel_id=1, source_target_pairs={{1,2},{3,4},{5,6},{7,8},{9,10},{11,12},{13,14},{15,16},{17,18},{19... | collective-permute-start | bytes 491528 | tf_op jit(solution)/shard_map/ppermute | solution.py:523
  10.8 1.0 %copy-start.4 = (f32[64,1728]{1,0:T(8,128)S(1)}, f32[64,1728]{1,0:T(8,128)}, u32[]{:S(2)}) copy-start(f32[64,1728]{1,0:T(8,128)} %weight_ref.1) | copy-start | bytes 1327108
  11.8 1.0 %copy-start.5 = (f32[64,1728]{1,0:T(8,128)S(1)}, f32[64,1728]{1,0:T(8,128)}, u32[]{:S(2)}) copy-start(f32[64,1728]{1,0:T(8,128)} %fine_ref.1) | copy-start | bytes 1327108
  11.8 1.0 %copy-start.6 = (f32[64,128]{1,0:T(8,128)S(1)}, f32[64,128]{1,0:T(8,128)}, u32[]{:S(2)}) copy-start(f32[64,128]{1,0:T(8,128)} %up_ref.1) | copy-start | bytes 98308
  12.9 1.5 %copy-start.1 = (f32[128,3456]{1,0:T(8,128)S(1)}, f32[128,3456]{1,0:T(8,128)}, u32[]{:S(2)}) copy-start(f32[128,3456]{1,0:T(8,128)} %second_ref.1) | copy-start | bytes 5308420
  14.3 1.5 %copy-start.7 = (s32[4,26]{1,0:T(4,128)S(1)}, s32[4,26]{1,0:T(4,128)}, u32[]{:S(2)}) copy-start(s32[4,26]{1,0:T(4,128)} %links_ref.5) | copy-start | bytes 1252
  14.3 1.6 %copy-start.8 = (s32[2,26]{1,0:T(2,128)S(1)}, s32[2,26]{1,0:T(2,128)}, u32[]{:S(2)}) copy-start(s32[2,26]{1,0:T(2,128)} %links_ref.4) | copy-start | bytes 628
  14.3 1.6 %copy-start.9 = (s32[4]{0:T(128)S(1)}, s32[4]{0:T(128)}, u32[]{:S(2)}) copy-start(s32[4]{0:T(128)} %codes_ref.1) | copy-start | bytes 52
  14.3 1.6 %copy-start.10 = (f32[64]{0:T(128)S(1)}, f32[64]{0:T(128)}, u32[]{:S(2)}) copy-start(f32[64]{0:T(128)} %param.19) | copy-start | bytes 772
  18.7 30.7 %copy-start.11 = (f32[128]{0:T(128)S(1)}, f32[128]{0:T(128)}, u32[]{:S(2)}) copy-start(f32[128]{0:T(128)} %param.22) | copy-start | bytes 1540
  42.8 10.2 %collective-permute-start.2 = (f32[840,128]{1,0:T(8,128)S(1)}, f32[840,128]{1,0:T(8,128)S(1)}, u32[]{:S(2)}, u32[]{:S(2)}) collective-permute-start(f32[840,128]{1,0:T(8,128)S(1)} %get-tuple-element.45), channel_id=1, source_target_pairs={{0,16},{1,17},{16,32},{17,33},{32,48},{33,49},{48,64},{49,65},{64,... | collective-permute-start | bytes 1290248 | tf_op jit(solution)/shard_map/ppermute | solution.py:604
  49.4 3.5 %copy-start.12 = (f32[128]{0:T(128)S(1)}, f32[128]{0:T(128)}, u32[]{:S(2)}) copy-start(f32[128]{0:T(128)} %param.24) | copy-start | bytes 1540
  64.7 32.8 %copy-start.3 = (f32[4,64,512]{2,1,0:T(8,128)S(1)}, f32[4,64,512]{2,1,0:T(8,128)}, u32[]{:S(2)}) copy-start(f32[4,64,512]{2,1,0:T(8,128)} %features_ref.3) | copy-start | bytes 1572868
  64.7 32.8 %copy-start.13 = (f32[64]{0:T(128)S(1)}, f32[64]{0:T(128)}, u32[]{:S(2)}) copy-start(f32[64]{0:T(128)} %param.27) | copy-start | bytes 772
  85.4 5.6 %collective-permute-start.3 = (f32[2,160,128]{2,1,0:T(8,128)S(1)}, f32[2,160,128]{2,1,0:T(8,128)S(1)}, u32[]{:S(2)}, u32[]{:S(2)}) collective-permute-start(f32[2,160,128]{2,1,0:T(8,128)S(1)} %get-tuple-element.50), channel_id=1, source_target_pairs={{0,1},{1,0},{2,3},{3,2},{4,5},{5,4},{6,7},{7,6},{8,9},{9,8},{10,11... | collective-permute-start | bytes 491528 | tf_op jit(solution)/shard_map/ppermute | solution.py:524
  85.8 11.7 %collective-permute-start.4 = (f32[2,160,128]{2,1,0:T(8,128)S(1)}, f32[2,160,128]{2,1,0:T(8,128)S(1)}, u32[]{:S(2)}, u32[]{:S(2)}) collective-permute-start(f32[2,160,128]{2,1,0:T(8,128)S(1)} %get-tuple-element.51), channel_id=1, source_target_pairs={{1,2},{3,4},{5,6},{7,8},{9,10},{11,12},{13,14},{15,16},{17,18},{19... | collective-permute-start | bytes 491528 | tf_op jit(solution)/shard_map/ppermute | solution.py:523

commit v5 on v4

--- a/solution.py
+++ b/solution.py
@@ -110,10 +110,14 @@
 
 
 def product(high, low, weight):
-    both = jnp.dot(high, weight, preferred_element_type=F32)
-    half = both.shape[1] // 2
-    rest = jnp.dot(low, weight[:, :half], preferred_element_type=F32)
-    return both[:, :half] + both[:, half:] + rest
+    half = weight.shape[1] // 2
+    again = jnp.concatenate([weight[:, :half], jnp.zeros((weight.shape[0], half), BF16)], axis=1)
+    both = jnp.dot(
+        jnp.concatenate([high, low], axis=1),
+        jnp.concatenate([weight, again], axis=0),
+        preferred_element_type=F32,
+    )
+    return both[:, :half] + both[:, half:]
 
 
 def filter_data(a, b, c, d):
@@ -225,23 +229,21 @@
             out_ref[at : at + 128, 128:256] = l
 
 
-def first_weight_kernel(weight_ref, out_ref):
+def fine_weight_kernel(weight_ref, out_ref):
     fine_weight_rows(weight_ref, out_ref)
 
 
-def later_weights_kernel(
-    first_ref, second_ref, down_ref, up_ref, fine_ref, first_out, second_out, down_out, up_out, fine_out
-):
+def down_weights_kernel(first_ref, down_ref, first_out, down_out):
     coarse_weight_rows(first_ref, first_out)
+    nothing = jnp.zeros((64, 128), F32)
+    for k, rows in enumerate(([down_ref[...], nothing], [nothing, down_ref[...]])):
+        h, l = split(jnp.concatenate(rows, axis=0))
+        down_out[:, 128 * k : 128 * k + 128] = h
+        down_out[:, 256 + 128 * k : 384 + 128 * k] = l
+
+
+def up_weights_kernel(second_ref, up_ref, second_out, up_out):
     coarse_weight_rows(second_ref, second_out)
-    fine_weight_rows(fine_ref, fine_out)
-    nothing = jnp.zeros((64, 128), F32)
-    h, l = split(jnp.concatenate([down_ref[...].T, nothing], axis=0))
-    down_out[:, 0:128] = h
-    down_out[:, 256:384] = l
-    h, l = split(jnp.concatenate([nothing, down_ref[...].T], axis=0))
-    down_out[:, 128:256] = h
-    down_out[:, 384:512] = l
     both = jnp.concatenate([up_ref[...], up_ref[...]], axis=0).T
     lower = low_lanes(both.shape)
     for k in range(2):
@@ -251,7 +253,7 @@
 
 
 def fine_in_kernel(
-    codes_ref, links_ref, coarse_links_ref, own_ref, first_ref, second_ref, weight_ref, bias_ref,
+    codes_ref, links_ref, coarse_links_ref, own_ref, second_ref, first_ref, weight_ref, bias_ref,
     hidden_ref, pooled_ref, source, high, low, sums, middle,
 ):
     source[8] = jnp.zeros((256, 128), F32)
@@ -493,7 +495,7 @@
 
 
 def fine_out_kernel(
-    links_ref, own_ref, first_ref, second_ref, features_ref, weight_ref, bias_ref,
+    links_ref, own_ref, second_ref, first_ref, features_ref, weight_ref, bias_ref,
     out_ref, source, flat, high, low, middle,
 ):
     source[8] = jnp.zeros((256, 128), F32)
@@ -559,31 +561,33 @@
         1 << 20,
     )
     first, second = exchanged(first, second)
-    weight_in = call(
-        first_weight_kernel, struct(3072, 256, dtype=BF16), [], [VMEM], (fine_in_weight,), 1 << 20
-    )
-    later = (coarse_first_weight, coarse_second_weight, down_weight, up_weight, fine_out_weight)
-    weight_first, weight_second, down, up, weight_out = call(
-        later_weights_kernel,
-        (
-            struct(4608, 256, dtype=BF16), struct(4608, 256, dtype=BF16),
-            struct(128, 512, dtype=BF16), struct(256, 256, dtype=BF16),
-            struct(3072, 256, dtype=BF16),
-        ),
+    fine_rows, coarse_rows = struct(3072, 256, dtype=BF16), struct(4608, 256, dtype=BF16)
+    weight_in = call(fine_weight_kernel, fine_rows, [], [VMEM], (fine_in_weight,), 1 << 20)
+    weight_first, down = call(
+        down_weights_kernel,
+        (coarse_rows, struct(128, 512, dtype=BF16)),
         [],
-        [VMEM] * 5,
-        later,
-        1 << 30,
-    )
-    weight_in, weight_first, weight_second, down, up, weight_out = lax.optimization_barrier(
-        (weight_in, weight_first, weight_second, down, up, weight_out)
+        [VMEM] * 2,
+        (coarse_first_weight, down_weight.T),
+        1 << 20,
+    )
+    weight_second, up = call(
+        up_weights_kernel,
+        (coarse_rows, struct(256, 256, dtype=BF16)),
+        [],
+        [VMEM] * 2,
+        (coarse_second_weight, up_weight),
+        1 << 20,
+    )
+    weight_in, weight_first, down, weight_second, up = lax.optimization_barrier(
+        (weight_in, weight_first, down, weight_second, up)
     )
     hidden, pooled = call(
         fine_in_kernel,
         (brick, struct(16, 136, 128)),
         [fine_source, *fine_padded, pltpu.VMEM((256, 128), F32), middle],
         [SMEM, SMEM] + [VMEM] * 6,
-        (codes, fine_links, coarse_links, own, first, second, weight_in, fine_in_bias[None]),
+        (codes, fine_links, coarse_links, own, second, first, weight_in, fine_in_bias[None]),
         2 * 1024 * 2304 * 384,
     )
     spread = lax.all_to_all(pooled, "dev", 0, 0, tiled=True)
@@ -643,13 +647,15 @@
         (hidden, risen),
         1 << 20,
     )
+    first, second, out_raw = lax.optimization_barrier((first, second, fine_out_weight))
+    weight_out = call(fine_weight_kernel, fine_rows, [], [VMEM], (out_raw,), 1 << 20)
     first, second = exchanged(first, second)
     return call(
         fine_out_kernel,
         struct(4, 64, 512),
         [fine_source, pltpu.VMEM((2, 512, 128), F32), *fine_padded, middle],
         [SMEM] + [VMEM] * 6,
-        (fine_links, blended, first, second, features, weight_out, fine_out_bias[None]),
+        (fine_links, blended, second, first, features, weight_out, fine_out_bias[None]),
         2 * 1024 * 2304 * 384,
     )
 

time: 102 us -> 101 us (level)
  waiting for transfers between devices: 8.14 us -> 10.2 us
  local copies, waits for them, and re-layouts: 5.08 us -> 3.22 us
  starting transfers between devices: 17 us -> 15.4 us
    ppermute x2, waiting for transfers between devices: 6.48 us -> 8.97 us  [exchanged(): second = lax.ppermute(second, BOTH, outer)]
    unnamed x29 -> x30, local copies, waits for them, and re-layouts: 5.08 us -> 3.22 us
    ppermute x2, starting transfers between devices: 1.67 us -> 0.4 us  [exchanged(): return (lax.ppermute(first, BOTH, inner), second)]
    pallas_call x10 -> x12, Pallas kernels: 28.1 us -> 28.3 us  [call(): pl.pallas_call(kernel, out_shape=out, in_specs=specs, out_specs=jax.tree....]
  transfers between devices with their start and end apart: 5 -> 5, of which waited for: 2 -> 3; matrix products, arithmetic and copies ran while one was open for 1% -> 0% of each run, Pallas kernels for 7% -> 7%
where the time goes in v5:
time: 101 us; the launch traced here: 100 us
  blocking collectives  42.7 us (42%)
  Pallas kernels  28.3 us (28%)
  starting transfers between devices  15.4 us (15%)
  waiting for transfers between devices  10.2 us (10%)
  local copies, waits for them, and re-layouts  3.22 us (3%)
    pallas_call x12, Pallas kernels, call(): pl.pallas_call(kernel, out_shape=out, in_specs=specs, out_specs=jax.tree....  28.3 us
    all_to_all x1, blocking collectives, per_device(): spread = lax.all_to_all(pooled, 'dev', 0, 0, tiled=True)  22.4 us
    all_to_all x1, blocking collectives, per_device(): lax.all_to_all(lifted.reshape(16, 128, 128), 'dev', 0, 0, tiled=True)  20.3 us
    ppermute x2, starting transfers between devices, exchanged(): second = lax.ppermute(second, BOTH, outer)  10.2 us
    ppermute x2, waiting for transfers between devices, exchanged(): second = lax.ppermute(second, BOTH, outer)  8.97 us
    ppermute x1, starting transfers between devices, per_device(): edge = lax.ppermute(cubes, BOTH, edges)  4.8 us
    unnamed x30, local copies, waits for them, and re-layouts  3.22 us
  transfers between devices with their start and end apart: 5, of which 3 were waited for; matrix products, arithmetic and copies ran while one was open for 0% of the time, Pallas kernels for 7%

profile of v5, /device:TPU:97, one launch (start us, length us, event | category | flops | bytes accessed | tf_op | source)
XLA Modules:
  0.0 100.1 jit_solution(18144580402604511317)
XLA Ops:
  0.0 1.2 %copy-done.2 = f32[4,64,512]{2,1,0:T(8,128)S(1)} copy-done((f32[4,64,512]{2,1,0:T(8,128)S(1)}, f32[4,64,512]{2,1,0:T(8,128)}, u32[]{:S(2)}) %copy-start.2) | copy-done | bytes 524312
  1.2 0.5 shard_map.136
  1.7 7.4 %collective-permute-start = (f32[2,160,128]{2,1,0:T(8,128)S(1)}, f32[2,160,128]{2,1,0:T(8,128)S(1)}, u32[]{:S(2)}, u32[]{:S(2)}) collective-permute-start(f32[2,160,128]{2,1,0:T(8,128)S(1)} %get-tuple-element.31), channel_id=1, source_target_pairs={{1,2},{3,4},{5,6},{7,8},{9,10},{11,12},{13,14},{15,16},{17,18},{19... | collective-permute-start | bytes 491528 | tf_op jit(solution)/shard_map/ppermute | solution.py:525
  9.1 0.0 copy-start.1
  9.1 0.1 collective-permute-start.1
  9.2 0.0 copy-start.4
  9.2 1.1 %copy-done.4 = f32[64,1728]{1,0:T(8,128)S(1)} copy-done((f32[64,1728]{1,0:T(8,128)S(1)}, f32[64,1728]{1,0:T(8,128)}, u32[]{:S(2)}) %copy-start.4) | copy-done | bytes 442392
  10.3 0.5 shard_map.137.weight_ref
  10.8 0.0 copy-start.6
  10.8 0.7 copy-done.6
  11.6 0.0 copy-start.11
  11.6 0.6 shard_map.138
  12.2 0.1 copy-done.7
  12.3 0.6 shard_map.139
  12.9 0.9 collective-permute-done.second_ref
  13.8 1.2 %collective-permute-done.1.first_ref = f32[2,160,128]{2,1,0:T(8,128)S(1)} collective-permute-done((f32[2,160,128]{2,1,0:T(8,128)S(1)}, f32[2,160,128]{2,1,0:T(8,128)S(1)}, u32[]{:S(2)}, u32[]{:S(2)}) %collective-permute-start.1) | collective-permute-done | bytes 163872 | tf_op jit(solution)/shard_map/ppermute | solution.py:526
  15.1 2.8 %shard_map.140 = (f32[4,256,128]{2,1,0:T(8,128)S(1)}, f32[16,136,128]{2,1,0:T(8,128)S(1)}) custom-call(s32[4]{0:T(128)S(1)} %copy-done.10, s32[4,26]{1,0:T(4,128)S(1)} %copy-done.8, s32[2,26]{1,0:T(2,128)S(1)} %copy-done.9, f32[4,256,128]{2,1,0:T(8,128)S(1)} %get-tuple-element.30.own_ref, f32[2,160,128]{2,1,0:T(8,128)S(1)} %collective-permute-done.second_ref, ...), custom_call_target="tpu_custom_call" | custom-call | flops 1811939328 | bytes 2097152 | tf_op jit(solution)/shard_map/pallas_call | solution.py:534
  17.9 0.0 copy-start.12
  17.9 22.4 %all_to_all.10.all_ref = f32[16,136,128]{2,1,0:T(8,128)S(1)} all-to-all(f32[16,136,128]{2,1,0:T(8,128)S(1)} %get-tuple-element.39), channel_id=1, replica_groups=mesh['grp'=16,'dev'=16] {'dev'}, dimensions={0} | all-to-all | bytes 2228224 | tf_op jit(solution)/shard_map/all_to_all | solution.py:593
  40.3 1.7 %shard_map.141 = (f32[840,128]{1,0:T(8,128)S(1)}, s32[256]{0:T(256)S(1)}, s32[64]{0:T(128)S(1)}) custom-call(f32[16,136,128]{2,1,0:T(8,128)S(1)} %all_to_all.10.all_ref), custom_call_target="tpu_custom_call" | custom-call | flops 1048576 | bytes 2097152 | tf_op jit(solution)/shard_map/pallas_call | solution.py:534
  42.0 4.8 %collective-permute-start.2 = (f32[840,128]{1,0:T(8,128)S(1)}, f32[840,128]{1,0:T(8,128)S(1)}, u32[]{:S(2)}, u32[]{:S(2)}) collective-permute-start(f32[840,128]{1,0:T(8,128)S(1)} %get-tuple-element.45), channel_id=1, source_target_pairs={{0,16},{1,17},{16,32},{17,33},{32,48},{33,49},{48,64},{49,65},{64,... | collective-permute-start | bytes 1290248 | tf_op jit(solution)/shard_map/ppermute | solution.py:608
  46.8 1.6 %shard_map.142 = (f32[11,512,128]{2,1,0:T(8,128)S(1)}, f32[8,128]{1,0:T(8,128)S(1)}) custom-call(f32[16,136,128]{2,1,0:T(8,128)S(1)} %all_to_all.10.all_ref, s32[256]{0:T(256)S(1)} %get-tuple-element.40.place_ref, bf16[128,512]{1,0:T(8,128)(2,1)S(1)} %get-tuple-element.41.down_ref), custom_call_target="tpu_custom_call" | custom-call | flops 268435456 | bytes 2097152 | tf_op jit(solution)/shard_map/pallas_call | solution.py:534
  48.4 0.0 copy-start.13
  48.4 3.7 %shard_map.143.inner_ref = f32[2,512,128]{2,1,0:T(8,128)S(1)} custom-call(f32[8,128]{1,0:T(8,128)S(1)} %get-tuple-element.42.links_ref.near_links_ref, f32[11,512,128]{2,1,0:T(8,128)S(1)} %get-tuple-element.44.based_ref, bf16[4608,256]{1,0:T(8,128)(2,1)S(1)} %get-tuple-element.46.weight_ref.first_weight_ref, f32[1,128]{1,0:T(1,128)S(1)} %bitcast.9), custom_call_target="tpu_custom_call" | custom-call | flops 2717908992 | bytes 2097152 | tf_op jit(solution)/shard_map/pallas_call | solution.py:534
  52.1 11.8 %shard_map.144 = f32[64,32,128]{2,1,0:T(8,128)S(1)} custom-call(s32[2,26]{1,0:T(2,128)S(1)} %copy-done.9, f32[8,128]{1,0:T(8,128)S(1)} %get-tuple-element.42.links_ref.near_links_ref, s32[64]{0:T(128)S(1)} %get-tuple-element.43.codes_ref, f32[11,512,128]{2,1,0:T(8,128)S(1)} %get-tuple-element.44.based_ref, f32[840,128]{1,0:T(8,128)S(1)} %collective-permute-done.2.edge_ref, ...), custom_call_target="tpu_custom_call" | custom-call | flops 8153726976 | bytes 2097152 | tf_op jit(solution)/shard_map/pallas_call | solution.py:534
  64.0 20.3 %all_to_all.11.risen_ref = f32[16,128,128]{2,1,0:T(8,128)S(1)} all-to-all(f32[16,128,128]{2,1,0:T(8,128)S(1)} %bitcast.6), channel_id=1, replica_groups=mesh['grp'=16,'dev'=16] {'dev'}, dimensions={0} | all-to-all | bytes 2097152 | tf_op jit(solution)/shard_map/all_to_all | solution.py:641
  84.2 0.4 shard_map.145
  84.6 2.8 %collective-permute-start.3 = (f32[2,160,128]{2,1,0:T(8,128)S(1)}, f32[2,160,128]{2,1,0:T(8,128)S(1)}, u32[]{:S(2)}, u32[]{:S(2)}) collective-permute-start(f32[2,160,128]{2,1,0:T(8,128)S(1)} %get-tuple-element.52), channel_id=1, source_target_pairs={{1,2},{3,4},{5,6},{7,8},{9,10},{11,12},{13,14},{15,16},{17,18},{19... | collective-permute-start | bytes 491528 | tf_op jit(solution)/shard_map/ppermute | solution.py:525
  87.4 0.3 collective-permute-start.4
  87.7 0.5 shard_map.146.weight_ref
  88.2 8.1 %collective-permute-done.3.second_ref = f32[2,160,128]{2,1,0:T(8,128)S(1)} collective-permute-done((f32[2,160,128]{2,1,0:T(8,128)S(1)}, f32[2,160,128]{2,1,0:T(8,128)S(1)}, u32[]{:S(2)}, u32[]{:S(2)}) %collective-permute-start.3) | collective-permute-done | bytes 163872 | tf_op jit(solution)/shard_map/ppermute | solution.py:525
  96.3 3.8 %shard_map.147 = f32[4,64,512]{2,1,0:T(8,128)} custom-call(s32[4,26]{1,0:T(4,128)S(1)} %copy-done.8, f32[4,256,128]{2,1,0:T(8,128)S(1)} %get-tuple-element.49.own_ref, f32[2,160,128]{2,1,0:T(8,128)S(1)} %collective-permute-done.3.second_ref, f32[2,160,128]{2,1,0:T(8,128)S(1)} %collective-permute-done.4.first_ref, f32[4,64,512]{2,1,0:T(8,128)S(1)} %copy-done.3, ...), custom_call_target="tpu_custom_call" | custom-call | flops 1811939328 | bytes 2097152 | tf_op jit(solution)/shard_map/pallas_call | solution.py:534
  (22 shorter events, 0.0 us)
Async XLA Ops:
  0.0 10.8 %copy-start = (f32[128,3456]{1,0:T(8,128)S(1)}, f32[128,3456]{1,0:T(8,128)}, u32[]{:S(2)}) copy-start(f32[128,3456]{1,0:T(8,128)} %first_ref.1) | copy-start | bytes 5308420
  0.0 1.2 %copy-start.2 = (f32[4,64,512]{2,1,0:T(8,128)S(1)}, f32[4,64,512]{2,1,0:T(8,128)}, u32[]{:S(2)}) copy-start(f32[4,64,512]{2,1,0:T(8,128)} %features_ref.3) | copy-start | bytes 1572868
  1.7 12.1 %collective-permute-start = (f32[2,160,128]{2,1,0:T(8,128)S(1)}, f32[2,160,128]{2,1,0:T(8,128)S(1)}, u32[]{:S(2)}, u32[]{:S(2)}) collective-permute-start(f32[2,160,128]{2,1,0:T(8,128)S(1)} %get-tuple-element.31), channel_id=1, source_target_pairs={{1,2},{3,4},{5,6},{7,8},{9,10},{11,12},{13,14},{15,16},{17,18},{19... | collective-permute-start | bytes 491528 | tf_op jit(solution)/shard_map/ppermute | solution.py:525
  9.1 3.1 %copy-start.1 = (f32[128,3456]{1,0:T(8,128)S(1)}, f32[128,3456]{1,0:T(8,128)}, u32[]{:S(2)}) copy-start(f32[128,3456]{1,0:T(8,128)} %second_ref.1) | copy-start | bytes 5308420
  9.1 6.0 %collective-permute-start.1 = (f32[2,160,128]{2,1,0:T(8,128)S(1)}, f32[2,160,128]{2,1,0:T(8,128)S(1)}, u32[]{:S(2)}, u32[]{:S(2)}) collective-permute-start(f32[2,160,128]{2,1,0:T(8,128)S(1)} %get-tuple-element.32), channel_id=1, source_target_pairs={{0,1},{1,0},{2,3},{3,2},{4,5},{5,4},{6,7},{7,6},{8,9},{9,8},{10,11... | collective-permute-start | bytes 491528 | tf_op jit(solution)/shard_map/ppermute | solution.py:526
  9.2 1.1 %copy-start.4 = (f32[64,1728]{1,0:T(8,128)S(1)}, f32[64,1728]{1,0:T(8,128)}, u32[]{:S(2)}) copy-start(f32[64,1728]{1,0:T(8,128)} %weight_ref.1) | copy-start | bytes 1327108
  10.8 0.8 copy-start.6
  11.6 0.8 copy-start.7
  11.6 3.5 %copy-start.8 = (s32[4,26]{1,0:T(4,128)S(1)}, s32[4,26]{1,0:T(4,128)}, u32[]{:S(2)}) copy-start(s32[4,26]{1,0:T(4,128)} %links_ref.5) | copy-start | bytes 1252
  11.6 3.5 %copy-start.9 = (s32[2,26]{1,0:T(2,128)S(1)}, s32[2,26]{1,0:T(2,128)}, u32[]{:S(2)}) copy-start(s32[2,26]{1,0:T(2,128)} %links_ref.4) | copy-start | bytes 628
  11.6 3.5 %copy-start.10 = (s32[4]{0:T(128)S(1)}, s32[4]{0:T(128)}, u32[]{:S(2)}) copy-start(s32[4]{0:T(128)} %codes_ref.1) | copy-start | bytes 52
  11.6 3.5 %copy-start.11 = (f32[64]{0:T(128)S(1)}, f32[64]{0:T(128)}, u32[]{:S(2)}) copy-start(f32[64]{0:T(128)} %param.19) | copy-start | bytes 772
  17.9 30.5 %copy-start.12 = (f32[128]{0:T(128)S(1)}, f32[128]{0:T(128)}, u32[]{:S(2)}) copy-start(f32[128]{0:T(128)} %param.22) | copy-start | bytes 1540
  42.0 10.1 %collective-permute-start.2 = (f32[840,128]{1,0:T(8,128)S(1)}, f32[840,128]{1,0:T(8,128)S(1)}, u32[]{:S(2)}, u32[]{:S(2)}) collective-permute-start(f32[840,128]{1,0:T(8,128)S(1)} %get-tuple-element.45), channel_id=1, source_target_pairs={{0,16},{1,17},{16,32},{17,33},{32,48},{33,49},{48,64},{49,65},{64,... | collective-permute-start | bytes 1290248 | tf_op jit(solution)/shard_map/ppermute | solution.py:608
  48.4 3.7 %copy-start.13 = (f32[128]{0:T(128)S(1)}, f32[128]{0:T(128)}, u32[]{:S(2)}) copy-start(f32[128]{0:T(128)} %param.24) | copy-start | bytes 1540
  64.0 23.8 %copy-start.5 = (f32[64,1728]{1,0:T(8,128)S(1)}, f32[64,1728]{1,0:T(8,128)}, u32[]{:S(2)}) copy-start(f32[64,1728]{1,0:T(8,128)} %weight_ref.2) | copy-start | bytes 1327108
  84.2 12.1 %copy-start.3 = (f32[4,64,512]{2,1,0:T(8,128)S(1)}, f32[4,64,512]{2,1,0:T(8,128)}, u32[]{:S(2)}) copy-start(f32[4,64,512]{2,1,0:T(8,128)} %features_ref.3) | copy-start | bytes 1572868
  84.2 12.1 %copy-start.14 = (f32[64]{0:T(128)S(1)}, f32[64]{0:T(128)}, u32[]{:S(2)}) copy-start(f32[64]{0:T(128)} %param.27) | copy-start | bytes 772
  84.6 11.7 %collective-permute-start.3 = (f32[2,160,128]{2,1,0:T(8,128)S(1)}, f32[2,160,128]{2,1,0:T(8,128)S(1)}, u32[]{:S(2)}, u32[]{:S(2)}) collective-permute-start(f32[2,160,128]{2,1,0:T(8,128)S(1)} %get-tuple-element.52), channel_id=1, source_target_pairs={{1,2},{3,4},{5,6},{7,8},{9,10},{11,12},{13,14},{15,16},{17,18},{19... | collective-permute-start | bytes 491528 | tf_op jit(solution)/shard_map/ppermute | solution.py:525
  87.4 8.9 %collective-permute-start.4 = (f32[2,160,128]{2,1,0:T(8,128)S(1)}, f32[2,160,128]{2,1,0:T(8,128)S(1)}, u32[]{:S(2)}, u32[]{:S(2)}) collective-permute-start(f32[2,160,128]{2,1,0:T(8,128)S(1)} %get-tuple-element.53), channel_id=1, source_target_pairs={{0,1},{1,0},{2,3},{3,2},{4,5},{5,4},{6,7},{7,6},{8,9},{9,8},{10,11... | collective-permute-start | bytes 491528 | tf_op jit(solution)/shard_map/ppermute | solution.py:526

commit v6 on v5

--- a/solution.py
+++ b/solution.py
@@ -253,7 +253,7 @@
 
 
 def fine_in_kernel(
-    codes_ref, links_ref, coarse_links_ref, own_ref, second_ref, first_ref, weight_ref, bias_ref,
+    codes_ref, links_ref, coarse_links_ref, own_ref, first_ref, second_ref, weight_ref, bias_ref,
     hidden_ref, pooled_ref, source, high, low, sums, middle,
 ):
     source[8] = jnp.zeros((256, 128), F32)
@@ -587,7 +587,7 @@
         (brick, struct(16, 136, 128)),
         [fine_source, *fine_padded, pltpu.VMEM((256, 128), F32), middle],
         [SMEM, SMEM] + [VMEM] * 6,
-        (codes, fine_links, coarse_links, own, second, first, weight_in, fine_in_bias[None]),
+        (codes, fine_links, coarse_links, own, first, second, weight_in, fine_in_bias[None]),
         2 * 1024 * 2304 * 384,
     )
     spread = lax.all_to_all(pooled, "dev", 0, 0, tiled=True)

time: 101 us -> 102 us (level)
  blocking collectives: 42.7 us -> 44 us
  waiting for transfers between devices: 10.2 us -> 9.02 us
    ppermute x2, waiting for transfers between devices: 1.25 us -> 0.01 us  [exchanged(): return (lax.ppermute(first, BOTH, inner), second)]
    ppermute x2, starting transfers between devices: 0.4 us -> 1.61 us  [exchanged(): return (lax.ppermute(first, BOTH, inner), second)]
    all_to_all x1, blocking collectives: 22.4 us -> 23.5 us  [per_device(): spread = lax.all_to_all(pooled, 'dev', 0, 0, tiled=True)]
  transfers between devices with their start and end apart: 5 -> 5, of which waited for: 3 -> 2; matrix products, arithmetic and copies ran while one was open for 0% -> 0% of each run, Pallas kernels for 7% -> 7%
where the time goes in v6:
time: 102 us; the launch traced here: 101 us
  blocking collectives  44 us (43%)
  Pallas kernels  28.3 us (28%)
  starting transfers between devices  16.4 us (16%)
  waiting for transfers between devices  9.02 us (9%)
  local copies, waits for them, and re-layouts  3.11 us (3%)
    pallas_call x12, Pallas kernels, call(): pl.pallas_call(kernel, out_shape=out, in_specs=specs, out_specs=jax.tree....  28.3 us
    all_to_all x1, blocking collectives, per_device(): spread = lax.all_to_all(pooled, 'dev', 0, 0, tiled=True)  23.5 us
    all_to_all x1, blocking collectives, per_device(): lax.all_to_all(lifted.reshape(16, 128, 128), 'dev', 0, 0, tiled=True)  20.5 us
    ppermute x2, starting transfers between devices, exchanged(): second = lax.ppermute(second, BOTH, outer)  10.1 us
    ppermute x2, waiting for transfers between devices, exchanged(): second = lax.ppermute(second, BOTH, outer)  9.02 us
    ppermute x1, starting transfers between devices, per_device(): edge = lax.ppermute(cubes, BOTH, edges)  4.72 us
    unnamed x30, local copies, waits for them, and re-layouts  3.11 us
  transfers between devices with their start and end apart: 5, of which 2 were waited for; matrix products, arithmetic and copies ran while one was open for 0% of the time, Pallas kernels for 7%

profile of v6, /device:TPU:97, one launch (start us, length us, event | category | flops | bytes accessed | tf_op | source)
XLA Modules:
  0.0 101.1 jit_solution(14778057848109600951)
XLA Ops:
  0.0 1.2 %copy-done.2 = f32[4,64,512]{2,1,0:T(8,128)S(1)} copy-done((f32[4,64,512]{2,1,0:T(8,128)S(1)}, f32[4,64,512]{2,1,0:T(8,128)}, u32[]{:S(2)}) %copy-start.2) | copy-done | bytes 524312
  1.2 0.5 shard_map.136
  1.7 1.3 %collective-permute-start = (f32[2,160,128]{2,1,0:T(8,128)S(1)}, f32[2,160,128]{2,1,0:T(8,128)S(1)}, u32[]{:S(2)}, u32[]{:S(2)}) collective-permute-start(f32[2,160,128]{2,1,0:T(8,128)S(1)} %get-tuple-element.31), channel_id=1, source_target_pairs={{0,1},{1,0},{2,3},{3,2},{4,5},{5,4},{6,7},{7,6},{8,9},{9,8},{10,11... | collective-permute-start | bytes 491528 | tf_op jit(solution)/shard_map/ppermute | solution.py:526
  3.0 7.1 %collective-permute-start.1 = (f32[2,160,128]{2,1,0:T(8,128)S(1)}, f32[2,160,128]{2,1,0:T(8,128)S(1)}, u32[]{:S(2)}, u32[]{:S(2)}) collective-permute-start(f32[2,160,128]{2,1,0:T(8,128)S(1)} %get-tuple-element.32), channel_id=1, source_target_pairs={{1,2},{3,4},{5,6},{7,8},{9,10},{11,12},{13,14},{15,16},{17,18},{19... | collective-permute-start | bytes 491528 | tf_op jit(solution)/shard_map/ppermute | solution.py:525
  10.1 0.0 copy-start.4
  10.1 1.0 copy-done.4
  11.1 0.5 shard_map.137.weight_ref
  11.6 0.0 copy-start.6
  11.6 0.7 copy-done.6
  12.4 0.0 copy-start.11
  12.4 0.6 shard_map.138
  13.0 0.1 copy-done.7
  13.1 0.6 shard_map.139
  13.7 0.0 collective-permute-done.first_ref
  13.7 1.1 %collective-permute-done.1.second_ref = f32[2,160,128]{2,1,0:T(8,128)S(1)} collective-permute-done((f32[2,160,128]{2,1,0:T(8,128)S(1)}, f32[2,160,128]{2,1,0:T(8,128)S(1)}, u32[]{:S(2)}, u32[]{:S(2)}) %collective-permute-start.1) | collective-permute-done | bytes 163872 | tf_op jit(solution)/shard_map/ppermute | solution.py:525
  14.9 2.8 %shard_map.140 = (f32[4,256,128]{2,1,0:T(8,128)S(1)}, f32[16,136,128]{2,1,0:T(8,128)S(1)}) custom-call(s32[4]{0:T(128)S(1)} %copy-done.10, s32[4,26]{1,0:T(4,128)S(1)} %copy-done.8, s32[2,26]{1,0:T(2,128)S(1)} %copy-done.9, f32[4,256,128]{2,1,0:T(8,128)S(1)} %get-tuple-element.30.own_ref, f32[2,160,128]{2,1,0:T(8,128)S(1)} %collective-permute-done.first_ref, ...), custom_call_target="tpu_custom_call" | custom-call | flops 1811939328 | bytes 2097152 | tf_op jit(solution)/shard_map/pallas_call | solution.py:534
  17.7 0.0 copy-start.12
  17.7 23.5 %all_to_all.10.all_ref = f32[16,136,128]{2,1,0:T(8,128)S(1)} all-to-all(f32[16,136,128]{2,1,0:T(8,128)S(1)} %get-tuple-element.39), channel_id=1, replica_groups=mesh['grp'=16,'dev'=16] {'dev'}, dimensions={0} | all-to-all | bytes 2228224 | tf_op jit(solution)/shard_map/all_to_all | solution.py:593
  41.2 1.7 %shard_map.141 = (f32[840,128]{1,0:T(8,128)S(1)}, s32[256]{0:T(256)S(1)}, s32[64]{0:T(128)S(1)}) custom-call(f32[16,136,128]{2,1,0:T(8,128)S(1)} %all_to_all.10.all_ref), custom_call_target="tpu_custom_call" | custom-call | flops 1048576 | bytes 2097152 | tf_op jit(solution)/shard_map/pallas_call | solution.py:534
  42.9 4.7 %collective-permute-start.2 = (f32[840,128]{1,0:T(8,128)S(1)}, f32[840,128]{1,0:T(8,128)S(1)}, u32[]{:S(2)}, u32[]{:S(2)}) collective-permute-start(f32[840,128]{1,0:T(8,128)S(1)} %get-tuple-element.45), channel_id=1, source_target_pairs={{0,16},{1,17},{16,32},{17,33},{32,48},{33,49},{48,64},{49,65},{64,... | collective-permute-start | bytes 1290248 | tf_op jit(solution)/shard_map/ppermute | solution.py:608
  47.6 1.6 %shard_map.142 = (f32[11,512,128]{2,1,0:T(8,128)S(1)}, f32[8,128]{1,0:T(8,128)S(1)}) custom-call(f32[16,136,128]{2,1,0:T(8,128)S(1)} %all_to_all.10.all_ref, s32[256]{0:T(256)S(1)} %get-tuple-element.40.place_ref, bf16[128,512]{1,0:T(8,128)(2,1)S(1)} %get-tuple-element.41.down_ref), custom_call_target="tpu_custom_call" | custom-call | flops 268435456 | bytes 2097152 | tf_op jit(solution)/shard_map/pallas_call | solution.py:534
  49.2 0.0 copy-start.13
  49.2 3.7 %shard_map.143.inner_ref = f32[2,512,128]{2,1,0:T(8,128)S(1)} custom-call(f32[8,128]{1,0:T(8,128)S(1)} %get-tuple-element.42.links_ref.near_links_ref, f32[11,512,128]{2,1,0:T(8,128)S(1)} %get-tuple-element.44.based_ref, bf16[4608,256]{1,0:T(8,128)(2,1)S(1)} %get-tuple-element.46.weight_ref.first_weight_ref, f32[1,128]{1,0:T(1,128)S(1)} %bitcast.9), custom_call_target="tpu_custom_call" | custom-call | flops 2717908992 | bytes 2097152 | tf_op jit(solution)/shard_map/pallas_call | solution.py:534
  52.9 11.8 %shard_map.144 = f32[64,32,128]{2,1,0:T(8,128)S(1)} custom-call(s32[2,26]{1,0:T(2,128)S(1)} %copy-done.9, f32[8,128]{1,0:T(8,128)S(1)} %get-tuple-element.42.links_ref.near_links_ref, s32[64]{0:T(128)S(1)} %get-tuple-element.43.codes_ref, f32[11,512,128]{2,1,0:T(8,128)S(1)} %get-tuple-element.44.based_ref, f32[840,128]{1,0:T(8,128)S(1)} %collective-permute-done.2.edge_ref, ...), custom_call_target="tpu_custom_call" | custom-call | flops 8153726976 | bytes 2097152 | tf_op jit(solution)/shard_map/pallas_call | solution.py:534
  64.7 0.0 copy-start.5
  64.8 20.5 %all_to_all.11.risen_ref = f32[16,128,128]{2,1,0:T(8,128)S(1)} all-to-all(f32[16,128,128]{2,1,0:T(8,128)S(1)} %bitcast.6), channel_id=1, replica_groups=mesh['grp'=16,'dev'=16] {'dev'}, dimensions={0} | all-to-all | bytes 2097152 | tf_op jit(solution)/shard_map/all_to_all | solution.py:641
  85.2 0.4 shard_map.145
  85.6 3.0 %collective-permute-start.3 = (f32[2,160,128]{2,1,0:T(8,128)S(1)}, f32[2,160,128]{2,1,0:T(8,128)S(1)}, u32[]{:S(2)}, u32[]{:S(2)}) collective-permute-start(f32[2,160,128]{2,1,0:T(8,128)S(1)} %get-tuple-element.52), channel_id=1, source_target_pairs={{1,2},{3,4},{5,6},{7,8},{9,10},{11,12},{13,14},{15,16},{17,18},{19... | collective-permute-start | bytes 491528 | tf_op jit(solution)/shard_map/ppermute | solution.py:525
  88.6 0.3 collective-permute-start.4
  88.9 0.5 shard_map.146.weight_ref
  89.4 7.9 %collective-permute-done.3.second_ref = f32[2,160,128]{2,1,0:T(8,128)S(1)} collective-permute-done((f32[2,160,128]{2,1,0:T(8,128)S(1)}, f32[2,160,128]{2,1,0:T(8,128)S(1)}, u32[]{:S(2)}, u32[]{:S(2)}) %collective-permute-start.3) | collective-permute-done | bytes 163872 | tf_op jit(solution)/shard_map/ppermute | solution.py:525
  97.3 3.8 %shard_map.147 = f32[4,64,512]{2,1,0:T(8,128)} custom-call(s32[4,26]{1,0:T(4,128)S(1)} %copy-done.8, f32[4,256,128]{2,1,0:T(8,128)S(1)} %get-tuple-element.49.own_ref, f32[2,160,128]{2,1,0:T(8,128)S(1)} %collective-permute-done.3.second_ref, f32[2,160,128]{2,1,0:T(8,128)S(1)} %collective-permute-done.4.first_ref, f32[4,64,512]{2,1,0:T(8,128)S(1)} %copy-done.3, ...), custom_call_target="tpu_custom_call" | custom-call | flops 1811939328 | bytes 2097152 | tf_op jit(solution)/shard_map/pallas_call | solution.py:534
  (22 shorter events, 0.0 us)
Async XLA Ops:
  0.0 11.6 %copy-start = (f32[128,3456]{1,0:T(8,128)S(1)}, f32[128,3456]{1,0:T(8,128)}, u32[]{:S(2)}) copy-start(f32[128,3456]{1,0:T(8,128)} %first_ref.1) | copy-start | bytes 5308420
  0.0 1.2 %copy-start.2 = (f32[4,64,512]{2,1,0:T(8,128)S(1)}, f32[4,64,512]{2,1,0:T(8,128)}, u32[]{:S(2)}) copy-start(f32[4,64,512]{2,1,0:T(8,128)} %features_ref.3) | copy-start | bytes 1572868
  1.7 12.1 %collective-permute-start = (f32[2,160,128]{2,1,0:T(8,128)S(1)}, f32[2,160,128]{2,1,0:T(8,128)S(1)}, u32[]{:S(2)}, u32[]{:S(2)}) collective-permute-start(f32[2,160,128]{2,1,0:T(8,128)S(1)} %get-tuple-element.31), channel_id=1, source_target_pairs={{0,1},{1,0},{2,3},{3,2},{4,5},{5,4},{6,7},{7,6},{8,9},{9,8},{10,11... | collective-permute-start | bytes 491528 | tf_op jit(solution)/shard_map/ppermute | solution.py:526
  3.0 10.1 %copy-start.1 = (f32[128,3456]{1,0:T(8,128)S(1)}, f32[128,3456]{1,0:T(8,128)}, u32[]{:S(2)}) copy-start(f32[128,3456]{1,0:T(8,128)} %second_ref.1) | copy-start | bytes 5308420
  3.0 11.9 %collective-permute-start.1 = (f32[2,160,128]{2,1,0:T(8,128)S(1)}, f32[2,160,128]{2,1,0:T(8,128)S(1)}, u32[]{:S(2)}, u32[]{:S(2)}) collective-permute-start(f32[2,160,128]{2,1,0:T(8,128)S(1)} %get-tuple-element.32), channel_id=1, source_target_pairs={{1,2},{3,4},{5,6},{7,8},{9,10},{11,12},{13,14},{15,16},{17,18},{19... | collective-permute-start | bytes 491528 | tf_op jit(solution)/shard_map/ppermute | solution.py:525
  10.1 1.0 %copy-start.4 = (f32[64,1728]{1,0:T(8,128)S(1)}, f32[64,1728]{1,0:T(8,128)}, u32[]{:S(2)}) copy-start(f32[64,1728]{1,0:T(8,128)} %weight_ref.1) | copy-start | bytes 1327108
  11.6 0.8 copy-start.6
  12.4 0.8 copy-start.7
  12.4 2.5 %copy-start.8 = (s32[4,26]{1,0:T(4,128)S(1)}, s32[4,26]{1,0:T(4,128)}, u32[]{:S(2)}) copy-start(s32[4,26]{1,0:T(4,128)} %links_ref.5) | copy-start | bytes 1252
  12.4 2.5 %copy-start.9 = (s32[2,26]{1,0:T(2,128)S(1)}, s32[2,26]{1,0:T(2,128)}, u32[]{:S(2)}) copy-start(s32[2,26]{1,0:T(2,128)} %links_ref.4) | copy-start | bytes 628
  12.4 2.5 %copy-start.10 = (s32[4]{0:T(128)S(1)}, s32[4]{0:T(128)}, u32[]{:S(2)}) copy-start(s32[4]{0:T(128)} %codes_ref.1) | copy-start | bytes 52
  12.4 2.5 %copy-start.11 = (f32[64]{0:T(128)S(1)}, f32[64]{0:T(128)}, u32[]{:S(2)}) copy-start(f32[64]{0:T(128)} %param.19) | copy-start | bytes 772
  17.7 31.5 %copy-start.12 = (f32[128]{0:T(128)S(1)}, f32[128]{0:T(128)}, u32[]{:S(2)}) copy-start(f32[128]{0:T(128)} %param.22) | copy-start | bytes 1540
  42.9 10.0 %collective-permute-start.2 = (f32[840,128]{1,0:T(8,128)S(1)}, f32[840,128]{1,0:T(8,128)S(1)}, u32[]{:S(2)}, u32[]{:S(2)}) collective-permute-start(f32[840,128]{1,0:T(8,128)S(1)} %get-tuple-element.45), channel_id=1, source_target_pairs={{0,16},{1,17},{16,32},{17,33},{32,48},{33,49},{48,64},{49,65},{64,... | collective-permute-start | bytes 1290248 | tf_op jit(solution)/shard_map/ppermute | solution.py:608
  49.2 3.7 %copy-start.13 = (f32[128]{0:T(128)S(1)}, f32[128]{0:T(128)}, u32[]{:S(2)}) copy-start(f32[128]{0:T(128)} %param.24) | copy-start | bytes 1540
  64.7 24.1 %copy-start.5 = (f32[64,1728]{1,0:T(8,128)S(1)}, f32[64,1728]{1,0:T(8,128)}, u32[]{:S(2)}) copy-start(f32[64,1728]{1,0:T(8,128)} %weight_ref.2) | copy-start | bytes 1327108
  85.2 12.1 %copy-start.3 = (f32[4,64,512]{2,1,0:T(8,128)S(1)}, f32[4,64,512]{2,1,0:T(8,128)}, u32[]{:S(2)}) copy-start(f32[4,64,512]{2,1,0:T(8,128)} %features_ref.3) | copy-start | bytes 1572868
  85.2 12.1 %copy-start.14 = (f32[64]{0:T(128)S(1)}, f32[64]{0:T(128)}, u32[]{:S(2)}) copy-start(f32[64]{0:T(128)} %param.27) | copy-start | bytes 772
  85.6 11.7 %collective-permute-start.3 = (f32[2,160,128]{2,1,0:T(8,128)S(1)}, f32[2,160,128]{2,1,0:T(8,128)S(1)}, u32[]{:S(2)}, u32[]{:S(2)}) collective-permute-start(f32[2,160,128]{2,1,0:T(8,128)S(1)} %get-tuple-element.52), channel_id=1, source_target_pairs={{1,2},{3,4},{5,6},{7,8},{9,10},{11,12},{13,14},{15,16},{17,18},{19... | collective-permute-start | bytes 491528 | tf_op jit(solution)/shard_map/ppermute | solution.py:525
  88.6 8.7 %collective-permute-start.4 = (f32[2,160,128]{2,1,0:T(8,128)S(1)}, f32[2,160,128]{2,1,0:T(8,128)S(1)}, u32[]{:S(2)}, u32[]{:S(2)}) collective-permute-start(f32[2,160,128]{2,1,0:T(8,128)S(1)} %get-tuple-element.53), channel_id=1, source_target_pairs={{0,1},{1,0},{2,3},{3,2},{4,5},{5,4},{6,7},{7,6},{8,9},{9,8},{10,11... | collective-permute-start | bytes 491528 | tf_op jit(solution)/shard_map/ppermute | solution.py:526
